TPU v7x, 32 devices: a whole 2x2x4 slice. The times are simulated.
32 devices in a mesh: pts: 32 (over z, y, x, core).
Axes of the slice: x: 2, y: 2, z: 4, core: 2. Of those that a mesh axis runs over, the one named last changes fastest.
Arguments:
- points: bfloat16 [16384, 1024], P('pts')
- weights: bfloat16 [16384, 512], P('pts'), may hold values from -2 to 2
- node_proj: bfloat16 [512, 16384], P(None, 'pts'), may hold values from -0.125 to 0.125
- skel_idx: int32 [32, 128], P('pts'), may hold values from 0 to 511, as said below
- near_list: int32 [32, 4], P('pts'), may hold values from 0 to 31, as said below
- near_count: int32 [32], P('pts'), may hold values from 1 to 4, as said below
- far_list: int32 [32, 4], P('pts'), may hold values from 0 to 7, as said below
- far_count: int32 [32], P('pts'), may hold values from 1 to 4
Outputs:
- potential: float32 [16384, 512], P('pts')
Inputs may be any that keep to these rules, and one draw needn't show every extreme that they name: `skel_idx`: each row holds 128 distinct local point indices. `near_list`: row t lists distinct leaves among t - 2, t - 1, t + 1, t + 2 in its first near_count[t] slots; the other slots hold t. `near_count`: at most the number of leaves among t - 2 to t + 2 other than t. `far_list`: row t lists distinct nodes that hold none of the leaves t - 2 to t + 2 in its first far_count[t] slots; the other slots repeat the first entry.
All inputs are finite; a program needn't handle non-finite values.
Results may differ from a plain program's by a relative error of at most 0.003.
Values may be sent and summed in bfloat16 or wider, within the bound.
No kernel may reach another device: no remote copies, remote signals or barrier semaphores. Data moves between devices by JAX's collectives and lax.ppermute only.
A program may use at most 128 MiB of HBM per device.

v0:
```python
import jax
import jax.numpy as jnp
from jax import lax
from jax.sharding import PartitionSpec as P

DIM = 1024
SKEL = 512
NODES = 8
NEAR = 4
FAR = 4


def partner(value, axis, stride):
    mask = 2**stride
    pairs = [(source, source ^ mask) for source in range(lax.axis_size(axis))]
    return lax.ppermute(value, axis, pairs)


def shifted(value, axis, steps):
    count = lax.axis_size(axis)
    leading, last = (max(0, -steps), min(count, count - steps))
    return lax.ppermute(value, axis, [(source, source + steps) for source in range(leading, last)])


def kernel_sum(xpts, xsq, ypts, wts, gate):
    ysq = jnp.sum(jnp.square(ypts.astype(jnp.float32)), axis=1)
    scores = lax.dot_general(
        xpts, ypts, (((1,), (1,)), ((), ())), preferred_element_type=jnp.float32
    )
    dist = xsq[:, None] + ysq[None, :] - 2.0 * scores
    kern = (jnp.exp(dist * (-0.5 / DIM)) * gate).astype(jnp.bfloat16)
    return jnp.dot(kern, wts, preferred_element_type=jnp.float32)


def shards(points, weights, node_proj, skel_idx, near_list, near_count, far_list, far_count):
    leaves = lax.axis_size("pts")
    leaf_id = lax.axis_index("pts")
    group = leaves // NODES
    levels = group.bit_length() - 1
    rows = points.shape[0]
    width = points.shape[1]
    xsq = jnp.sum(jnp.square(points.astype(jnp.float32)), axis=1)
    partial_value = jnp.dot(node_proj, weights, preferred_element_type=jnp.float32)
    block = partial_value
    for level in reversed(range(levels)):
        half = block.shape[0] // 2
        upper = leaf_id // 2**level % 2
        keep = lax.dynamic_slice_in_dim(block, upper * half, half, 0)
        give = lax.dynamic_slice_in_dim(block, (1 - upper) * half, half, 0)
        block = keep + partner(give.astype(jnp.bfloat16), "pts", level).astype(give.dtype)
    share_w = block.astype(jnp.bfloat16)
    skel_rows = jnp.take(points, skel_idx[0], axis=0)
    stacked = jnp.concatenate([points, weights], axis=1)
    total = kernel_sum(points, xsq, points, weights, jnp.float32(1.0))
    moved = {}
    for step_by in (2, 1, -1, -2):
        moved[step_by] = shifted(stacked, "pts", step_by)
    wide = jnp.concatenate([moved[2], moved[1], stacked, moved[-1], moved[-2]], axis=0)
    for slot in range(NEAR):
        offset = near_list[0, slot] - leaf_id + 2
        source = lax.dynamic_slice_in_dim(wide, offset * rows, rows, 0)
        gate = (slot < near_count[0]).astype(jnp.float32)
        total = total + kernel_sum(points, xsq, source[:, :width], source[:, width:], gate)
    slots = jnp.arange(FAR, dtype=jnp.int32)[:, None]
    piece = (
        lax.all_gather(skel_rows, "pts", axis=0, tiled=True),
        lax.all_gather(share_w, "pts", axis=0, tiled=True),
    )
    count = piece[0].shape[0]
    node_ids = jnp.arange(count, dtype=jnp.int32) // SKEL
    hits = (far_list[0][:, None] == node_ids[None, :]) & (slots < far_count[0])
    gate = jnp.max(hits.astype(jnp.float32), axis=0)[None, :]
    return total + kernel_sum(points, xsq, piece[0], piece[1], gate)


def solution(mesh):
    in_specs = (
        P("pts", None),
        P("pts", None),
        P(None, "pts"),
        P("pts", None),
        P("pts", None),
        P("pts"),
        P("pts", None),
        P("pts"),
    )
    out_specs = P("pts", None)
    return jax.shard_map(shards, mesh=mesh, in_specs=in_specs, out_specs=out_specs, check_vma=False)
```

profile of v0, /device:TPU:7, one launch (start us, length us, event | category | flops | bytes accessed | tf_op | source)
XLA Modules:
  0.0 249.9 jit_solution(9357158357340823124)
XLA Ops:
  6.6 0.8 fusion.84
  8.1 2.4 gather_fusion
  10.5 0.8 broadcast_select_fusion
  11.4 1.5 fusion.98
  13.9 7.1 %collective-permute-done.4 = bf16[256,512]{1,0:T(8,128)(2,1)S(1)} collective-permute-done((bf16[256,512]{1,0:T(8,128)(2,1)}, bf16[256,512]{1,0:T(8,128)(2,1)S(1)}, u32[]{:S(2)}, u32[]{:S(2)}) %collective-permute-start.4) | collective-permute-done | bytes 262176 | tf_op jit(solution)/shard_map/ppermute | solution.py:16
  21.1 0.8 copy-done.4
  21.9 1.6 collective-permute-start.5
  23.5 1.0 collective-permute-done.5
  24.5 1.6 add_convert_fusion
  26.2 1.1 constant_dynamic-update-slice_fusion.1
  27.3 0.9 constant_dynamic-update-slice_fusion
  28.2 3.1 %collective-permute-start = (bf16[512,1536]{1,0:T(8,128)(2,1)}, bf16[512,1536]{1,0:T(8,128)(2,1)}, u32[]{:S(2)}, u32[]{:S(2)}) collective-permute-start(bf16[512,1536]{1,0:T(8,128)(2,1)} %constant_dynamic-update-slice_fusion), channel_id=1, source_target_pairs={{0,2},{1,3},{2,4},{3,5},{4,6},{5,7},{6,8},{7,9},{8,10},{9,11},{10,... | collective-permute-start | bytes 4718600 | tf_op jit(solution)/shard_map/ppermute | solution.py:22
  31.3 3.6 %collective-permute-start.1 = (bf16[512,1536]{1,0:T(8,128)(2,1)}, bf16[512,1536]{1,0:T(8,128)(2,1)}, u32[]{:S(2)}, u32[]{:S(2)}) collective-permute-start(bf16[512,1536]{1,0:T(8,128)(2,1)} %constant_dynamic-update-slice_fusion), channel_id=1, source_target_pairs={{0,1},{1,2},{2,3},{3,4},{4,5},{5,6},{6,7},{7,8},{8,9},{9,10},{10,1... | collective-permute-start | bytes 4718600 | tf_op jit(solution)/shard_map/ppermute | solution.py:22
  35.0 1.9 collective-permute-start.2
  36.9 2.2 collective-permute-start.3
  44.0 2.2 fusion.21
  46.2 30.8 %collective-permute-done = bf16[512,1536]{1,0:T(8,128)(2,1)} collective-permute-done((bf16[512,1536]{1,0:T(8,128)(2,1)}, bf16[512,1536]{1,0:T(8,128)(2,1)}, u32[]{:S(2)}, u32[]{:S(2)}) %collective-permute-start) | collective-permute-done | bytes 1572896 | tf_op jit(solution)/shard_map/ppermute | solution.py:22
  77.0 1.5 constant_dynamic-update-slice_fusion.6
  78.5 15.7 %collective-permute-done.1 = bf16[512,1536]{1,0:T(8,128)(2,1)} collective-permute-done((bf16[512,1536]{1,0:T(8,128)(2,1)}, bf16[512,1536]{1,0:T(8,128)(2,1)}, u32[]{:S(2)}, u32[]{:S(2)}) %collective-permute-start.1) | collective-permute-done | bytes 1572896 | tf_op jit(solution)/shard_map/ppermute | solution.py:22
  94.2 1.5 constant_dynamic-update-slice_fusion.5
  95.8 1.5 constant_dynamic-update-slice_fusion.3
  97.4 1.5 constant_dynamic-update-slice_fusion.2
  98.9 3.1 %copy-done.3 = bf16[2560,1536]{1,0:T(8,128)(2,1)} copy-done((bf16[2560,1536]{1,0:T(8,128)(2,1)}, bf16[2560,1536]{1,0:T(8,128)(2,1)S(1)}, u32[]{:S(2)}) %copy-start.3) | copy-done | bytes 7864344
  102.0 0.9 multiply_reduce_fusion.3
  102.9 2.5 fusion.27
  105.4 3.4 %fusion.33 = f32[512,512]{1,0:T(8,128)} fusion(bf16[512,1024]{1,0:T(8,128)(2,1)S(1)} %copy-done.1, bf16[2560,1536]{1,0:T(8,128)(2,1)} %copy-done.3, s32[]{:T(128)S(6)} %select_n.71, s32[]{:T(128)S(6)} %add.201, f32[]{:T(128)} %bitcast.8, f32[512]{0:T(512)S(1)} %get-tuple-element.7, f32[512]{0:T(512)S(1)} %multiply_reduce_fusion.5), kind=kOutput, calls=%fused_computation.45 | convolution fusion | flops 806879232 | bytes 3676160 | tf_op jit(solution)/shard_map/dot_general | solution.py:32
  108.8 3.8 %convolution_add_fusion.1 = f32[512,512]{1,0:T(8,128)} fusion(f32[512,512]{1,0:T(8,128)} %fusion.21, bf16[512,1024]{1,0:T(8,128)(2,1)S(1)} %copy-done.1, bf16[2560,1536]{1,0:T(8,128)(2,1)} %copy-done.3, s32[]{:T(128)S(6)} %select_n.69, s32[]{:T(128)S(6)} %add.201, f32[]{:T(128)} %bitcast.2, f32[512]{0:T(512)S(1)} %get-tuple-element.8, ...), kind=kOutput, calls=%fused_computation.28 | convolution fusion | flops 807141376 | bytes 4724736 | tf_op jit(solution)/shard_map/dot_general | solution.py:32
  112.6 49.7 %all-gather.3.cloned.1.call-done = bf16[4096,1024]{1,0:T(8,128)(2,1)} async-done(((bf16[128,1024]{1,0:T(8,128)(2,1)}), bf16[4096,1024]{1,0:T(8,128)(2,1)}) %all-gather.3.cloned.1.call-update) | async-done | bytes 8388624 | tf_op jit(solution)/shard_map/all_gather | solution.py:66
  162.3 5.1 %multiply_reduce_fusion = f32[4096]{0:T(1024)S(1)} fusion(bf16[4096,1024]{1,0:T(8,128)(2,1)} %all-gather.3.cloned.1.call-done), kind=kLoop, calls=%fused_computation.1 | loop fusion | flops 12578816 | bytes 8404992 | tf_op jit(solution)/shard_map/reduce_sum | solution.py:26
  167.4 58.3 %all-gather.5.cloned.1.call-done = bf16[4096,512]{1,0:T(8,128)(2,1)} async-done(((bf16[128,512]{1,0:T(8,128)(2,1)}), bf16[4096,512]{1,0:T(8,128)(2,1)}) %all-gather.5.cloned.1.call-update) | async-done | bytes 4194320 | tf_op jit(solution)/shard_map/all_gather | solution.py:67
  225.7 12.8 %fusion.4 = f32[512,512]{1,0:T(8,128)} fusion(bf16[4096,512]{1,0:T(8,128)(2,1)} %all-gather.5.cloned.1.call-done, bf16[4096,1024]{1,0:T(8,128)(2,1)} %all-gather.3.cloned.1.call-done, bf16[512,1024]{1,0:T(8,128)(2,1)S(1)} %copy-done.1, f32[4096]{0:T(1024)S(1)} %convert_reduce_fusion, f32[4096]{0:T(1024)S(1)} %multiply_reduce_fusion, ...), kind=kOutput, calls=%fused_computation.7 | convolution fusion | flops 6455033856 | bytes 14714880 | tf_op jit(solution)/shard_map/dot_general | solution.py:32
  238.5 4.5 %fusion.14 = f32[512,512]{1,0:T(8,128)} fusion(f32[512,512]{1,0:T(8,128)} %fusion.4, f32[512,512]{1,0:T(8,128)S(1)} %fusion.27, f32[512,512]{1,0:T(8,128)} %fusion.33, f32[512,512]{1,0:T(8,128)} %convolution_add_fusion.1, bf16[512,1024]{1,0:T(8,128)(2,1)S(1)} %copy-done.1, bf16[2560,1536]{1,0:T(8,128)(2,1)} %copy-done.3, s32[]{:T(128)S(6)} %select_n.70, ...), kind=kOutput, calls=%fused_computation.25 | convolution fusion | flops 807927808 | bytes 7870464 | tf_op jit(solution)/shard_map/dot_general | solution.py:32
  (31 shorter events, 3.1 us)
Async XLA Ops:
  6.5 4.9 %copy-start = (bf16[512,512]{1,0:T(8,128)(2,1)S(1)}, bf16[512,512]{1,0:T(8,128)(2,1)}, u32[]{:S(2)}) copy-start(bf16[512,512]{1,0:T(8,128)(2,1)} %param.10) | copy-start | bytes 1572868
  6.5 19.6 %copy-start.1 = (bf16[512,1024]{1,0:T(8,128)(2,1)S(1)}, bf16[512,1024]{1,0:T(8,128)(2,1)}, u32[]{:S(2)}) copy-start(bf16[512,1024]{1,0:T(8,128)(2,1)} %param.8) | copy-start | bytes 3145732
  6.5 20.7 %copy-start.2 = (bf16[512,512]{1,0:T(8,128)(2,1)S(1)}, bf16[512,512]{1,0:T(8,128)(2,1)}, u32[]{:S(2)}) copy-start(bf16[512,512]{1,0:T(8,128)(2,1)} %param.9) | copy-start | bytes 1572868
  6.5 33.2 %copy-start.5 = (s32[1,4]{1,0:T(1,128)S(1)}, s32[1,4]{1,0:T(1,128)}, u32[]{:S(2)}) copy-start(s32[1,4]{1,0:T(1,128)} %param.12) | copy-start | bytes 52
  6.5 37.0 %copy-start.6 = (s32[1,4]{1,0:T(1,128)S(1)}, s32[1,4]{1,0:T(1,128)}, u32[]{:S(2)}) copy-start(s32[1,4]{1,0:T(1,128)} %param.14) | copy-start | bytes 52
  6.5 155.8 %all-gather.3.cloned.1.call-start = ((), (), s32[]{:S(2)}) async-start(), calls=%async_computation | async-start | bytes 8650752 | tf_op jit(solution)/shard_map/all_gather | solution.py:66
  11.3 214.4 %all-gather.5.cloned.1.call-start = ((), (), s32[]{:S(2)}) async-start(), calls=%async_computation.1 | async-start | bytes 4325376 | tf_op jit(solution)/shard_map/all_gather | solution.py:67
  13.6 7.4 %collective-permute-start.4 = (bf16[256,512]{1,0:T(8,128)(2,1)}, bf16[256,512]{1,0:T(8,128)(2,1)S(1)}, u32[]{:S(2)}, u32[]{:S(2)}) collective-permute-start(bf16[256,512]{1,0:T(8,128)(2,1)} %dynamic-slice_convert_fusion), channel_id=1, source_target_pairs={{0,2},{1,3},{2,0},{3,1},{4,6},{5,7},{6,4},{7,5},{8,10},{9,11},{10,... | collective-permute-start | bytes 786440 | tf_op jit(solution)/shard_map/ppermute | solution.py:16
  21.1 0.8 copy-start.4
  21.9 2.6 %collective-permute-start.5 = (bf16[128,512]{1,0:T(8,128)(2,1)S(1)}, bf16[128,512]{1,0:T(8,128)(2,1)S(1)}, u32[]{:S(2)}, u32[]{:S(2)}) collective-permute-start(bf16[128,512]{1,0:T(8,128)(2,1)S(1)} %dynamic-slice_convert_fusion.1), channel_id=1, source_target_pairs={{0,1},{1,0},{2,3},{3,2},{4,5},{5,4},{6,7},{7,6},{8,9},{9,8},{10,11... | collective-permute-start | bytes 393224 | tf_op jit(solution)/shard_map/ppermute | solution.py:16
  28.2 48.8 %collective-permute-start = (bf16[512,1536]{1,0:T(8,128)(2,1)}, bf16[512,1536]{1,0:T(8,128)(2,1)}, u32[]{:S(2)}, u32[]{:S(2)}) collective-permute-start(bf16[512,1536]{1,0:T(8,128)(2,1)} %constant_dynamic-update-slice_fusion), channel_id=1, source_target_pairs={{0,2},{1,3},{2,4},{3,5},{4,6},{5,7},{6,8},{7,9},{8,10},{9,11},{10,... | collective-permute-start | bytes 4718600 | tf_op jit(solution)/shard_map/ppermute | solution.py:22
  31.3 62.9 %collective-permute-start.1 = (bf16[512,1536]{1,0:T(8,128)(2,1)}, bf16[512,1536]{1,0:T(8,128)(2,1)}, u32[]{:S(2)}, u32[]{:S(2)}) collective-permute-start(bf16[512,1536]{1,0:T(8,128)(2,1)} %constant_dynamic-update-slice_fusion), channel_id=1, source_target_pairs={{0,1},{1,2},{2,3},{3,4},{4,5},{5,6},{6,7},{7,8},{8,9},{9,10},{10,1... | collective-permute-start | bytes 4718600 | tf_op jit(solution)/shard_map/ppermute | solution.py:22
  35.0 60.9 %collective-permute-start.2 = (bf16[512,1536]{1,0:T(8,128)(2,1)}, bf16[512,1536]{1,0:T(8,128)(2,1)}, u32[]{:S(2)}, u32[]{:S(2)}) collective-permute-start(bf16[512,1536]{1,0:T(8,128)(2,1)} %constant_dynamic-update-slice_fusion), channel_id=1, source_target_pairs={{1,0},{2,1},{3,2},{4,3},{5,4},{6,5},{7,6},{8,7},{9,8},{10,9},{11,1... | collective-permute-start | bytes 4718600 | tf_op jit(solution)/shard_map/ppermute | solution.py:22
  36.9 60.5 %collective-permute-start.3 = (bf16[512,1536]{1,0:T(8,128)(2,1)}, bf16[512,1536]{1,0:T(8,128)(2,1)}, u32[]{:S(2)}, u32[]{:S(2)}) collective-permute-start(bf16[512,1536]{1,0:T(8,128)(2,1)} %constant_dynamic-update-slice_fusion), channel_id=1, source_target_pairs={{2,0},{3,1},{4,2},{5,3},{6,4},{7,5},{8,6},{9,7},{10,8},{11,9},{12,... | collective-permute-start | bytes 4718600 | tf_op jit(solution)/shard_map/ppermute | solution.py:22
  98.9 3.1 %copy-start.3 = (bf16[2560,1536]{1,0:T(8,128)(2,1)}, bf16[2560,1536]{1,0:T(8,128)(2,1)S(1)}, u32[]{:S(2)}) copy-start(bf16[2560,1536]{1,0:T(8,128)(2,1)S(1)} %constant_dynamic-update-slice_fusion.2) | copy-start | bytes 23592964
Sparse Core Ops, SparseCore 0:
  11.4 150.8 all-gather.2
  165.2 60.4 all-gather.4
where the time goes:
time: 253 us; the launch traced here: 250 us
  waiting for transfers between devices  163 us (64%)
  matrix products  30.8 us (12%)
  between operations  17.5 us (7%)
  local copies, waits for them, and re-layouts  15.9 us (6%)
  starting transfers between devices  12.8 us (5%)
  other arithmetic  10.4 us (4%)
    all_gather x1, waiting for transfers between devices, shards(): lax.all_gather(share_w, 'pts', axis=0, tiled=True)  58.3 us
    all_gather x1, waiting for transfers between devices, shards(): lax.all_gather(skel_rows, 'pts', axis=0, tiled=True)  49.7 us
    ppermute x4, waiting for transfers between devices, shifted(): lax.ppermute(value, axis, [(source, source + steps) for source in range(l...  46.5 us
    dot_general x6, matrix products, kernel_sum(): return jnp.dot(kern, wts, preferred_element_type=jnp.float32)  29.3 us
    ppermute x4, starting transfers between devices, shifted(): lax.ppermute(value, axis, [(source, source + steps) for source in range(l...  10.8 us
    unnamed x20, local copies, waits for them, and re-layouts  9.64 us
    ppermute x2, waiting for transfers between devices, partner(): return lax.ppermute(value, axis, pairs)  8.12 us
    reduce_sum x2, other arithmetic, kernel_sum(): ysq = jnp.sum(jnp.square(ypts.astype(jnp.float32)), axis=1)  5.98 us
  transfers between devices with their start and end apart: 8, of which 6 were waited for; matrix products, arithmetic and copies ran while one was open for 12% of the time, Pallas kernels for 0%

commit v1 on v0

v1 whole, which is shorter than its diff:
```python
import functools

import jax
import jax.numpy as jnp
from jax import lax
from jax.experimental import pallas as pl
from jax.experimental.pallas import tpu as pltpu
from jax.sharding import PartitionSpec as P

NODES = 8
NEAR = 4
FAR = 4
QUAD = 4
F32 = jnp.float32
BF16 = jnp.bfloat16
MIB = 1 << 20

NEAR_COUNT = NEAR
FAR_LIST = NEAR + 1
FAR_COUNT = FAR_LIST + FAR
LEAF = FAR_COUNT + 1
META = 16


def vmem():
    return pl.BlockSpec(memory_space=pltpu.VMEM)


def smem():
    return pl.BlockSpec(memory_space=pltpu.SMEM)


def params():
    return pltpu.CompilerParams(vmem_limit_bytes=48 * MIB)


def norm_column(points):
    wide = points.astype(F32)
    return jnp.sum(wide * wide, axis=1, keepdims=True)


def norm_row(points):
    column = norm_column(points)
    return jnp.transpose(jnp.broadcast_to(column, (column.shape[0], 128)))[0:1, :]


def listed(meta, row, first, count, value):
    hit = jnp.bool_(False)
    for slot in range(count):
        hit = hit | ((meta[row, first + slot] == value) & (slot < meta[row, first + count]))
    return hit


def near_hit(meta, row, leaf):
    return listed(meta, row, 0, NEAR, leaf)


def far_hit(meta, row, node):
    return listed(meta, row, FAR_LIST, FAR, node)


def add_terms(acc, xpts, xsq, ypts, ysq, wts, gate):
    rows = xpts.shape[0]
    step = min(256, rows)
    dim = xpts.shape[1]
    for first in range(0, rows, step):
        part = pl.ds(first, step)
        scores = lax.dot_general(
            xpts[part, :], ypts, (((1,), (1,)), ((), ())), preferred_element_type=F32
        )
        dist = xsq[first : first + step] + ysq - 2.0 * scores
        kern = jnp.exp(dist * (-0.5 / dim))
        if gate is not None:
            kern = kern * gate
        acc[part, :] += jnp.dot(kern.astype(BF16), wts, preferred_element_type=F32)


def prepare_body(group, idx, pts, wts, proj, skel, keep, give, whole):
    core = lax.axis_index("pts") % 2
    rows = pts.shape[0]
    count = idx.shape[1]
    whole[...] = jnp.dot(proj[...], wts[...], preferred_element_type=F32).reshape(whole.shape)
    keep[...] = whole[:, core]
    give[...] = whole[:, 1 - core].astype(BF16)
    place = lax.broadcasted_iota(jnp.int32, (rows, count), 0)
    pick = (place == idx[...]).astype(F32).astype(BF16)
    skel[...] = lax.dot_general(
        pick, pts[...], (((0,), (0,)), ((), ())), preferred_element_type=F32
    ).astype(BF16)


def prepare(group, pts, wts, proj, idx):
    count = idx.shape[1]
    wcols = wts.shape[1]
    half = (group // 2, count, wcols)
    return pl.pallas_call(
        functools.partial(prepare_body, group),
        out_shape=(
            jax.ShapeDtypeStruct((count, pts.shape[1]), BF16),
            jax.ShapeDtypeStruct(half, F32),
            jax.ShapeDtypeStruct(half, BF16),
        ),
        in_specs=[vmem()] * 4,
        out_specs=(vmem(),) * 3,
        scratch_shapes=[pltpu.VMEM((group // 2, 2, count, wcols), F32)],
        compiler_params=params(),
        cost_estimate=pl.CostEstimate(
            flops=2 * proj.size * wcols + 2 * count * pts.size, bytes_accessed=4 * MIB, transcendentals=0
        ),
    )(idx, pts, wts, proj)


def own_body(meta, ypts, wts, *refs):
    leaf = meta[0, LEAF]
    count = len(refs) // 2
    ysq = norm_row(ypts[...])
    for place in range(count):
        xpts, acc = refs[place], refs[count + place]
        acc[...] = jnp.zeros_like(acc)
        row = meta.shape[0] - count + place if meta.shape[0] > 1 else 0

        def work(xpts=xpts, acc=acc):
            add_terms(acc, xpts, norm_column(xpts[...]), ypts[...], ysq, wts[...], None)

        if row == 0:
            work()
        else:
            pl.when(near_hit(meta, row, leaf))(work)


def pair_cost(pairs, rows, dim, wcols):
    return pl.CostEstimate(
        flops=2 * pairs * rows * rows * (dim + wcols),
        bytes_accessed=pairs * rows * (2 * dim + 4 * wcols),
        transcendentals=pairs * rows * rows,
    )


def own_terms(meta, ypts, wts, targets):
    rows, wcols = wts.shape
    return pl.pallas_call(
        own_body,
        out_shape=(jax.ShapeDtypeStruct((rows, wcols), F32),) * len(targets),
        in_specs=[smem()] + [vmem()] * (2 + len(targets)),
        out_specs=(vmem(),) * len(targets),
        compiler_params=params(),
        cost_estimate=pair_cost(len(targets), rows, ypts.shape[1], wcols),
    )(meta, ypts, wts, *targets)


def far_body(group, flip, turns, first, targets, casts, meta, *refs):
    shards = len(turns)
    skel, wts = refs[:shards], refs[shards : 2 * shards]
    xpts = refs[2 * shards : 2 * shards + targets]
    start = refs[2 * shards + targets : 2 * shards + 2 * targets]
    outs = refs[2 * shards + 2 * targets : 2 * shards + 3 * targets]
    work = refs[2 * shards + 3 * targets]
    quads = lax.axis_size("pts") // QUAD
    mine = meta[0, LEAF] // QUAD
    count = skel[0].shape[0]
    nodes = []
    for turn in turns:
        deep = (mine // 2 - turn + quads // 2) % (quads // 2)
        side = (mine + flip) % 2
        nodes.append((deep * 2 + side) * QUAD // group)
    per = max(1, min(shards, 256 // count))
    squares = [norm_row(ref[...]) for ref in skel]
    for place in range(targets):
        work[...] = start[place][...]
        xsq = norm_column(xpts[place][...])
        for low in range(0, shards, per):
            high = min(shards, low + per)
            hits = [far_hit(meta, first + place, node) for node in nodes[low:high]]
            some = functools.reduce(jnp.logical_or, hits)

            @pl.when(some)
            def _(place=place, xsq=xsq, low=low, high=high, hits=hits):
                gate = jnp.concatenate(
                    [jnp.full((1, count), hit.astype(F32), F32) for hit in hits], axis=1
                )
                ysq = jnp.concatenate(squares[low:high], axis=1)
                ypts = jnp.concatenate([ref[...] for ref in skel[low:high]], axis=0)
                values = jnp.concatenate([ref[...] for ref in wts[low:high]], axis=0)
                add_terms(work, xpts[place], xsq, ypts, ysq, values, gate)

        outs[place][...] = work[...].astype(outs[place].dtype)


def far_terms(group, flip, turns, first, meta, skel, wts, xpts, start, kinds):
    rows, wcols = start[0].shape
    targets = len(xpts)
    return pl.pallas_call(
        functools.partial(far_body, group, flip, turns, first, targets, kinds),
        out_shape=tuple(jax.ShapeDtypeStruct((rows, wcols), kind) for kind in kinds),
        in_specs=[smem()] + [vmem()] * (2 * len(skel) + 2 * targets),
        out_specs=(vmem(),) * targets,
        scratch_shapes=[pltpu.VMEM((rows, wcols), F32)],
        compiler_params=params(),
        cost_estimate=pair_cost(targets, rows, xpts[0].shape[1], wcols),
    )(meta, *skel, *wts, *xpts, *start)


def cross_body(meta, xpts, start, extra, *refs):
    leaf = meta[0, LEAF]
    outer = leaf // 2 % 2
    ways = (2 * outer - 1, 2 * (2 * outer - 1))
    acc = refs[-1]
    acc[...] = start[...] + extra[...].astype(F32)
    xsq = norm_column(xpts[...])
    for place, way in ((0, ways[1]), (1, ways[0])):
        ypts, wts = refs[2 * place], refs[2 * place + 1]
        hit = near_hit(meta, 0, leaf + way)
        if place == 1:
            hit = hit & (leaf % 2 == outer)

        @pl.when(hit)
        def _(ypts=ypts, wts=wts):
            add_terms(acc, xpts, xsq, ypts[...], norm_row(ypts[...]), wts[...], None)


def cross_terms(meta, xpts, start, extra, sources):
    return pl.pallas_call(
        cross_body,
        out_shape=jax.ShapeDtypeStruct(start.shape, F32),
        in_specs=[smem()] + [vmem()] * (3 + len(sources)),
        out_specs=vmem(),
        compiler_params=params(),
        cost_estimate=pair_cost(2, start.shape[0], xpts.shape[1], start.shape[1]),
    )(meta, xpts, start, extra, *sources)


def shards(points, weights, node_proj, skel_idx, near_list, near_count, far_list, far_count):
    leaves = lax.axis_size("pts")
    me = lax.axis_index("pts")
    group = leaves // NODES
    quads = leaves // QUAD
    depth = quads // 2

    def move(value, where):
        pairs = [(source, where(source)) for source in range(leaves)]
        return lax.ppermute(value, "pts", [(a, b) for a, b in pairs if b is not None])

    def bit(level):
        return lambda source: source ^ (1 << level)

    def deeper(turn):
        def where(source):
            quad, place = divmod(source, QUAD)
            deep, side = divmod(quad, 2)
            return ((deep + turn) % depth * 2 + side) * QUAD + place

        return where

    def across(source):
        target = source + 2 if source // 2 % 2 else source - 2
        return target if 0 <= target < leaves else None

    def inward(source):
        return source ^ 1 if source % 2 != source // 2 % 2 else None

    core, side, row = bit(0), bit(1), bit(2)

    meta = jnp.concatenate(
        [near_list[0], near_count, far_list[0], far_count, me[None], jnp.zeros((META - LEAF - 1,), jnp.int32)]
    )[None]
    meta = jnp.concatenate([meta, move(meta, core)], axis=0)
    meta = jnp.concatenate([meta, move(meta, side)], axis=0)

    skel, keep, give = prepare(group, points, weights, node_proj, skel_idx)

    level = 0
    while True:
        keep = keep + move(give, bit(level)).astype(F32)
        level += 1
        if keep.shape[0] == 1:
            break
        count = keep.shape[0]
        keep = keep.reshape(count // 2, 2, *keep.shape[1:])
        upper = (me >> level) % 2 == 1
        give = jnp.where(upper, keep[:, 0], keep[:, 1]).astype(BF16)
        keep = jnp.where(upper, keep[:, 1], keep[:, 0])
    share = keep[0].astype(BF16)

    pts_core = move(points, core)
    pts_side = move(points, side)
    pts_both = move(pts_side, core)

    skel_z = [skel] + [move(skel, deeper(turn)) for turn in range(1, depth)]
    share_z = [share] + [move(share, deeper(turn)) for turn in range(1, depth)]
    skel_y = [move(value, row) for value in skel_z]
    share_y = [move(value, row) for value in share_z]

    cross_p = move(points, across)
    cross_w = move(weights, across)
    cross_pm = move(cross_p, inward)
    cross_wm = move(cross_w, inward)

    turns = tuple(range(depth))
    acc0, acc1 = own_terms(meta[:2], points, weights, (points, pts_core))
    acc2, acc3 = own_terms(meta, points, weights, (pts_side, pts_both))
    acc0, acc1, acc2, acc3 = far_terms(
        group, 0, turns, 0, meta, skel_z, share_z,
        (points, pts_core, pts_side, pts_both), (acc0, acc1, acc2, acc3), (F32,) * 4,
    )
    acc2, out3 = far_terms(
        group, 1, turns, 2, meta, skel_y, share_y, (pts_side, pts_both), (acc2, acc3), (F32, BF16)
    )
    out2 = (acc2 + move(out3, core).astype(F32)).astype(BF16)
    last = move(out2, side)
    acc0, out1 = far_terms(
        group, 1, turns, 0, meta, skel_y, share_y, (points, pts_core), (acc0, acc1), (F32, BF16)
    )
    extra = move(out1, core)
    total = cross_terms(meta, points, acc0, extra, (cross_p, cross_w, cross_pm, cross_wm))
    return total + last.astype(F32)


def solution(mesh):
    in_specs = (
        P("pts", None),
        P("pts", None),
        P(None, "pts"),
        P("pts", None),
        P("pts", None),
        P("pts"),
        P("pts", None),
        P("pts"),
    )
    out_specs = P("pts", None)
    return jax.shard_map(shards, mesh=mesh, in_specs=in_specs, out_specs=out_specs, check_vma=False)
```

time: 253 us -> 138 us (0.55)
  waiting for transfers between devices: 163 us -> 50.2 us
  Pallas kernels: 0 us -> 32 us
  matrix products: 30.8 us -> 0 us
  starting transfers between devices: 12.8 us -> 38.8 us
  between operations: 17.5 us -> 1.63 us
  other arithmetic: 10.4 us -> 2.41 us
  local copies, waits for them, and re-layouts: 15.9 us -> 10.4 us
    all_gather x2 -> x0, waiting for transfers between devices: 108 us -> none  [the longest x1 58.3 us: shards(): lax.all_gather(share_w, 'pts', axis=0, tiled=True)]
    pallas_call x0 -> x7, Pallas kernels: none -> 32 us  [the longest x3 19.8 us: far_terms(): pl.pallas_call(functools.partial(far_body, group, flip, turns, first, tar...]
    dot_general x7 -> x0, matrix products: 30.8 us -> none  [the longest x6 29.3 us: kernel_sum(): return jnp.dot(kern, wts, preferred_element_type=jnp.float32)]
    ppermute x6 -> x28, starting transfers between devices: 12.7 us -> 38.8 us  [move(): lax.ppermute(value, 'pts', [(a, b) for a, b in pairs if b is not None])]
    reduce_sum x3 -> x0, other arithmetic: 6.26 us -> none  [the longest x2 5.98 us: kernel_sum(): ysq = jnp.sum(jnp.square(ypts.astype(jnp.float32)), axis=1)]
    ppermute x6 -> x28, waiting for transfers between devices: 54.6 us -> 50.2 us  [move(): lax.ppermute(value, 'pts', [(a, b) for a, b in pairs if b is not None])]
    unnamed x20 -> x42, local copies, waits for them, and re-layouts: 9.64 us -> 10.3 us
  transfers between devices with their start and end apart: 8 -> 28, of which waited for: 6 -> 8; matrix products, arithmetic and copies ran while one was open for 12% -> 1% of each run, Pallas kernels for 0% -> 24%
where the time goes in v1:
time: 138 us; the launch traced here: 135 us
  waiting for transfers between devices  50.2 us (36%)
  starting transfers between devices  38.8 us (28%)
  Pallas kernels  32 us (23%)
  local copies, waits for them, and re-layouts  10.4 us (8%)
  other arithmetic  2.41 us (2%)
  between operations  1.63 us (1%)
    ppermute x28, waiting for transfers between devices, move(): lax.ppermute(value, 'pts', [(a, b) for a, b in pairs if b is not None])  50.2 us
    ppermute x28, starting transfers between devices, move(): lax.ppermute(value, 'pts', [(a, b) for a, b in pairs if b is not None])  38.8 us
    pallas_call x3, Pallas kernels, far_terms(): pl.pallas_call(functools.partial(far_body, group, flip, turns, first, tar...  19.8 us
    unnamed x42, local copies, waits for them, and re-layouts  10.3 us
    pallas_call x2, Pallas kernels, own_terms(): pl.pallas_call(own_body, out_shape=(jax.ShapeDtypeStruct((rows, wcols), F...  7.15 us
    pallas_call x1, Pallas kernels, cross_terms(): pl.pallas_call(cross_body, out_shape=jax.ShapeDtypeStruct(start.shape, F3...  3.19 us
  transfers between devices with their start and end apart: 28, of which 8 were waited for; matrix products, arithmetic and copies ran while one was open for 1% of the time, Pallas kernels for 24%

profile of v1, /device:TPU:7, one launch (start us, length us, event | category | flops | bytes accessed | tf_op | source)
XLA Modules:
  0.0 135.4 jit_solution(12541822636245763567)
XLA Ops:
  0.3 1.0 copy-done
  3.0 1.9 %shard_map.82 = (bf16[128,1024]{1,0:T(8,128)(2,1)S(1)}, f32[2,128,512]{2,1,0:T(8,128)S(1)}, bf16[2,128,512]{2,1,0:T(8,128)(2,1)S(1)}) custom-call(s32[1,128]{1,0:T(1,128)S(1)} %copy-done.3, bf16[512,1024]{1,0:T(8,128)(2,1)} %xpts.1, bf16[512,512]{1,0:T(8,128)(2,1)S(1)} %copy-done.1, bf16[512,512]{1,0:T(8,128)(2,1)S(1)} %copy-done), custom_call_target="tpu_custom_call" | custom-call | flops 402653184 | bytes 4194304 | tf_op jit(solution)/shard_map/pallas_call | solution.py:96
  8.5 1.3 collective-permute-start.3
  9.8 2.3 %collective-permute-start.5 = (bf16[128,1024]{1,0:T(8,128)(2,1)S(1)}, bf16[128,1024]{1,0:T(8,128)(2,1)S(1)}, u32[]{:S(2)}, u32[]{:S(2)}) collective-permute-start(bf16[128,1024]{1,0:T(8,128)(2,1)S(1)} %get-tuple-element.20.refs_0_), channel_id=1, source_target_pairs={{0,16},{1,17},{2,18},{3,19},{4,20},{5,21},{6,22},{7,23},{8,24},{9,... | collective-permute-start | bytes 786440 | tf_op jit(solution)/shard_map/ppermute | solution.py:241
  12.1 1.3 collective-permute-start.1
  13.4 10.8 %collective-permute-done.19.refs_0_.refs_10_.refs_8_ = bf16[512,1024]{1,0:T(8,128)(2,1)S(1)} collective-permute-done((bf16[512,1024]{1,0:T(8,128)(2,1)}, bf16[512,1024]{1,0:T(8,128)(2,1)S(1)}, u32[]{:S(2)}, u32[]{:S(2)}) %collective-permute-start.19) | collective-permute-done | bytes 1048608 | tf_op jit(solution)/shard_map/ppermute | solution.py:241
  24.2 1.6 %collective-permute-start.20 = (bf16[512,1024]{1,0:T(8,128)(2,1)S(1)}, bf16[512,1024]{1,0:T(8,128)(2,1)S(1)}, u32[]{:S(2)}, u32[]{:S(2)}) collective-permute-start(bf16[512,1024]{1,0:T(8,128)(2,1)S(1)} %collective-permute-done.19.refs_0_.refs_10_.refs_8_), channel_id=1, source_target_pairs={{0,1},{1,0},{2,3},{3,2},{4,5},{5,4},{6,7},{7,6},{8,9},{9,8},{10,11... | collective-permute-start | bytes 3145736 | tf_op jit(solution)/shard_map/ppermute | solution.py:241
  27.2 3.3 %collective-permute-start.7 = (bf16[128,1024]{1,0:T(8,128)(2,1)S(1)}, bf16[128,1024]{1,0:T(8,128)(2,1)S(1)}, u32[]{:S(2)}, u32[]{:S(2)}) collective-permute-start(bf16[128,1024]{1,0:T(8,128)(2,1)S(1)} %get-tuple-element.20.refs_0_), channel_id=1, source_target_pairs={{0,24},{1,25},{2,26},{3,27},{4,28},{5,29},{6,30},{7,31},{8,0},{9,1... | collective-permute-start | bytes 786440 | tf_op jit(solution)/shard_map/ppermute | solution.py:241
  30.8 1.1 collective-permute-done.10
  31.9 3.1 %collective-permute-start.22 = (bf16[512,1024]{1,0:T(8,128)(2,1)}, bf16[512,1024]{1,0:T(8,128)(2,1)S(1)}, u32[]{:S(2)}, u32[]{:S(2)}) collective-permute-start(bf16[512,1024]{1,0:T(8,128)(2,1)} %xpts.1), channel_id=1, source_target_pairs={{2,4},{3,5},{4,2},{5,3},{6,8},{7,9},{8,6},{9,7},{10,12},{11,13},{1... | collective-permute-start | bytes 3145736 | tf_op jit(solution)/shard_map/ppermute | solution.py:241
  36.4 1.2 collective-permute-done.2.refs_0_
  37.9 23.2 %collective-permute-done.12.refs_5_ = bf16[128,512]{1,0:T(8,128)(2,1)S(1)} collective-permute-done((bf16[128,512]{1,0:T(8,128)(2,1)S(1)}, bf16[128,512]{1,0:T(8,128)(2,1)S(1)}, u32[]{:S(2)}, u32[]{:S(2)}) %collective-permute-start.12) | collective-permute-done | bytes 131104 | tf_op jit(solution)/shard_map/ppermute | solution.py:241
  61.0 3.3 %collective-permute-start.14 = (bf16[128,512]{1,0:T(8,128)(2,1)S(1)}, bf16[128,512]{1,0:T(8,128)(2,1)S(1)}, u32[]{:S(2)}, u32[]{:S(2)}) collective-permute-start(bf16[128,512]{1,0:T(8,128)(2,1)S(1)} %fusion.2.refs_4_), channel_id=1, source_target_pairs={{0,16},{1,17},{2,18},{3,19},{4,20},{5,21},{6,22},{7,23},{8,24},{9,... | collective-permute-start | bytes 393224 | tf_op jit(solution)/shard_map/ppermute | solution.py:241
  64.4 4.3 %shard_map.83 = (f32[512,512]{1,0:T(8,128)S(1)}, f32[512,512]{1,0:T(8,128)S(1)}) custom-call(s32[2,16]{1,0:T(2,128)S(1)} %pad_add_fusion.1.meta, bf16[512,1024]{1,0:T(8,128)(2,1)} %xpts.1, bf16[512,512]{1,0:T(8,128)(2,1)S(1)} %copy-done.2, bf16[512,1024]{1,0:T(8,128)(2,1)} %xpts.1, bf16[512,1024]{1,0:T(8,128)(2,1)S(1)} %collective-permute-done.18.refs_1_.refs_9_), custom_call_target="tpu_custom_call" | custom-call | flops 1610612736 | bytes 4194304 | tf_op jit(solution)/shard_map/pallas_call | solution.py:141
  70.6 3.7 %collective-permute-start.16 = (bf16[128,512]{1,0:T(8,128)(2,1)S(1)}, bf16[128,512]{1,0:T(8,128)(2,1)S(1)}, u32[]{:S(2)}, u32[]{:S(2)}) collective-permute-start(bf16[128,512]{1,0:T(8,128)(2,1)S(1)} %fusion.2.refs_4_), channel_id=1, source_target_pairs={{0,24},{1,25},{2,26},{3,27},{4,28},{5,29},{6,30},{7,31},{8,0},{9,1... | collective-permute-start | bytes 393224 | tf_op jit(solution)/shard_map/ppermute | solution.py:241
  74.3 1.1 collective-permute-start.11
  75.3 2.9 %shard_map.84 = (f32[512,512]{1,0:T(8,128)S(1)}, f32[512,512]{1,0:T(8,128)S(1)}) custom-call(s32[4,16]{1,0:T(4,128)S(1)} %pad_add_fusion.meta, bf16[512,1024]{1,0:T(8,128)(2,1)} %xpts.1, bf16[512,512]{1,0:T(8,128)(2,1)S(1)} %copy-done.2, bf16[512,1024]{1,0:T(8,128)(2,1)S(1)} %collective-permute-done.19.refs_0_.refs_10_.refs_8_, ...), custom_call_target="tpu_custom_call" | custom-call | flops 1610612736 | bytes 4194304 | tf_op jit(solution)/shard_map/pallas_call | solution.py:141
  80.6 1.1 collective-permute-start.13
  82.1 1.1 collective-permute-start.17
  83.2 10.9 %shard_map.85 = (f32[512,512]{1,0:T(8,128)S(1)}, f32[512,512]{1,0:T(8,128)S(1)}, f32[512,512]{1,0:T(8,128)S(1)}, f32[512,512]{1,0:T(8,128)S(1)}) custom-call(s32[4,16]{1,0:T(4,128)S(1)} %pad_add_fusion.meta, bf16[128,1024]{1,0:T(8,128)(2,1)S(1)} %get-tuple-element.20.refs_0_, bf16[128,1024]{1,0:T(8,128)(2,1)S(1)} %collective-permute-done.3.refs_1_, ...), custom_call_target="tpu_custom_call" | custom-call | flops 3221225472 | bytes 8388608 | tf_op jit(solution)/shard_map/pallas_call | solution.py:192
  97.0 1.9 %collective-permute-start.23 = (bf16[512,512]{1,0:T(8,128)(2,1)S(1)}, bf16[512,512]{1,0:T(8,128)(2,1)S(1)}, u32[]{:S(2)}, u32[]{:S(2)}) collective-permute-start(bf16[512,512]{1,0:T(8,128)(2,1)S(1)} %copy-done.2), channel_id=1, source_target_pairs={{2,4},{3,5},{4,2},{5,3},{6,8},{7,9},{8,6},{9,7},{10,12},{11,13},{1... | collective-permute-start | bytes 1572872 | tf_op jit(solution)/shard_map/ppermute | solution.py:241
  99.0 4.8 %shard_map.88 = (f32[512,512]{1,0:T(8,128)S(1)}, bf16[512,512]{1,0:T(8,128)(2,1)S(1)}) custom-call(s32[4,16]{1,0:T(4,128)S(1)} %pad_add_fusion.meta, bf16[128,1024]{1,0:T(8,128)(2,1)S(1)} %collective-permute-done.2.refs_0_, bf16[128,1024]{1,0:T(8,128)(2,1)S(1)} %collective-permute-done.4.refs_1_, bf16[128,1024]{1,0:T(8,128)(2,1)S(1)} %collective-permute-done.6.refs_2_, ...), custom_call_target="tpu_custom_call" | custom-call | flops 1610612736 | bytes 4194304 | tf_op jit(solution)/shard_map/pallas_call | solution.py:192
  103.8 3.5 %collective-permute-start.26 = (bf16[512,512]{1,0:T(8,128)(2,1)S(1)}, bf16[512,512]{1,0:T(8,128)(2,1)S(1)}, u32[]{:S(2)}, u32[]{:S(2)}) collective-permute-start(bf16[512,512]{1,0:T(8,128)(2,1)S(1)} %get-tuple-element.34), channel_id=1, source_target_pairs={{0,1},{1,0},{2,3},{3,2},{4,5},{5,4},{6,7},{7,6},{8,9},{9,8},{10,11... | collective-permute-start | bytes 1572872 | tf_op jit(solution)/shard_map/ppermute | solution.py:241
  107.3 1.3 collective-permute-start.24
  108.6 2.8 %collective-permute-done.23.refs_1_ = bf16[512,512]{1,0:T(8,128)(2,1)S(1)} collective-permute-done((bf16[512,512]{1,0:T(8,128)(2,1)S(1)}, bf16[512,512]{1,0:T(8,128)(2,1)S(1)}, u32[]{:S(2)}, u32[]{:S(2)}) %collective-permute-start.23) | collective-permute-done | bytes 524320 | tf_op jit(solution)/shard_map/ppermute | solution.py:241
  111.4 1.3 collective-permute-start.25
  112.7 4.1 %shard_map.86 = (f32[512,512]{1,0:T(8,128)S(1)}, bf16[512,512]{1,0:T(8,128)(2,1)S(1)}) custom-call(s32[4,16]{1,0:T(4,128)S(1)} %pad_add_fusion.meta, bf16[128,1024]{1,0:T(8,128)(2,1)S(1)} %collective-permute-done.2.refs_0_, bf16[128,1024]{1,0:T(8,128)(2,1)S(1)} %collective-permute-done.4.refs_1_, bf16[128,1024]{1,0:T(8,128)(2,1)S(1)} %collective-permute-done.6.refs_2_, ...), custom_call_target="tpu_custom_call" | custom-call | flops 1610612736 | bytes 4194304 | tf_op jit(solution)/shard_map/pallas_call | solution.py:192
  116.8 3.7 %collective-permute-start.21 = (bf16[512,512]{1,0:T(8,128)(2,1)S(1)}, bf16[512,512]{1,0:T(8,128)(2,1)S(1)}, u32[]{:S(2)}, u32[]{:S(2)}) collective-permute-start(bf16[512,512]{1,0:T(8,128)(2,1)S(1)} %get-tuple-element.30), channel_id=1, source_target_pairs={{0,1},{1,0},{2,3},{3,2},{4,5},{5,4},{6,7},{7,6},{8,9},{9,8},{10,11... | collective-permute-start | bytes 1572872 | tf_op jit(solution)/shard_map/ppermute | solution.py:241
  120.8 1.3 collective-permute-done.21.extra
  122.1 3.2 %shard_map.87 = f32[512,512]{1,0:T(8,128)S(1)} custom-call(s32[4,16]{1,0:T(4,128)S(1)} %pad_add_fusion.meta, bf16[512,1024]{1,0:T(8,128)(2,1)} %xpts.1, f32[512,512]{1,0:T(8,128)S(1)} %get-tuple-element.29.start, bf16[512,512]{1,0:T(8,128)(2,1)S(1)} %collective-permute-done.21.extra, bf16[512,1024]{1,0:T(8,128)(2,1)S(1)} %collective-permute-done.22.refs_0_, ...), custom_call_target="tpu_custom_call" | custom-call | flops 1610612736 | bytes 4194304 | tf_op jit(solution)/shard_map/pallas_call | solution.py:222
  125.3 9.0 %collective-permute-done.27 = bf16[512,512]{1,0:T(8,128)(2,1)S(1)} collective-permute-done((bf16[512,512]{1,0:T(8,128)(2,1)S(1)}, bf16[512,512]{1,0:T(8,128)(2,1)S(1)}, u32[]{:S(2)}, u32[]{:S(2)}) %collective-permute-start.27) | collective-permute-done | bytes 524320 | tf_op jit(solution)/shard_map/ppermute | solution.py:241
  134.3 1.1 convert_add_fusion
  (82 shorter events, 15.5 us)
Async XLA Ops:
  0.0 24.2 %collective-permute-start.19 = (bf16[512,1024]{1,0:T(8,128)(2,1)}, bf16[512,1024]{1,0:T(8,128)(2,1)S(1)}, u32[]{:S(2)}, u32[]{:S(2)}) collective-permute-start(bf16[512,1024]{1,0:T(8,128)(2,1)} %xpts.1), channel_id=1, source_target_pairs={{0,2},{1,3},{2,0},{3,1},{4,6},{5,7},{6,4},{7,5},{8,10},{9,11},{10,... | collective-permute-start | bytes 3145736 | tf_op jit(solution)/shard_map/ppermute | solution.py:241
  4.9 7.2 %collective-permute-start.9 = (bf16[2,128,512]{2,1,0:T(8,128)(2,1)S(1)}, bf16[2,128,512]{2,1,0:T(8,128)(2,1)}, u32[]{:S(2)}, u32[]{:S(2)}) collective-permute-start(bf16[2,128,512]{2,1,0:T(8,128)(2,1)S(1)} %get-tuple-element.22), channel_id=1, source_target_pairs={{0,1},{1,0},{2,3},{3,2},{4,5},{5,4},{6,7},{7,6},{8,9},{9,8},{10,11... | collective-permute-start | bytes 786440 | tf_op jit(solution)/shard_map/ppermute | solution.py:241
  5.9 55.1 %collective-permute-start.18 = (bf16[512,1024]{1,0:T(8,128)(2,1)}, bf16[512,1024]{1,0:T(8,128)(2,1)S(1)}, u32[]{:S(2)}, u32[]{:S(2)}) collective-permute-start(bf16[512,1024]{1,0:T(8,128)(2,1)} %xpts.1), channel_id=1, source_target_pairs={{0,1},{1,0},{2,3},{3,2},{4,5},{5,4},{6,7},{7,6},{8,9},{9,8},{10,11... | collective-permute-start | bytes 3145736 | tf_op jit(solution)/shard_map/ppermute | solution.py:241
  8.1 1.8 %collective-permute-start = (s32[1,16]{1,0:T(1,128)S(1)}, s32[1,16]{1,0:T(1,128)S(1)}, u32[]{:S(2)}, u32[]{:S(2)}) collective-permute-start(s32[1,16]{1,0:T(1,128)S(1)} %bitcast.16), channel_id=1, source_target_pairs={{0,1},{1,0},{2,3},{3,2},{4,5},{5,4},{6,7},{7,6},{8,9},{9,8},{10,11... | collective-permute-start | bytes 200 | tf_op jit(solution)/shard_map/ppermute | solution.py:241
  8.5 18.7 %collective-permute-start.3 = (bf16[128,1024]{1,0:T(8,128)(2,1)S(1)}, bf16[128,1024]{1,0:T(8,128)(2,1)S(1)}, u32[]{:S(2)}, u32[]{:S(2)}) collective-permute-start(bf16[128,1024]{1,0:T(8,128)(2,1)S(1)} %get-tuple-element.20.refs_0_), channel_id=1, source_target_pairs={{0,8},{1,9},{2,10},{3,11},{4,12},{5,13},{6,14},{7,15},{8,16},{9,17... | collective-permute-start | bytes 786440 | tf_op jit(solution)/shard_map/ppermute | solution.py:241
  9.8 20.7 %collective-permute-start.5 = (bf16[128,1024]{1,0:T(8,128)(2,1)S(1)}, bf16[128,1024]{1,0:T(8,128)(2,1)S(1)}, u32[]{:S(2)}, u32[]{:S(2)}) collective-permute-start(bf16[128,1024]{1,0:T(8,128)(2,1)S(1)} %get-tuple-element.20.refs_0_), channel_id=1, source_target_pairs={{0,16},{1,17},{2,18},{3,19},{4,20},{5,21},{6,22},{7,23},{8,24},{9,... | collective-permute-start | bytes 786440 | tf_op jit(solution)/shard_map/ppermute | solution.py:241
  12.1 14.7 %collective-permute-start.1 = (s32[2,16]{1,0:T(2,128)S(1)}, s32[2,16]{1,0:T(2,128)S(1)}, u32[]{:S(2)}, u32[]{:S(2)}) collective-permute-start(s32[2,16]{1,0:T(2,128)S(1)} %pad_add_fusion.1.meta), channel_id=1, source_target_pairs={{0,2},{1,3},{2,0},{3,1},{4,6},{5,7},{6,4},{7,5},{8,10},{9,11},{10,... | collective-permute-start | bytes 392 | tf_op jit(solution)/shard_map/ppermute | solution.py:241
  24.2 51.1 %copy-start.6 = (bf16[512,1024]{1,0:T(8,128)(2,1)}, bf16[512,1024]{1,0:T(8,128)(2,1)S(1)}, u32[]{:S(2)}) copy-start(bf16[512,1024]{1,0:T(8,128)(2,1)S(1)} %collective-permute-done.19.refs_0_.refs_10_.refs_8_) | copy-start | bytes 3145732
  24.2 50.0 %collective-permute-start.20 = (bf16[512,1024]{1,0:T(8,128)(2,1)S(1)}, bf16[512,1024]{1,0:T(8,128)(2,1)S(1)}, u32[]{:S(2)}, u32[]{:S(2)}) collective-permute-start(bf16[512,1024]{1,0:T(8,128)(2,1)S(1)} %collective-permute-done.19.refs_0_.refs_10_.refs_8_), channel_id=1, source_target_pairs={{0,1},{1,0},{2,3},{3,2},{4,5},{5,4},{6,7},{7,6},{8,9},{9,8},{10,11... | collective-permute-start | bytes 3145736 | tf_op jit(solution)/shard_map/ppermute | solution.py:241
  26.8 37.5 %copy-start.2 = (bf16[512,512]{1,0:T(8,128)(2,1)S(1)}, bf16[512,512]{1,0:T(8,128)(2,1)}, u32[]{:S(2)}) copy-start(bf16[512,512]{1,0:T(8,128)(2,1)} %wts.5) | copy-start | bytes 1572868
  26.9 5.0 %collective-permute-start.10 = (bf16[1,128,512]{2,1,0:T(8,128)(2,1)S(1)}, bf16[1,128,512]{2,1,0:T(8,128)(2,1)S(1)}, u32[]{:S(2)}, u32[]{:S(2)}) collective-permute-start(bf16[1,128,512]{2,1,0:T(8,128)(2,1)S(1)} %fusion.1), channel_id=1, source_target_pairs={{0,2},{1,3},{2,0},{3,1},{4,6},{5,7},{6,4},{7,5},{8,10},{9,11},{10,... | collective-permute-start | bytes 393224 | tf_op jit(solution)/shard_map/ppermute | solution.py:241
  27.2 8.6 %collective-permute-start.7 = (bf16[128,1024]{1,0:T(8,128)(2,1)S(1)}, bf16[128,1024]{1,0:T(8,128)(2,1)S(1)}, u32[]{:S(2)}, u32[]{:S(2)}) collective-permute-start(bf16[128,1024]{1,0:T(8,128)(2,1)S(1)} %get-tuple-element.20.refs_0_), channel_id=1, source_target_pairs={{0,24},{1,25},{2,26},{3,27},{4,28},{5,29},{6,30},{7,31},{8,0},{9,1... | collective-permute-start | bytes 786440 | tf_op jit(solution)/shard_map/ppermute | solution.py:241
  30.5 7.1 %collective-permute-start.2 = (bf16[128,1024]{1,0:T(8,128)(2,1)S(1)}, bf16[128,1024]{1,0:T(8,128)(2,1)S(1)}, u32[]{:S(2)}, u32[]{:S(2)}) collective-permute-start(bf16[128,1024]{1,0:T(8,128)(2,1)S(1)} %get-tuple-element.20.refs_0_), channel_id=1, source_target_pairs={{0,4},{1,5},{2,6},{3,7},{4,0},{5,1},{6,2},{7,3},{8,12},{9,13},{10,... | collective-permute-start | bytes 786440 | tf_op jit(solution)/shard_map/ppermute | solution.py:241
  31.9 75.4 %collective-permute-start.22 = (bf16[512,1024]{1,0:T(8,128)(2,1)}, bf16[512,1024]{1,0:T(8,128)(2,1)S(1)}, u32[]{:S(2)}, u32[]{:S(2)}) collective-permute-start(bf16[512,1024]{1,0:T(8,128)(2,1)} %xpts.1), channel_id=1, source_target_pairs={{2,4},{3,5},{4,2},{5,3},{6,8},{7,9},{8,6},{9,7},{10,12},{11,13},{1... | collective-permute-start | bytes 3145736 | tf_op jit(solution)/shard_map/ppermute | solution.py:241
  35.8 25.3 %collective-permute-start.12 = (bf16[128,512]{1,0:T(8,128)(2,1)S(1)}, bf16[128,512]{1,0:T(8,128)(2,1)S(1)}, u32[]{:S(2)}, u32[]{:S(2)}) collective-permute-start(bf16[128,512]{1,0:T(8,128)(2,1)S(1)} %fusion.2.refs_4_), channel_id=1, source_target_pairs={{0,8},{1,9},{2,10},{3,11},{4,12},{5,13},{6,14},{7,15},{8,16},{9,17... | collective-permute-start | bytes 393224 | tf_op jit(solution)/shard_map/ppermute | solution.py:241
  37.6 44.0 %collective-permute-start.4 = (bf16[128,1024]{1,0:T(8,128)(2,1)S(1)}, bf16[128,1024]{1,0:T(8,128)(2,1)S(1)}, u32[]{:S(2)}, u32[]{:S(2)}) collective-permute-start(bf16[128,1024]{1,0:T(8,128)(2,1)S(1)} %collective-permute-done.3.refs_1_), channel_id=1, source_target_pairs={{0,4},{1,5},{2,6},{3,7},{4,0},{5,1},{6,2},{7,3},{8,12},{9,13},{10,... | collective-permute-start | bytes 786440 | tf_op jit(solution)/shard_map/ppermute | solution.py:241
  61.0 21.1 %collective-permute-start.6 = (bf16[128,1024]{1,0:T(8,128)(2,1)S(1)}, bf16[128,1024]{1,0:T(8,128)(2,1)S(1)}, u32[]{:S(2)}, u32[]{:S(2)}) collective-permute-start(bf16[128,1024]{1,0:T(8,128)(2,1)S(1)} %collective-permute-done.5.refs_2_), channel_id=1, source_target_pairs={{0,4},{1,5},{2,6},{3,7},{4,0},{5,1},{6,2},{7,3},{8,12},{9,13},{10,... | collective-permute-start | bytes 786440 | tf_op jit(solution)/shard_map/ppermute | solution.py:241
  61.0 9.5 %collective-permute-start.14 = (bf16[128,512]{1,0:T(8,128)(2,1)S(1)}, bf16[128,512]{1,0:T(8,128)(2,1)S(1)}, u32[]{:S(2)}, u32[]{:S(2)}) collective-permute-start(bf16[128,512]{1,0:T(8,128)(2,1)S(1)} %fusion.2.refs_4_), channel_id=1, source_target_pairs={{0,16},{1,17},{2,18},{3,19},{4,20},{5,21},{6,22},{7,23},{8,24},{9,... | collective-permute-start | bytes 393224 | tf_op jit(solution)/shard_map/ppermute | solution.py:241
  70.6 9.6 %collective-permute-start.16 = (bf16[128,512]{1,0:T(8,128)(2,1)S(1)}, bf16[128,512]{1,0:T(8,128)(2,1)S(1)}, u32[]{:S(2)}, u32[]{:S(2)}) collective-permute-start(bf16[128,512]{1,0:T(8,128)(2,1)S(1)} %fusion.2.refs_4_), channel_id=1, source_target_pairs={{0,24},{1,25},{2,26},{3,27},{4,28},{5,29},{6,30},{7,31},{8,0},{9,1... | collective-permute-start | bytes 393224 | tf_op jit(solution)/shard_map/ppermute | solution.py:241
  74.3 6.4 %collective-permute-start.11 = (bf16[128,512]{1,0:T(8,128)(2,1)S(1)}, bf16[128,512]{1,0:T(8,128)(2,1)S(1)}, u32[]{:S(2)}, u32[]{:S(2)}) collective-permute-start(bf16[128,512]{1,0:T(8,128)(2,1)S(1)} %fusion.2.refs_4_), channel_id=1, source_target_pairs={{0,4},{1,5},{2,6},{3,7},{4,0},{5,1},{6,2},{7,3},{8,12},{9,13},{10,... | collective-permute-start | bytes 393224 | tf_op jit(solution)/shard_map/ppermute | solution.py:241
  80.2 16.8 %collective-permute-start.8 = (bf16[128,1024]{1,0:T(8,128)(2,1)S(1)}, bf16[128,1024]{1,0:T(8,128)(2,1)S(1)}, u32[]{:S(2)}, u32[]{:S(2)}) collective-permute-start(bf16[128,1024]{1,0:T(8,128)(2,1)S(1)} %collective-permute-done.7.refs_3_), channel_id=1, source_target_pairs={{0,4},{1,5},{2,6},{3,7},{4,0},{5,1},{6,2},{7,3},{8,12},{9,13},{10,... | collective-permute-start | bytes 786440 | tf_op jit(solution)/shard_map/ppermute | solution.py:241
  80.6 18.3 %collective-permute-start.13 = (bf16[128,512]{1,0:T(8,128)(2,1)S(1)}, bf16[128,512]{1,0:T(8,128)(2,1)S(1)}, u32[]{:S(2)}, u32[]{:S(2)}) collective-permute-start(bf16[128,512]{1,0:T(8,128)(2,1)S(1)} %collective-permute-done.12.refs_5_), channel_id=1, source_target_pairs={{0,4},{1,5},{2,6},{3,7},{4,0},{5,1},{6,2},{7,3},{8,12},{9,13},{10,... | collective-permute-start | bytes 393224 | tf_op jit(solution)/shard_map/ppermute | solution.py:241
  81.7 17.3 %collective-permute-start.15 = (bf16[128,512]{1,0:T(8,128)(2,1)S(1)}, bf16[128,512]{1,0:T(8,128)(2,1)S(1)}, u32[]{:S(2)}, u32[]{:S(2)}) collective-permute-start(bf16[128,512]{1,0:T(8,128)(2,1)S(1)} %collective-permute-done.14.refs_6_), channel_id=1, source_target_pairs={{0,4},{1,5},{2,6},{3,7},{4,0},{5,1},{6,2},{7,3},{8,12},{9,13},{10,... | collective-permute-start | bytes 393224 | tf_op jit(solution)/shard_map/ppermute | solution.py:241
  82.1 16.9 %collective-permute-start.17 = (bf16[128,512]{1,0:T(8,128)(2,1)S(1)}, bf16[128,512]{1,0:T(8,128)(2,1)S(1)}, u32[]{:S(2)}, u32[]{:S(2)}) collective-permute-start(bf16[128,512]{1,0:T(8,128)(2,1)S(1)} %collective-permute-done.16.refs_7_), channel_id=1, source_target_pairs={{0,4},{1,5},{2,6},{3,7},{4,0},{5,1},{6,2},{7,3},{8,12},{9,13},{10,... | collective-permute-start | bytes 393224 | tf_op jit(solution)/shard_map/ppermute | solution.py:241
  83.2 15.8 %copy-start.7 = (bf16[512,1024]{1,0:T(8,128)(2,1)S(1)}, bf16[512,1024]{1,0:T(8,128)(2,1)}, u32[]{:S(2)}) copy-start(bf16[512,1024]{1,0:T(8,128)(2,1)} %copy-done.6) | copy-start | bytes 3145732
  83.2 15.8 %copy-start.9 = (bf16[512,1024]{1,0:T(8,128)(2,1)S(1)}, bf16[512,1024]{1,0:T(8,128)(2,1)}, u32[]{:S(2)}) copy-start(bf16[512,1024]{1,0:T(8,128)(2,1)} %copy-done.8) | copy-start | bytes 3145732
  97.0 14.4 %collective-permute-start.23 = (bf16[512,512]{1,0:T(8,128)(2,1)S(1)}, bf16[512,512]{1,0:T(8,128)(2,1)S(1)}, u32[]{:S(2)}, u32[]{:S(2)}) collective-permute-start(bf16[512,512]{1,0:T(8,128)(2,1)S(1)} %copy-done.2), channel_id=1, source_target_pairs={{2,4},{3,5},{4,2},{5,3},{6,8},{7,9},{8,6},{9,7},{10,12},{11,13},{1... | collective-permute-start | bytes 1572872 | tf_op jit(solution)/shard_map/ppermute | solution.py:241
  103.8 16.7 %collective-permute-start.26 = (bf16[512,512]{1,0:T(8,128)(2,1)S(1)}, bf16[512,512]{1,0:T(8,128)(2,1)S(1)}, u32[]{:S(2)}, u32[]{:S(2)}) collective-permute-start(bf16[512,512]{1,0:T(8,128)(2,1)S(1)} %get-tuple-element.34), channel_id=1, source_target_pairs={{0,1},{1,0},{2,3},{3,2},{4,5},{5,4},{6,7},{7,6},{8,9},{9,8},{10,11... | collective-permute-start | bytes 1572872 | tf_op jit(solution)/shard_map/ppermute | solution.py:241
  107.3 13.5 %collective-permute-start.24 = (bf16[512,1024]{1,0:T(8,128)(2,1)S(1)}, bf16[512,1024]{1,0:T(8,128)(2,1)S(1)}, u32[]{:S(2)}, u32[]{:S(2)}) collective-permute-start(bf16[512,1024]{1,0:T(8,128)(2,1)S(1)} %collective-permute-done.22.refs_0_), channel_id=1, source_target_pairs={{1,0},{2,3},{5,4},{6,7},{9,8},{10,11},{13,12},{14,15},{17,16},{18,... | collective-permute-start | bytes 3145736 | tf_op jit(solution)/shard_map/ppermute | solution.py:241
  111.4 9.3 %collective-permute-start.25 = (bf16[512,512]{1,0:T(8,128)(2,1)S(1)}, bf16[512,512]{1,0:T(8,128)(2,1)S(1)}, u32[]{:S(2)}, u32[]{:S(2)}) collective-permute-start(bf16[512,512]{1,0:T(8,128)(2,1)S(1)} %collective-permute-done.23.refs_1_), channel_id=1, source_target_pairs={{1,0},{2,3},{5,4},{6,7},{9,8},{10,11},{13,12},{14,15},{17,16},{18,... | collective-permute-start | bytes 1572872 | tf_op jit(solution)/shard_map/ppermute | solution.py:241
  116.8 5.2 %collective-permute-start.21 = (bf16[512,512]{1,0:T(8,128)(2,1)S(1)}, bf16[512,512]{1,0:T(8,128)(2,1)S(1)}, u32[]{:S(2)}, u32[]{:S(2)}) collective-permute-start(bf16[512,512]{1,0:T(8,128)(2,1)S(1)} %get-tuple-element.30), channel_id=1, source_target_pairs={{0,1},{1,0},{2,3},{3,2},{4,5},{5,4},{6,7},{7,6},{8,9},{9,8},{10,11... | collective-permute-start | bytes 1572872 | tf_op jit(solution)/shard_map/ppermute | solution.py:241
  120.7 13.6 %collective-permute-start.27 = (bf16[512,512]{1,0:T(8,128)(2,1)S(1)}, bf16[512,512]{1,0:T(8,128)(2,1)S(1)}, u32[]{:S(2)}, u32[]{:S(2)}) collective-permute-start(bf16[512,512]{1,0:T(8,128)(2,1)S(1)} %add_convert_fusion), channel_id=1, source_target_pairs={{0,2},{1,3},{2,0},{3,1},{4,6},{5,7},{6,4},{7,5},{8,10},{9,11},{10,... | collective-permute-start | bytes 1572872 | tf_op jit(solution)/shard_map/ppermute | solution.py:241
  (17 other events, 44.3 us)

commit v2 on v0

v2 whole, which is shorter than its diff:
```python
import functools
import math

import jax
import jax.numpy as jnp
from jax import lax
from jax.experimental import pallas as pl
from jax.experimental.pallas import tpu as pltpu
from jax.sharding import PartitionSpec as P

NODES = 8
NEAR = 4
FAR = 4
QUAD = 4
F32 = jnp.float32
BF16 = jnp.bfloat16
MIB = 1 << 20

NEAR_COUNT = NEAR
FAR_LIST = NEAR + 1
FAR_COUNT = FAR_LIST + FAR
LEAF = FAR_COUNT + 1
META = 16


def vmem():
    return pl.BlockSpec(memory_space=pltpu.VMEM)


def smem():
    return pl.BlockSpec(memory_space=pltpu.SMEM)


def params():
    return pltpu.CompilerParams(vmem_limit_bytes=24 * MIB)


def norm_column(points, scale):
    wide = points.astype(F32)
    return jnp.sum(wide * wide, axis=1, keepdims=True) * scale


def norm_row(points, scale):
    column = norm_column(points, scale)
    return jnp.transpose(jnp.broadcast_to(column, (column.shape[0], 128)))[0:1, :]


def listed(meta, row, first, count, value):
    hit = jnp.bool_(False)
    for slot in range(count):
        hit = hit | ((meta[row, first + slot] == value) & (slot < meta[row, first + count]))
    return hit


def near_hit(meta, row, leaf):
    return listed(meta, row, 0, NEAR, leaf)


def far_hit(meta, row, node):
    return listed(meta, row, FAR_LIST, FAR, node)


def half_scale(dim):
    return 0.5 * math.log2(math.e) / dim


def kernel_sum(xpts, xsq, ypts, ysq, wts):
    dim = xpts.shape[1]
    scores = lax.dot_general(
        xpts, ypts, (((1,), (1,)), ((), ())), preferred_element_type=F32
    )
    kern = jnp.exp2(scores * (2.0 * half_scale(dim)) - xsq - ysq)
    return jnp.dot(kern.astype(BF16), wts, preferred_element_type=F32)


def call(body, kinds, scalars, arrays, scratch=()):
    return pl.pallas_call(
        body,
        out_shape=kinds,
        in_specs=[smem()] * len(scalars) + [vmem()] * len(arrays),
        out_specs=jax.tree.map(lambda _: vmem(), kinds),
        scratch_shapes=scratch,
        compiler_params=params(),
        cost_estimate=pl.CostEstimate(flops=1000, bytes_accessed=1000, transcendentals=0),
    )(*scalars, *arrays)


def project_body(wts, proj, keep, give, whole):
    core = lax.axis_index("pts") % 2
    whole[...] = jnp.dot(proj[...], wts[...], preferred_element_type=F32).reshape(whole.shape)
    keep[...] = whole[:, core]
    give[...] = whole[:, 1 - core].astype(BF16)


def project(group, wts, proj):
    count, wcols = proj.shape[0] // group, wts.shape[1]
    half = (group // 2, count, wcols)
    return call(
        project_body,
        (jax.ShapeDtypeStruct(half, F32), jax.ShapeDtypeStruct(half, BF16)),
        (),
        (wts, proj),
        [pltpu.VMEM((group // 2, 2, count, wcols), F32)],
    )


def pack_body(idx, pts, keep, got, packed):
    rows, dim = pts.shape
    place = lax.broadcasted_iota(jnp.int32, (rows, idx.shape[1]), 0)
    pick = (place == idx[...]).astype(F32).astype(BF16)
    packed[:, :dim] = lax.dot_general(
        pick, pts[...], (((0,), (0,)), ((), ())), preferred_element_type=F32
    ).astype(BF16)
    packed[:, dim:] = (keep[0] + got[0].astype(F32)).astype(BF16)


def pack(idx, pts, keep, got):
    shape = (idx.shape[1], pts.shape[1] + keep.shape[2])
    return call(pack_body, jax.ShapeDtypeStruct(shape, BF16), (), (idx, pts, keep, got))


def quad_body(group, places, first, own, meta, *refs):
    packed, refs = refs[: len(places)], refs[len(places) :]
    xpts, refs = refs[:2], refs[2:]
    if own:
        mine, mine_w, *outs = refs
    else:
        start, outs = refs[:2], refs[2:]
    dim = xpts[0].shape[1]
    scale = half_scale(dim)
    quads = lax.axis_size("pts") // QUAD
    leaf = meta[0, LEAF]
    quad = leaf // QUAD
    count = packed[0].shape[0]
    nodes = []
    for turn, flip in places:
        deep = (quad // 2 - turn + quads // 2) % (quads // 2)
        nodes.append((deep * 2 + (quad + flip) % 2) * QUAD // group)
    everything = jnp.concatenate([ref[...] for ref in packed], axis=0)
    ypts, wts = everything[:, :dim], everything[:, dim:]
    ysq = norm_row(ypts, scale)
    if own:
        own_sq = norm_row(mine[...], scale)
    for place in range(2):
        hits = [far_hit(meta, first + place, node) for node in nodes]
        some = functools.reduce(jnp.logical_or, hits)
        away = [jnp.full((1, count), jnp.where(hit, 0.0, 1e30), F32) for hit in hits]
        far_sq = ysq + jnp.concatenate(away, axis=1)
        xsq = norm_column(xpts[place][...], scale)

        def far(place=place, xsq=xsq, far_sq=far_sq):
            return kernel_sum(xpts[place][...], xsq, ypts, far_sq, wts)

        out = outs[place]
        if own:
            def near(place=place, xsq=xsq):
                return kernel_sum(xpts[place][...], xsq, mine[...], own_sq, mine_w[...])

            if first + place == 0:
                out[...] = near()
            else:
                hit = near_hit(meta, first + place, leaf)

                @pl.when(hit)
                def _(out=out, near=near):
                    out[...] = near()

                @pl.when(jnp.logical_not(hit))
                def _(out=out):
                    out[...] = jnp.zeros_like(out)

            @pl.when(some)
            def _(out=out, far=far):
                out[...] += far()
        else:
            @pl.when(some)
            def _(out=out, far=far, place=place):
                out[...] = (start[place][...] + far()).astype(out.dtype)

            @pl.when(jnp.logical_not(some))
            def _(out=out, place=place):
                out[...] = start[place][...].astype(out.dtype)


def quad_terms(group, places, first, meta, packed, xpts, mine, start, kinds):
    rows = xpts[0].shape[0]
    wcols = packed[0].shape[1] - xpts[0].shape[1]
    body = functools.partial(quad_body, group, tuple(places), first, bool(mine))
    shapes = tuple(jax.ShapeDtypeStruct((rows, wcols), kind) for kind in kinds)
    return call(body, shapes, (meta,), (*packed, *xpts, *mine, *start))


def sum_body(one, two, out):
    out[...] = (one[...] + two[...].astype(F32)).astype(BF16)


def sum_terms(one, two):
    return call(sum_body, jax.ShapeDtypeStruct(one.shape, BF16), (), (one, two))


def cross_body(meta, own, other, start, start_other, ypts, wts, acc, *halves):
    leaf = meta[0, LEAF]
    away = leaf + 4 * (leaf // 2 % 2) - 2
    scale = half_scale(own.shape[1])
    ysq = norm_row(ypts[...], scale)

    def term(xpts):
        return kernel_sum(xpts[...], norm_column(xpts[...], scale), ypts[...], ysq, wts[...])

    acc[...] = start[...]
    hit = near_hit(meta, 0, away)

    @pl.when(hit)
    def _():
        acc[...] += term(own)

    def put(value):
        first = 0
        for half in halves:
            half[...] = value[first : first + half.shape[0]].astype(BF16)
            first += half.shape[0]

    hit = near_hit(meta, 1, away)

    @pl.when(hit)
    def _():
        put(start_other[...] + term(other))

    @pl.when(jnp.logical_not(hit))
    def _():
        put(start_other[...])


def cross_terms(meta, xpts, start, ypts, wts):
    rows, wcols = start[0].shape
    half = jax.ShapeDtypeStruct((rows // 2, wcols), BF16)
    shapes = (jax.ShapeDtypeStruct((rows, wcols), F32), half, half)
    return call(cross_body, shapes, (meta,), (*xpts, *start, ypts, wts))


def shards(points, weights, node_proj, skel_idx, near_list, near_count, far_list, far_count):
    leaves = lax.axis_size("pts")
    me = lax.axis_index("pts")
    group = leaves // NODES
    quads = leaves // QUAD
    depth = quads // 2

    def move(value, where):
        pairs = [(source, where(source)) for source in range(leaves)]
        return lax.ppermute(value, "pts", [(a, b) for a, b in pairs if b is not None])

    def bit(level):
        return lambda source: source ^ (1 << level)

    def deeper(turn):
        def where(source):
            quad, place = divmod(source, QUAD)
            deep, side = divmod(quad, 2)
            return ((deep + turn) % depth * 2 + side) * QUAD + place

        return where

    def after(values):
        return lax.optimization_barrier(values)

    def across(source):
        target = source + 2 if source // 2 % 2 else source - 2
        return target if 0 <= target < leaves else None

    def along(source):
        target = source - QUAD if source // 2 % 2 else source + QUAD
        return target if 0 <= target < leaves else None

    core, side, row = bit(0), bit(1), bit(2)

    meta = jnp.concatenate(
        [near_list[0], near_count, far_list[0], far_count, me[None], jnp.zeros((META - LEAF - 1,), jnp.int32)]
    )[None]
    keep, give = project(group, weights, node_proj)
    level = 0
    while True:
        got = move(give, bit(level))
        if level < 2:
            got, lists = after((got, move(meta, bit(level))))
            meta = jnp.concatenate([meta, lists], axis=0)
        level += 1
        if keep.shape[0] == 1:
            break
        count = keep.shape[0]
        keep = (keep + got.astype(F32)).reshape(count // 2, 2, *keep.shape[1:])
        upper = (me >> level) % 2 == 1
        give = jnp.where(upper, keep[:, 0], keep[:, 1]).astype(BF16)
        keep = jnp.where(upper, keep[:, 1], keep[:, 0])
    cross_w = move(weights, across)
    got, meta, cross_w = after((got, meta, cross_w))
    packed = pack(skel_idx, points, keep, got)

    up, down = deeper(1), deeper(depth - 1)
    top = depth // 2
    gathered = {(0, 0): packed}
    packed, pts_later = after((packed, points))
    pts_side = move(pts_later, side)
    pts_core = move(pts_later, core)
    gathered[1, 0] = move(packed, up)
    gathered[0, 1] = move(packed, row)
    gathered, packed = after((gathered, packed))
    if depth > 2:
        gathered[depth - 1, 0] = move(packed, down)
    gathered[1, 1] = move(gathered[1, 0], row)
    gathered, pts_side = after((gathered, pts_side))
    pts_both = move(pts_side, core)
    first_places = sorted(set(gathered) - {(1, 1)})
    if depth > 2:
        gathered[depth - 1, 1] = move(gathered[depth - 1, 0], row)
    for turn in range(2, top + 1):
        gathered[turn, 0] = move(gathered[turn - 1, 0], up)
    for turn in range(depth - 2, top, -1):
        gathered[turn, 0] = move(gathered[turn + 1, 0], down)

    mine = (points, weights)
    near_x = (points, pts_core)
    side_x = (pts_side, pts_both)
    some = [gathered[place] for place in first_places]
    acc0, acc1 = quad_terms(group, first_places, 0, meta, some, near_x, mine, (), (F32, F32))
    acc2, acc3 = quad_terms(group, first_places, 2, meta, some, side_x, mine, (), (F32, F32))
    gathered, acc0, acc1, acc2, acc3, pts_last = after((gathered, acc0, acc1, acc2, acc3, pts_side))

    for turn in range(2, top + 1):
        gathered[turn, 1] = move(gathered[turn - 1, 1], up)
    for turn in range(depth - 2, top, -1):
        gathered[turn, 1] = move(gathered[turn + 1, 1], down)
    cross_p = move(pts_last, along)
    last_places = sorted(set(gathered) - set(first_places))
    rest = [gathered[place] for place in last_places]
    acc2, out3 = quad_terms(
        group, last_places, 2, meta, rest, side_x, (), (acc2, acc3), (F32, BF16)
    )
    got3 = move(out3, core)
    acc0, acc1 = quad_terms(group, last_places, 0, meta, rest, near_x, (), (acc0, acc1), (F32, F32))
    got3, acc0, acc1 = after((got3, acc0, acc1))
    last = move(sum_terms(acc2, got3), side)
    acc0, *out1 = cross_terms(meta, near_x, (acc0, acc1), cross_p, cross_w)
    extra = jnp.concatenate([move(half, core) for half in out1], axis=0)
    return acc0 + extra.astype(F32) + last.astype(F32)


def solution(mesh):
    in_specs = (
        P("pts", None),
        P("pts", None),
        P(None, "pts"),
        P("pts", None),
        P("pts", None),
        P("pts"),
        P("pts", None),
        P("pts"),
    )
    out_specs = P("pts", None)
    return jax.shard_map(shards, mesh=mesh, in_specs=in_specs, out_specs=out_specs, check_vma=False)
```

time: 253 us -> 103 us (0.41); the launches traced: 250 us -> 103 us
  waiting for transfers between devices: 163 us -> 53.1 us
  matrix products: 30.8 us -> 0 us
  Pallas kernels: 0 us -> 19.9 us
  between operations: 17.5 us -> 1.51 us
  local copies, waits for them, and re-layouts: 15.9 us -> 1.78 us
  starting transfers between devices: 12.8 us -> 25.6 us
  other arithmetic: 10.4 us -> 1.33 us
    all_gather x2 -> x0, waiting for transfers between devices: 108 us -> none  [the longest x1 58.3 us: shards(): lax.all_gather(share_w, 'pts', axis=0, tiled=True)]
    dot_general x7 -> x0, matrix products: 30.8 us -> none  [the longest x6 29.3 us: kernel_sum(): return jnp.dot(kern, wts, preferred_element_type=jnp.float32)]
    pallas_call x0 -> x8, Pallas kernels: none -> 19.9 us  [call(): pl.pallas_call(body, out_shape=kinds, in_specs=[smem()] * len(scalars) +...]
    ppermute x6 -> x20, starting transfers between devices: 12.7 us -> 25.6 us  [move(): lax.ppermute(value, 'pts', [(a, b) for a, b in pairs if b is not None])]
    unnamed x20 -> x10, local copies, waits for them, and re-layouts: 9.64 us -> 1.7 us
    reduce_sum x3 -> x0, other arithmetic: 6.26 us -> none  [the longest x2 5.98 us: kernel_sum(): ysq = jnp.sum(jnp.square(ypts.astype(jnp.float32)), axis=1)]
    ppermute x6 -> x20, waiting for transfers between devices: 54.6 us -> 53.1 us  [move(): lax.ppermute(value, 'pts', [(a, b) for a, b in pairs if b is not None])]
  transfers between devices with their start and end apart: 8 -> 20, of which waited for: 6 -> 11; matrix products, arithmetic and copies ran while one was open for 12% -> 0% of each run, Pallas kernels for 0% -> 17%
where the time goes in v2:
time: 103 us
  waiting for transfers between devices  53.1 us (52%)
  starting transfers between devices  25.6 us (25%)
  Pallas kernels  19.9 us (19%)
  local copies, waits for them, and re-layouts  1.78 us (2%)
  between operations  1.51 us (1%)
  other arithmetic  1.33 us (1%)
    ppermute x20, waiting for transfers between devices, move(): lax.ppermute(value, 'pts', [(a, b) for a, b in pairs if b is not None])  53.1 us
    ppermute x20, starting transfers between devices, move(): lax.ppermute(value, 'pts', [(a, b) for a, b in pairs if b is not None])  25.6 us
    pallas_call x8, Pallas kernels, call(): pl.pallas_call(body, out_shape=kinds, in_specs=[smem()] * len(scalars) +...  19.9 us
  transfers between devices with their start and end apart: 20, of which 11 were waited for; matrix products, arithmetic and copies ran while one was open for 0% of the time, Pallas kernels for 17%

profile of v2, /device:TPU:7, one launch (start us, length us, event | category | flops | bytes accessed | tf_op | source)
XLA Modules:
  0.0 103.2 jit_solution(5660012926974808872)
XLA Ops:
  0.0 1.0 %copy-done.1 = bf16[512,512]{1,0:T(8,128)(2,1)S(1)} copy-done((bf16[512,512]{1,0:T(8,128)(2,1)S(1)}, bf16[512,512]{1,0:T(8,128)(2,1)}, u32[]{:S(2)}) %copy-start.1) | copy-done | bytes 524312
  1.0 1.6 %shard_map.82 = (f32[2,128,512]{2,1,0:T(8,128)S(1)}, bf16[2,128,512]{2,1,0:T(8,128)(2,1)S(1)}) custom-call(bf16[512,512]{1,0:T(8,128)(2,1)} %refs_7_.3, bf16[512,512]{1,0:T(8,128)(2,1)S(1)} %copy-done.1), custom_call_target="tpu_custom_call" | custom-call | flops 1000 | bytes 1000 | tf_op jit(solution)/shard_map/pallas_call | solution.py:77
  2.6 0.7 collective-permute-start
  3.4 3.1 %collective-permute-start.4 = (bf16[512,512]{1,0:T(8,128)(2,1)}, bf16[512,512]{1,0:T(8,128)(2,1)S(1)}, u32[]{:S(2)}, u32[]{:S(2)}) collective-permute-start(bf16[512,512]{1,0:T(8,128)(2,1)} %refs_7_.3), channel_id=1, source_target_pairs={{2,4},{3,5},{4,2},{5,3},{6,8},{7,9},{8,6},{9,7},{10,12},{11,13},{1... | collective-permute-start | bytes 1572872 | tf_op jit(solution)/shard_map/ppermute | solution.py:250
  7.8 0.6 copy-done.3
  8.8 0.8 collective-permute-done.1
  10.0 1.3 %collective-permute-start.2 = (bf16[1,128,512]{2,1,0:T(8,128)(2,1)S(1)}, bf16[1,128,512]{2,1,0:T(8,128)(2,1)S(1)}, u32[]{:S(2)}, u32[]{:S(2)}) collective-permute-start(bf16[1,128,512]{2,1,0:T(8,128)(2,1)S(1)} %fusion), channel_id=1, source_target_pairs={{0,2},{1,3},{2,0},{3,1},{4,6},{5,7},{6,4},{7,5},{8,10},{9,11},{10,... | collective-permute-start | bytes 393224 | tf_op jit(solution)/shard_map/ppermute | solution.py:250
  11.4 7.5 %collective-permute-done.3 = s32[2,16]{1,0:T(2,128)S(1)} collective-permute-done((s32[2,16]{1,0:T(2,128)S(1)}, s32[2,16]{1,0:T(2,128)S(1)}, u32[]{:S(2)}, u32[]{:S(2)}) %collective-permute-start.3) | collective-permute-done | bytes 160 | tf_op jit(solution)/shard_map/ppermute | solution.py:250
  18.9 2.8 %collective-permute-done.2.got = bf16[1,128,512]{2,1,0:T(8,128)(2,1)S(1)} collective-permute-done((bf16[1,128,512]{2,1,0:T(8,128)(2,1)S(1)}, bf16[1,128,512]{2,1,0:T(8,128)(2,1)S(1)}, u32[]{:S(2)}, u32[]{:S(2)}) %collective-permute-start.2) | collective-permute-done | bytes 131104 | tf_op jit(solution)/shard_map/ppermute | solution.py:250
  22.2 2.8 %collective-permute-start.7 = (bf16[128,1536]{1,0:T(8,128)(2,1)S(1)}, bf16[128,1536]{1,0:T(8,128)(2,1)S(1)}, u32[]{:S(2)}, u32[]{:S(2)}) collective-permute-start(bf16[128,1536]{1,0:T(8,128)(2,1)S(1)} %shard_map.83.refs_0_), channel_id=1, source_target_pairs={{0,8},{1,9},{2,10},{3,11},{4,12},{5,13},{6,14},{7,15},{8,16},{9,17... | collective-permute-start | bytes 1179656 | tf_op jit(solution)/shard_map/ppermute | solution.py:250
  25.0 1.0 %collective-permute-start.6 = (bf16[128,1536]{1,0:T(8,128)(2,1)S(1)}, bf16[128,1536]{1,0:T(8,128)(2,1)S(1)}, u32[]{:S(2)}, u32[]{:S(2)}) collective-permute-start(bf16[128,1536]{1,0:T(8,128)(2,1)S(1)} %shard_map.83.refs_0_), channel_id=1, source_target_pairs={{0,4},{1,5},{2,6},{3,7},{4,0},{5,1},{6,2},{7,3},{8,12},{9,13},{10,... | collective-permute-start | bytes 1179656 | tf_op jit(solution)/shard_map/ppermute | solution.py:250
  26.0 9.7 %collective-permute-done.7.refs_2_ = bf16[128,1536]{1,0:T(8,128)(2,1)S(1)} collective-permute-done((bf16[128,1536]{1,0:T(8,128)(2,1)S(1)}, bf16[128,1536]{1,0:T(8,128)(2,1)S(1)}, u32[]{:S(2)}, u32[]{:S(2)}) %collective-permute-start.7) | collective-permute-done | bytes 393248 | tf_op jit(solution)/shard_map/ppermute | solution.py:250
  35.8 1.1 %collective-permute-start.9 = (bf16[128,1536]{1,0:T(8,128)(2,1)S(1)}, bf16[128,1536]{1,0:T(8,128)(2,1)S(1)}, u32[]{:S(2)}, u32[]{:S(2)}) collective-permute-start(bf16[128,1536]{1,0:T(8,128)(2,1)S(1)} %shard_map.83.refs_0_), channel_id=1, source_target_pairs={{0,24},{1,25},{2,26},{3,27},{4,28},{5,29},{6,30},{7,31},{8,0},{9,1... | collective-permute-start | bytes 1179656 | tf_op jit(solution)/shard_map/ppermute | solution.py:250
  36.9 1.0 collective-permute-start.8
  37.9 2.2 %collective-permute-start.5 = (bf16[512,1024]{1,0:T(8,128)(2,1)S(1)}, bf16[512,1024]{1,0:T(8,128)(2,1)S(1)}, u32[]{:S(2)}, u32[]{:S(2)}) collective-permute-start(bf16[512,1024]{1,0:T(8,128)(2,1)S(1)} %copy-done), channel_id=1, source_target_pairs={{0,1},{1,0},{2,3},{3,2},{4,5},{5,4},{6,7},{7,6},{8,9},{9,8},{10,11... | collective-permute-start | bytes 3145736 | tf_op jit(solution)/shard_map/ppermute | solution.py:250
  40.1 5.0 %collective-permute-done.9.refs_3_ = bf16[128,1536]{1,0:T(8,128)(2,1)S(1)} collective-permute-done((bf16[128,1536]{1,0:T(8,128)(2,1)S(1)}, bf16[128,1536]{1,0:T(8,128)(2,1)S(1)}, u32[]{:S(2)}, u32[]{:S(2)}) %collective-permute-start.9) | collective-permute-done | bytes 393248 | tf_op jit(solution)/shard_map/ppermute | solution.py:250
  46.1 2.4 %collective-permute-start.13 = (bf16[512,1024]{1,0:T(8,128)(2,1)S(1)}, bf16[512,1024]{1,0:T(8,128)(2,1)S(1)}, u32[]{:S(2)}, u32[]{:S(2)}) collective-permute-start(bf16[512,1024]{1,0:T(8,128)(2,1)S(1)} %collective-permute-done.10.refs_4_), channel_id=1, source_target_pairs={{0,1},{1,0},{2,3},{3,2},{4,5},{5,4},{6,7},{7,6},{8,9},{9,8},{10,11... | collective-permute-start | bytes 3145736 | tf_op jit(solution)/shard_map/ppermute | solution.py:250
  48.5 0.6 collective-permute-start.11
  49.1 2.4 %collective-permute-start.12 = (bf16[128,1536]{1,0:T(8,128)(2,1)S(1)}, bf16[128,1536]{1,0:T(8,128)(2,1)S(1)}, u32[]{:S(2)}, u32[]{:S(2)}) collective-permute-start(bf16[128,1536]{1,0:T(8,128)(2,1)S(1)} %collective-permute-done.9.refs_3_), channel_id=1, source_target_pairs={{0,4},{1,5},{2,6},{3,7},{4,0},{5,1},{6,2},{7,3},{8,12},{9,13},{10,... | collective-permute-start | bytes 1179656 | tf_op jit(solution)/shard_map/ppermute | solution.py:250
  51.6 4.7 %shard_map.84 = (f32[512,512]{1,0:T(8,128)S(1)}, f32[512,512]{1,0:T(8,128)S(1)}) custom-call(s32[4,16]{1,0:T(4,128)S(1)} %pad_add_fusion.meta, bf16[128,1536]{1,0:T(8,128)(2,1)S(1)} %shard_map.83.refs_0_, bf16[128,1536]{1,0:T(8,128)(2,1)S(1)} %collective-permute-done.6.refs_1_, bf16[128,1536]{1,0:T(8,128)(2,1)S(1)} %collective-permute-done.7.refs_2_, ...), custom_call_target="tpu_custom_call" | custom-call | flops 1000 | bytes 1000 | tf_op jit(solution)/shard_map/pallas_call | solution.py:77
  56.3 5.3 %shard_map.85 = (f32[512,512]{1,0:T(8,128)S(1)}, f32[512,512]{1,0:T(8,128)S(1)}) custom-call(s32[4,16]{1,0:T(4,128)S(1)} %pad_add_fusion.meta, bf16[128,1536]{1,0:T(8,128)(2,1)S(1)} %shard_map.83.refs_0_, bf16[128,1536]{1,0:T(8,128)(2,1)S(1)} %collective-permute-done.6.refs_1_, bf16[128,1536]{1,0:T(8,128)(2,1)S(1)} %collective-permute-done.7.refs_2_, ...), custom_call_target="tpu_custom_call" | custom-call | flops 1000 | bytes 1000 | tf_op jit(solution)/shard_map/pallas_call | solution.py:77
  61.6 0.6 collective-permute-start.14
  62.1 3.0 %collective-permute-start.16 = (bf16[512,1024]{1,0:T(8,128)(2,1)S(1)}, bf16[512,1024]{1,0:T(8,128)(2,1)S(1)}, u32[]{:S(2)}, u32[]{:S(2)}) collective-permute-start(bf16[512,1024]{1,0:T(8,128)(2,1)S(1)} %collective-permute-done.10.refs_4_), channel_id=1, source_target_pairs={{0,4},{1,5},{4,8},{5,9},{6,2},{7,3},{8,12},{9,13},{10,6},{11,7},{1... | collective-permute-start | bytes 3145736 | tf_op jit(solution)/shard_map/ppermute | solution.py:250
  65.2 8.3 %collective-permute-done.14.refs_2_ = bf16[128,1536]{1,0:T(8,128)(2,1)S(1)} collective-permute-done((bf16[128,1536]{1,0:T(8,128)(2,1)S(1)}, bf16[128,1536]{1,0:T(8,128)(2,1)S(1)}, u32[]{:S(2)}, u32[]{:S(2)}) %collective-permute-start.14) | collective-permute-done | bytes 393248 | tf_op jit(solution)/shard_map/ppermute | solution.py:250
  73.5 2.5 %shard_map.86 = (f32[512,512]{1,0:T(8,128)S(1)}, bf16[512,512]{1,0:T(8,128)(2,1)S(1)}) custom-call(s32[4,16]{1,0:T(4,128)S(1)} %pad_add_fusion.meta, bf16[128,1536]{1,0:T(8,128)(2,1)S(1)} %collective-permute-done.8.refs_0_, bf16[128,1536]{1,0:T(8,128)(2,1)S(1)} %collective-permute-done.11.refs_1_, bf16[128,1536]{1,0:T(8,128)(2,1)S(1)} %collective-permute-done.14.refs_2_, ...), custom_call_target="tpu_custom_call" | custom-call | flops 1000 | bytes 1000 | tf_op jit(solution)/shard_map/pallas_call | solution.py:77
  76.1 1.5 %collective-permute-start.15 = (bf16[512,512]{1,0:T(8,128)(2,1)S(1)}, bf16[512,512]{1,0:T(8,128)(2,1)S(1)}, u32[]{:S(2)}, u32[]{:S(2)}) collective-permute-start(bf16[512,512]{1,0:T(8,128)(2,1)S(1)} %get-tuple-element.77), channel_id=1, source_target_pairs={{0,1},{1,0},{2,3},{3,2},{4,5},{5,4},{6,7},{7,6},{8,9},{9,8},{10,11... | collective-permute-start | bytes 1572872 | tf_op jit(solution)/shard_map/ppermute | solution.py:250
  77.6 3.4 %shard_map.87 = (f32[512,512]{1,0:T(8,128)S(1)}, f32[512,512]{1,0:T(8,128)S(1)}) custom-call(s32[4,16]{1,0:T(4,128)S(1)} %pad_add_fusion.meta, bf16[128,1536]{1,0:T(8,128)(2,1)S(1)} %collective-permute-done.8.refs_0_, bf16[128,1536]{1,0:T(8,128)(2,1)S(1)} %collective-permute-done.11.refs_1_, bf16[128,1536]{1,0:T(8,128)(2,1)S(1)} %collective-permute-done.14.refs_2_, ...), custom_call_target="tpu_custom_call" | custom-call | flops 1000 | bytes 1000 | tf_op jit(solution)/shard_map/pallas_call | solution.py:77
  81.4 16.4 %collective-permute-done.16.ypts = bf16[512,1024]{1,0:T(8,128)(2,1)S(1)} collective-permute-done((bf16[512,1024]{1,0:T(8,128)(2,1)S(1)}, bf16[512,1024]{1,0:T(8,128)(2,1)S(1)}, u32[]{:S(2)}, u32[]{:S(2)}) %collective-permute-start.16) | collective-permute-done | bytes 1048608 | tf_op jit(solution)/shard_map/ppermute | solution.py:250
  97.8 2.0 %shard_map.88 = (f32[512,512]{1,0:T(8,128)S(1)}, bf16[256,512]{1,0:T(8,128)(2,1)S(1)}, bf16[256,512]{1,0:T(8,128)(2,1)S(1)}) custom-call(s32[4,16]{1,0:T(4,128)S(1)} %pad_add_fusion.meta, bf16[512,1024]{1,0:T(8,128)(2,1)S(1)} %copy-done, bf16[512,1024]{1,0:T(8,128)(2,1)S(1)} %collective-permute-done.5.refs_5_.other, f32[512,512]{1,0:T(8,128)S(1)} %get-tuple-element.82.start, ...), custom_call_target="tpu_custom_call" | custom-call | flops 1000 | bytes 1000 | tf_op jit(solution)/shard_map/pallas_call | solution.py:77
  99.9 0.6 collective-permute-start.17
  100.5 1.1 %collective-permute-done.17 = bf16[256,512]{1,0:T(8,128)(2,1)S(1)} collective-permute-done((bf16[256,512]{1,0:T(8,128)(2,1)S(1)}, bf16[256,512]{1,0:T(8,128)(2,1)S(1)}, u32[]{:S(2)}, u32[]{:S(2)}) %collective-permute-start.17) | collective-permute-done | bytes 262176 | tf_op jit(solution)/shard_map/ppermute | solution.py:250
  102.0 1.2 %convert_add_fusion = f32[512,512]{1,0:T(8,128)} fusion(bf16[512,512]{1,0:T(8,128)(2,1)S(1)} %collective-permute-done.19, f32[512,512]{1,0:T(8,128)S(1)} %get-tuple-element.86, bf16[256,512]{1,0:T(8,128)(2,1)S(1)} %collective-permute-done.18, bf16[256,512]{1,0:T(8,128)(2,1)S(1)} %collective-permute-done.17), kind=kLoop, calls=%fused_computation | loop fusion | flops 1835008 | bytes 3145728 | tf_op jit(solution)/shard_map/add | solution.py:344
  (34 shorter events, 3.2 us)
Async XLA Ops:
  0.0 1.0 %copy-start.1 = (bf16[512,512]{1,0:T(8,128)(2,1)S(1)}, bf16[512,512]{1,0:T(8,128)(2,1)}, u32[]{:S(2)}) copy-start(bf16[512,512]{1,0:T(8,128)(2,1)} %proj.1) | copy-start | bytes 1572868
  2.6 7.0 %collective-permute-start = (bf16[2,128,512]{2,1,0:T(8,128)(2,1)S(1)}, bf16[2,128,512]{2,1,0:T(8,128)(2,1)S(1)}, u32[]{:S(2)}, u32[]{:S(2)}) collective-permute-start(bf16[2,128,512]{2,1,0:T(8,128)(2,1)S(1)} %get-tuple-element.49), channel_id=1, source_target_pairs={{0,1},{1,0},{2,3},{3,2},{4,5},{5,4},{6,7},{7,6},{8,9},{9,8},{10,11... | collective-permute-start | bytes 786440 | tf_op jit(solution)/shard_map/ppermute | solution.py:250
  3.4 18.4 %collective-permute-start.4 = (bf16[512,512]{1,0:T(8,128)(2,1)}, bf16[512,512]{1,0:T(8,128)(2,1)S(1)}, u32[]{:S(2)}, u32[]{:S(2)}) collective-permute-start(bf16[512,512]{1,0:T(8,128)(2,1)} %refs_7_.3), channel_id=1, source_target_pairs={{2,4},{3,5},{4,2},{5,3},{6,8},{7,9},{8,6},{9,7},{10,12},{11,13},{1... | collective-permute-start | bytes 1572872 | tf_op jit(solution)/shard_map/ppermute | solution.py:250
  7.8 0.7 copy-start.3
  7.8 0.7 copy-start.4
  8.5 1.1 %collective-permute-start.1 = (s32[1,16]{1,0:T(1,128)S(1)}, s32[1,16]{1,0:T(1,128)S(1)}, u32[]{:S(2)}, u32[]{:S(2)}) collective-permute-start(s32[1,16]{1,0:T(1,128)S(1)} %bitcast.10), channel_id=1, source_target_pairs={{0,1},{1,0},{2,3},{3,2},{4,5},{5,4},{6,7},{7,6},{8,9},{9,8},{10,11... | collective-permute-start | bytes 200 | tf_op jit(solution)/shard_map/ppermute | solution.py:250
  9.7 9.3 %collective-permute-start.3 = (s32[2,16]{1,0:T(2,128)S(1)}, s32[2,16]{1,0:T(2,128)S(1)}, u32[]{:S(2)}, u32[]{:S(2)}) collective-permute-start(s32[2,16]{1,0:T(2,128)S(1)} %pad_add_fusion.1), channel_id=1, source_target_pairs={{0,2},{1,3},{2,0},{3,1},{4,6},{5,7},{6,4},{7,5},{8,10},{9,11},{10,... | collective-permute-start | bytes 392 | tf_op jit(solution)/shard_map/ppermute | solution.py:250
  9.9 11.8 %copy-start = (bf16[512,1024]{1,0:T(8,128)(2,1)S(1)}, bf16[512,1024]{1,0:T(8,128)(2,1)}, u32[]{:S(2)}) copy-start(bf16[512,1024]{1,0:T(8,128)(2,1)} %own.1) | copy-start | bytes 3145732
  10.0 11.7 %collective-permute-start.2 = (bf16[1,128,512]{2,1,0:T(8,128)(2,1)S(1)}, bf16[1,128,512]{2,1,0:T(8,128)(2,1)S(1)}, u32[]{:S(2)}, u32[]{:S(2)}) collective-permute-start(bf16[1,128,512]{2,1,0:T(8,128)(2,1)S(1)} %fusion), channel_id=1, source_target_pairs={{0,2},{1,3},{2,0},{3,1},{4,6},{5,7},{6,4},{7,5},{8,10},{9,11},{10,... | collective-permute-start | bytes 393224 | tf_op jit(solution)/shard_map/ppermute | solution.py:250
  11.4 10.4 %copy-start.2 = (s32[1,128]{1,0:T(1,128)S(1)}, s32[1,128]{1,0:T(1,128)}, u32[]{:S(2)}) copy-start(s32[1,128]{1,0:T(1,128)} %idx.1) | copy-start | bytes 1540
  22.1 23.9 %collective-permute-start.10 = (bf16[512,1024]{1,0:T(8,128)(2,1)S(1)}, bf16[512,1024]{1,0:T(8,128)(2,1)S(1)}, u32[]{:S(2)}, u32[]{:S(2)}) collective-permute-start(bf16[512,1024]{1,0:T(8,128)(2,1)S(1)} %copy-done), channel_id=1, source_target_pairs={{0,2},{1,3},{2,0},{3,1},{4,6},{5,7},{6,4},{7,5},{8,10},{9,11},{10,... | collective-permute-start | bytes 3145736 | tf_op jit(solution)/shard_map/ppermute | solution.py:250
  22.2 13.6 %collective-permute-start.7 = (bf16[128,1536]{1,0:T(8,128)(2,1)S(1)}, bf16[128,1536]{1,0:T(8,128)(2,1)S(1)}, u32[]{:S(2)}, u32[]{:S(2)}) collective-permute-start(bf16[128,1536]{1,0:T(8,128)(2,1)S(1)} %shard_map.83.refs_0_), channel_id=1, source_target_pairs={{0,8},{1,9},{2,10},{3,11},{4,12},{5,13},{6,14},{7,15},{8,16},{9,17... | collective-permute-start | bytes 1179656 | tf_op jit(solution)/shard_map/ppermute | solution.py:250
  25.0 10.8 %collective-permute-start.6 = (bf16[128,1536]{1,0:T(8,128)(2,1)S(1)}, bf16[128,1536]{1,0:T(8,128)(2,1)S(1)}, u32[]{:S(2)}, u32[]{:S(2)}) collective-permute-start(bf16[128,1536]{1,0:T(8,128)(2,1)S(1)} %shard_map.83.refs_0_), channel_id=1, source_target_pairs={{0,4},{1,5},{2,6},{3,7},{4,0},{5,1},{6,2},{7,3},{8,12},{9,13},{10,... | collective-permute-start | bytes 1179656 | tf_op jit(solution)/shard_map/ppermute | solution.py:250
  35.8 9.3 %collective-permute-start.9 = (bf16[128,1536]{1,0:T(8,128)(2,1)S(1)}, bf16[128,1536]{1,0:T(8,128)(2,1)S(1)}, u32[]{:S(2)}, u32[]{:S(2)}) collective-permute-start(bf16[128,1536]{1,0:T(8,128)(2,1)S(1)} %shard_map.83.refs_0_), channel_id=1, source_target_pairs={{0,24},{1,25},{2,26},{3,27},{4,28},{5,29},{6,30},{7,31},{8,0},{9,1... | collective-permute-start | bytes 1179656 | tf_op jit(solution)/shard_map/ppermute | solution.py:250
  36.9 8.7 %collective-permute-start.8 = (bf16[128,1536]{1,0:T(8,128)(2,1)S(1)}, bf16[128,1536]{1,0:T(8,128)(2,1)S(1)}, u32[]{:S(2)}, u32[]{:S(2)}) collective-permute-start(bf16[128,1536]{1,0:T(8,128)(2,1)S(1)} %collective-permute-done.7.refs_2_), channel_id=1, source_target_pairs={{0,4},{1,5},{2,6},{3,7},{4,0},{5,1},{6,2},{7,3},{8,12},{9,13},{10,... | collective-permute-start | bytes 1179656 | tf_op jit(solution)/shard_map/ppermute | solution.py:250
  37.9 13.6 %collective-permute-start.5 = (bf16[512,1024]{1,0:T(8,128)(2,1)S(1)}, bf16[512,1024]{1,0:T(8,128)(2,1)S(1)}, u32[]{:S(2)}, u32[]{:S(2)}) collective-permute-start(bf16[512,1024]{1,0:T(8,128)(2,1)S(1)} %copy-done), channel_id=1, source_target_pairs={{0,1},{1,0},{2,3},{3,2},{4,5},{5,4},{6,7},{7,6},{8,9},{9,8},{10,11... | collective-permute-start | bytes 3145736 | tf_op jit(solution)/shard_map/ppermute | solution.py:250
  46.1 10.2 %collective-permute-start.13 = (bf16[512,1024]{1,0:T(8,128)(2,1)S(1)}, bf16[512,1024]{1,0:T(8,128)(2,1)S(1)}, u32[]{:S(2)}, u32[]{:S(2)}) collective-permute-start(bf16[512,1024]{1,0:T(8,128)(2,1)S(1)} %collective-permute-done.10.refs_4_), channel_id=1, source_target_pairs={{0,1},{1,0},{2,3},{3,2},{4,5},{5,4},{6,7},{7,6},{8,9},{9,8},{10,11... | collective-permute-start | bytes 3145736 | tf_op jit(solution)/shard_map/ppermute | solution.py:250
  48.5 13.1 %collective-permute-start.11 = (bf16[128,1536]{1,0:T(8,128)(2,1)S(1)}, bf16[128,1536]{1,0:T(8,128)(2,1)S(1)}, u32[]{:S(2)}, u32[]{:S(2)}) collective-permute-start(bf16[128,1536]{1,0:T(8,128)(2,1)S(1)} %collective-permute-done.7.refs_2_), channel_id=1, source_target_pairs={{0,8},{1,9},{2,10},{3,11},{4,12},{5,13},{6,14},{7,15},{8,16},{9,17... | collective-permute-start | bytes 1179656 | tf_op jit(solution)/shard_map/ppermute | solution.py:250
  49.1 12.5 %collective-permute-start.12 = (bf16[128,1536]{1,0:T(8,128)(2,1)S(1)}, bf16[128,1536]{1,0:T(8,128)(2,1)S(1)}, u32[]{:S(2)}, u32[]{:S(2)}) collective-permute-start(bf16[128,1536]{1,0:T(8,128)(2,1)S(1)} %collective-permute-done.9.refs_3_), channel_id=1, source_target_pairs={{0,4},{1,5},{2,6},{3,7},{4,0},{5,1},{6,2},{7,3},{8,12},{9,13},{10,... | collective-permute-start | bytes 1179656 | tf_op jit(solution)/shard_map/ppermute | solution.py:250
  61.6 12.0 %collective-permute-start.14 = (bf16[128,1536]{1,0:T(8,128)(2,1)S(1)}, bf16[128,1536]{1,0:T(8,128)(2,1)S(1)}, u32[]{:S(2)}, u32[]{:S(2)}) collective-permute-start(bf16[128,1536]{1,0:T(8,128)(2,1)S(1)} %collective-permute-done.8.refs_0_), channel_id=1, source_target_pairs={{0,8},{1,9},{2,10},{3,11},{4,12},{5,13},{6,14},{7,15},{8,16},{9,17... | collective-permute-start | bytes 1179656 | tf_op jit(solution)/shard_map/ppermute | solution.py:250
  62.1 35.7 %collective-permute-start.16 = (bf16[512,1024]{1,0:T(8,128)(2,1)S(1)}, bf16[512,1024]{1,0:T(8,128)(2,1)S(1)}, u32[]{:S(2)}, u32[]{:S(2)}) collective-permute-start(bf16[512,1024]{1,0:T(8,128)(2,1)S(1)} %collective-permute-done.10.refs_4_), channel_id=1, source_target_pairs={{0,4},{1,5},{4,8},{5,9},{6,2},{7,3},{8,12},{9,13},{10,6},{11,7},{1... | collective-permute-start | bytes 3145736 | tf_op jit(solution)/shard_map/ppermute | solution.py:250
  76.1 4.9 %collective-permute-start.15 = (bf16[512,512]{1,0:T(8,128)(2,1)S(1)}, bf16[512,512]{1,0:T(8,128)(2,1)S(1)}, u32[]{:S(2)}, u32[]{:S(2)}) collective-permute-start(bf16[512,512]{1,0:T(8,128)(2,1)S(1)} %get-tuple-element.77), channel_id=1, source_target_pairs={{0,1},{1,0},{2,3},{3,2},{4,5},{5,4},{6,7},{7,6},{8,9},{9,8},{10,11... | collective-permute-start | bytes 1572872 | tf_op jit(solution)/shard_map/ppermute | solution.py:250
  81.1 20.9 %collective-permute-start.19 = (bf16[512,512]{1,0:T(8,128)(2,1)S(1)}, bf16[512,512]{1,0:T(8,128)(2,1)S(1)}, u32[]{:S(2)}, u32[]{:S(2)}) collective-permute-start(bf16[512,512]{1,0:T(8,128)(2,1)S(1)} %shard_map.89), channel_id=1, source_target_pairs={{0,2},{1,3},{2,0},{3,1},{4,6},{5,7},{6,4},{7,5},{8,10},{9,11},{10,... | collective-permute-start | bytes 1572872 | tf_op jit(solution)/shard_map/ppermute | solution.py:250
  99.9 1.7 %collective-permute-start.17 = (bf16[256,512]{1,0:T(8,128)(2,1)S(1)}, bf16[256,512]{1,0:T(8,128)(2,1)S(1)}, u32[]{:S(2)}, u32[]{:S(2)}) collective-permute-start(bf16[256,512]{1,0:T(8,128)(2,1)S(1)} %get-tuple-element.87), channel_id=1, source_target_pairs={{0,1},{1,0},{2,3},{3,2},{4,5},{5,4},{6,7},{7,6},{8,9},{9,8},{10,11... | collective-permute-start | bytes 786440 | tf_op jit(solution)/shard_map/ppermute | solution.py:250
  100.4 1.5 %collective-permute-start.18 = (bf16[256,512]{1,0:T(8,128)(2,1)S(1)}, bf16[256,512]{1,0:T(8,128)(2,1)S(1)}, u32[]{:S(2)}, u32[]{:S(2)}) collective-permute-start(bf16[256,512]{1,0:T(8,128)(2,1)S(1)} %get-tuple-element.88), channel_id=1, source_target_pairs={{0,1},{1,0},{2,3},{3,2},{4,5},{5,4},{6,7},{7,6},{8,9},{9,8},{10,11... | collective-permute-start | bytes 786440 | tf_op jit(solution)/shard_map/ppermute | solution.py:250

commit v3 on v2

--- a/solution.py
+++ b/solution.py
@@ -20,7 +20,8 @@
 FAR_LIST = NEAR + 1
 FAR_COUNT = FAR_LIST + FAR
 LEAF = FAR_COUNT + 1
-META = 16
+META = 128
+PIECES = 4
 
 
 def vmem():
@@ -85,23 +86,37 @@
     )(*scalars, *arrays)
 
 
-def project_body(wts, proj, keep, give, whole):
-    core = lax.axis_index("pts") % 2
-    whole[...] = jnp.dot(proj[...], wts[...], preferred_element_type=F32).reshape(whole.shape)
-    keep[...] = whole[:, core]
-    give[...] = whole[:, 1 - core].astype(BF16)
-
-
-def project(group, wts, proj):
+def project_body(near_list, near_count, far_list, far_count, wts, proj, keep, meta, *pieces):
+    leaf = lax.axis_index("pts")
+    core = leaf % 2
+    fields = [near_list[0, slot] for slot in range(NEAR)] + [near_count[0]]
+    fields += [far_list[0, slot] for slot in range(FAR)] + [far_count[0], leaf]
+    lane = lax.broadcasted_iota(jnp.int32, meta.shape, 1)
+    row = jnp.zeros(meta.shape, jnp.int32)
+    for place, field in enumerate(fields):
+        row = jnp.where(lane == place, field, row)
+    meta[...] = row
+    whole = jnp.dot(proj[...], wts[...], preferred_element_type=F32)
+    pairs, count, wcols = keep.shape
+    whole = whole.reshape(pairs, 2, count, wcols)
+    other = jnp.where(core == 0, whole[:, 1], whole[:, 0])
+    keep[...] = jnp.where(core == 0, whole[:, 0], whole[:, 1])
+    other = other.reshape(pairs * count, wcols).astype(BF16)
+    first = 0
+    for piece in pieces:
+        piece[...] = other[first : first + piece.shape[0]]
+        first += piece.shape[0]
+
+
+def project(group, lists, wts, proj):
     count, wcols = proj.shape[0] // group, wts.shape[1]
-    half = (group // 2, count, wcols)
-    return call(
-        project_body,
-        (jax.ShapeDtypeStruct(half, F32), jax.ShapeDtypeStruct(half, BF16)),
-        (),
-        (wts, proj),
-        [pltpu.VMEM((group // 2, 2, count, wcols), F32)],
-    )
+    pairs = group // 2
+    piece = jax.ShapeDtypeStruct((pairs * count // PIECES, wcols), BF16)
+    kinds = (
+        jax.ShapeDtypeStruct((pairs, count, wcols), F32),
+        jax.ShapeDtypeStruct((1, META), jnp.int32),
+    ) + (piece,) * PIECES
+    return call(project_body, kinds, lists, (wts, proj))
 
 
 def pack_body(idx, pts, keep, got, packed):
@@ -119,13 +134,14 @@
     return call(pack_body, jax.ShapeDtypeStruct(shape, BF16), (), (idx, pts, keep, got))
 
 
-def quad_body(group, places, first, own, meta, *refs):
+def quad_body(group, places, targets, own, meta, *refs):
     packed, refs = refs[: len(places)], refs[len(places) :]
-    xpts, refs = refs[:2], refs[2:]
+    many = len(targets)
+    xpts, refs = refs[:many], refs[many:]
     if own:
         mine, mine_w, *outs = refs
     else:
-        start, outs = refs[:2], refs[2:]
+        start, outs = refs[:many], refs[many:]
     dim = xpts[0].shape[1]
     scale = half_scale(dim)
     quads = lax.axis_size("pts") // QUAD
@@ -141,8 +157,8 @@
     ysq = norm_row(ypts, scale)
     if own:
         own_sq = norm_row(mine[...], scale)
-    for place in range(2):
-        hits = [far_hit(meta, first + place, node) for node in nodes]
+    for place, target in enumerate(targets):
+        hits = [far_hit(meta, target, node) for node in nodes]
         some = functools.reduce(jnp.logical_or, hits)
         away = [jnp.full((1, count), jnp.where(hit, 0.0, 1e30), F32) for hit in hits]
         far_sq = ysq + jnp.concatenate(away, axis=1)
@@ -156,10 +172,10 @@
             def near(place=place, xsq=xsq):
                 return kernel_sum(xpts[place][...], xsq, mine[...], own_sq, mine_w[...])
 
-            if first + place == 0:
+            if target == 0:
                 out[...] = near()
             else:
-                hit = near_hit(meta, first + place, leaf)
+                hit = near_hit(meta, target, leaf)
 
                 @pl.when(hit)
                 def _(out=out, near=near):
@@ -182,10 +198,10 @@
                 out[...] = start[place][...].astype(out.dtype)
 
 
-def quad_terms(group, places, first, meta, packed, xpts, mine, start, kinds):
+def quad_terms(group, places, targets, meta, packed, xpts, mine, start, kinds):
     rows = xpts[0].shape[0]
     wcols = packed[0].shape[1] - xpts[0].shape[1]
-    body = functools.partial(quad_body, group, tuple(places), first, bool(mine))
+    body = functools.partial(quad_body, group, tuple(places), targets, bool(mine))
     shapes = tuple(jax.ShapeDtypeStruct((rows, wcols), kind) for kind in kinds)
     return call(body, shapes, (meta,), (*packed, *xpts, *mine, *start))
 
@@ -263,26 +279,21 @@
     def after(values):
         return lax.optimization_barrier(values)
 
-    def across(source):
-        target = source + 2 if source // 2 % 2 else source - 2
-        return target if 0 <= target < leaves else None
-
-    def along(source):
-        target = source - QUAD if source // 2 % 2 else source + QUAD
-        return target if 0 <= target < leaves else None
+    def along(way):
+        def where(source):
+            target = source - way * QUAD if source // 2 % 2 else source + way * QUAD
+            return target if 0 <= target < leaves else None
+
+        return where
 
     core, side, row = bit(0), bit(1), bit(2)
 
-    meta = jnp.concatenate(
-        [near_list[0], near_count, far_list[0], far_count, me[None], jnp.zeros((META - LEAF - 1,), jnp.int32)]
-    )[None]
-    keep, give = project(group, weights, node_proj)
+    lists = (near_list, near_count, far_list, far_count)
+    keep, meta, *give = project(group, lists, weights, node_proj)
     level = 0
     while True:
-        got = move(give, bit(level))
-        if level < 2:
-            got, lists = after((got, move(meta, bit(level))))
-            meta = jnp.concatenate([meta, lists], axis=0)
+        got = [move(piece, bit(level)) for piece in give]
+        got = jnp.concatenate(got, axis=0).reshape(keep.shape)
         level += 1
         if keep.shape[0] == 1:
             break
@@ -290,55 +301,56 @@
         keep = (keep + got.astype(F32)).reshape(count // 2, 2, *keep.shape[1:])
         upper = (me >> level) % 2 == 1
         give = jnp.where(upper, keep[:, 0], keep[:, 1]).astype(BF16)
+        give = [give.reshape(-1, give.shape[-1])]
         keep = jnp.where(upper, keep[:, 1], keep[:, 0])
-    cross_w = move(weights, across)
-    got, meta, cross_w = after((got, meta, cross_w))
+    cross_w = move(weights, along(-1))
+    cross_w = [move(half, core) for half in jnp.split(cross_w, 2)]
+    got, pts_later = after((got, points))
     packed = pack(skel_idx, points, keep, got)
 
     up, down = deeper(1), deeper(depth - 1)
     top = depth // 2
     gathered = {(0, 0): packed}
-    packed, pts_later = after((packed, points))
     pts_side = move(pts_later, side)
     pts_core = move(pts_later, core)
     gathered[1, 0] = move(packed, up)
     gathered[0, 1] = move(packed, row)
-    gathered, packed = after((gathered, packed))
+    gathered, packed, cross_w = after((gathered, packed, cross_w))
     if depth > 2:
         gathered[depth - 1, 0] = move(packed, down)
     gathered[1, 1] = move(gathered[1, 0], row)
-    gathered, pts_side = after((gathered, pts_side))
+    for hop in (core, side):
+        meta = jnp.concatenate([meta, move(meta, hop)], axis=0)
+    gathered, pts_side, meta = after((gathered, pts_side, meta))
+    cross_w = move(move(jnp.concatenate(cross_w, axis=0), side), core)
+    cross_p = move(pts_side, along(1))
     pts_both = move(pts_side, core)
     first_places = sorted(set(gathered) - {(1, 1)})
     if depth > 2:
         gathered[depth - 1, 1] = move(gathered[depth - 1, 0], row)
-    for turn in range(2, top + 1):
-        gathered[turn, 0] = move(gathered[turn - 1, 0], up)
-    for turn in range(depth - 2, top, -1):
-        gathered[turn, 0] = move(gathered[turn + 1, 0], down)
+    for flip in range(2):
+        for turn in range(2, top + 1):
+            gathered[turn, flip] = move(gathered[turn - 1, flip], up)
+        for turn in range(depth - 2, top, -1):
+            gathered[turn, flip] = move(gathered[turn + 1, flip], down)
 
     mine = (points, weights)
     near_x = (points, pts_core)
     side_x = (pts_side, pts_both)
     some = [gathered[place] for place in first_places]
-    acc0, acc1 = quad_terms(group, first_places, 0, meta, some, near_x, mine, (), (F32, F32))
-    acc2, acc3 = quad_terms(group, first_places, 2, meta, some, side_x, mine, (), (F32, F32))
-    gathered, acc0, acc1, acc2, acc3, pts_last = after((gathered, acc0, acc1, acc2, acc3, pts_side))
-
-    for turn in range(2, top + 1):
-        gathered[turn, 1] = move(gathered[turn - 1, 1], up)
-    for turn in range(depth - 2, top, -1):
-        gathered[turn, 1] = move(gathered[turn + 1, 1], down)
-    cross_p = move(pts_last, along)
+    acc0, acc1 = quad_terms(group, first_places, (0, 1), meta, some, near_x, mine, (), (F32, F32))
+    acc2, acc3 = quad_terms(group, first_places, (2, 3), meta, some, side_x, mine, (), (F32, F32))
+    gathered, acc0, acc1, acc2, acc3 = after((gathered, acc0, acc1, acc2, acc3))
+
     last_places = sorted(set(gathered) - set(first_places))
     rest = [gathered[place] for place in last_places]
-    acc2, out3 = quad_terms(
-        group, last_places, 2, meta, rest, side_x, (), (acc2, acc3), (F32, BF16)
+    (out3,) = quad_terms(group, last_places, (3,), meta, rest, (pts_both,), (), (acc3,), (BF16,))
+    got3 = move(out3, core)
+    (acc2,) = quad_terms(group, last_places, (2,), meta, rest, (pts_side,), (), (acc2,), (F32,))
+    last = move(sum_terms(acc2, got3), side)
+    acc0, acc1 = quad_terms(
+        group, last_places, (0, 1), meta, rest, near_x, (), (acc0, acc1), (F32, F32)
     )
-    got3 = move(out3, core)
-    acc0, acc1 = quad_terms(group, last_places, 0, meta, rest, near_x, (), (acc0, acc1), (F32, F32))
-    got3, acc0, acc1 = after((got3, acc0, acc1))
-    last = move(sum_terms(acc2, got3), side)
     acc0, *out1 = cross_terms(meta, near_x, (acc0, acc1), cross_p, cross_w)
     extra = jnp.concatenate([move(half, core) for half in out1], axis=0)
     return acc0 + extra.astype(F32) + last.astype(F32)

time: 103 us -> 93.5 us (0.908); the launches traced: 103 us -> 92 us
  waiting for transfers between devices: 53.1 us -> 42.8 us
  starting transfers between devices: 25.6 us -> 24.4 us
    ppermute x20 -> x27, waiting for transfers between devices: 53.1 us -> 42.8 us  [move(): lax.ppermute(value, 'pts', [(a, b) for a, b in pairs if b is not None])]
    ppermute x20 -> x27, starting transfers between devices: 25.6 us -> 24.4 us  [move(): lax.ppermute(value, 'pts', [(a, b) for a, b in pairs if b is not None])]
    pallas_call x8 -> x9, Pallas kernels: 19.9 us -> 20.4 us  [call(): pl.pallas_call(body, out_shape=kinds, in_specs=[smem()] * len(scalars) +...]
  transfers between devices with their start and end apart: 20 -> 27, of which waited for: 11 -> 10; matrix products, arithmetic and copies ran while one was open for 0% -> 0% of each run, Pallas kernels for 17% -> 21%
where the time goes in v3:
time: 93.5 us; the launch traced here: 92 us
  waiting for transfers between devices  42.8 us (46%)
  starting transfers between devices  24.4 us (26%)
  Pallas kernels  20.4 us (22%)
  between operations  1.61 us (2%)
  other arithmetic  1.44 us (2%)
  local copies, waits for them, and re-layouts  1.38 us (1%)
    ppermute x27, waiting for transfers between devices, move(): lax.ppermute(value, 'pts', [(a, b) for a, b in pairs if b is not None])  42.8 us
    ppermute x27, starting transfers between devices, move(): lax.ppermute(value, 'pts', [(a, b) for a, b in pairs if b is not None])  24.4 us
    pallas_call x9, Pallas kernels, call(): pl.pallas_call(body, out_shape=kinds, in_specs=[smem()] * len(scalars) +...  20.4 us
  transfers between devices with their start and end apart: 27, of which 10 were waited for; matrix products, arithmetic and copies ran while one was open for 0% of the time, Pallas kernels for 21%

profile of v3, /device:TPU:7, one launch (start us, length us, event | category | flops | bytes accessed | tf_op | source)
XLA Modules:
  0.0 92.0 jit_solution(13972028238296657805)
XLA Ops:
  1.4 1.0 %copy-done.1 = bf16[512,512]{1,0:T(8,128)(2,1)S(1)} copy-done((bf16[512,512]{1,0:T(8,128)(2,1)S(1)}, bf16[512,512]{1,0:T(8,128)(2,1)}, u32[]{:S(2)}) %copy-start.1) | copy-done | bytes 524312
  2.4 1.5 %shard_map.82 = (f32[2,128,512]{2,1,0:T(8,128)S(1)}, s32[1,128]{1,0:T(1,128)S(1)}, bf16[64,512]{1,0:T(8,128)(2,1)S(1)}, bf16[64,512]{1,0:T(8,128)(2,1)S(1)}, bf1...) custom-call(s32[1,4]{1,0:T(1,128)S(1)} %copy-done.2, s32[1]{0:T(128)S(6)} %copy.9.near_count, s32[1,4]{1,0:T(1,128)S(1)} %copy-done.3, ...), custom_call_target="tpu_custom_call" | custom-call | flops 1000 | bytes 1000 | tf_op jit(solution)/shard_map/pallas_call | solution.py:78
  3.9 0.7 collective-permute-start.3
  4.7 0.4 collective-permute-start.1
  5.2 3.1 %collective-permute-start.7 = (bf16[512,512]{1,0:T(8,128)(2,1)}, bf16[512,512]{1,0:T(8,128)(2,1)S(1)}, u32[]{:S(2)}, u32[]{:S(2)}) collective-permute-start(bf16[512,512]{1,0:T(8,128)(2,1)} %refs_7_.3), channel_id=1, source_target_pairs={{2,6},{3,7},{4,0},{5,1},{6,10},{7,11},{8,4},{9,5},{10,14},{11,15},... | collective-permute-start | bytes 1572872 | tf_op jit(solution)/shard_map/ppermute | solution.py:266
  8.7 4.3 %collective-permute-done.4 = bf16[128,512]{1,0:T(8,128)(2,1)S(1)} collective-permute-done((bf16[128,512]{1,0:T(8,128)(2,1)S(1)}, bf16[128,512]{1,0:T(8,128)(2,1)S(1)}, u32[]{:S(2)}, u32[]{:S(2)}) %collective-permute-start.4) | collective-permute-done | bytes 131104 | tf_op jit(solution)/shard_map/ppermute | solution.py:266
  14.3 1.3 %collective-permute-start.6 = (bf16[128,1536]{1,0:T(8,128)(2,1)S(1)}, bf16[128,1536]{1,0:T(8,128)(2,1)S(1)}, u32[]{:S(2)}, u32[]{:S(2)}) collective-permute-start(bf16[128,1536]{1,0:T(8,128)(2,1)S(1)} %shard_map.83.refs_0_), channel_id=1, source_target_pairs={{0,8},{1,9},{2,10},{3,11},{4,12},{5,13},{6,14},{7,15},{8,16},{9,17... | collective-permute-start | bytes 1179656 | tf_op jit(solution)/shard_map/ppermute | solution.py:266
  15.6 4.8 %collective-permute-done.7 = bf16[512,512]{1,0:T(8,128)(2,1)S(1)} collective-permute-done((bf16[512,512]{1,0:T(8,128)(2,1)}, bf16[512,512]{1,0:T(8,128)(2,1)S(1)}, u32[]{:S(2)}, u32[]{:S(2)}) %collective-permute-start.7) | collective-permute-done | bytes 524320 | tf_op jit(solution)/shard_map/ppermute | solution.py:266
  20.4 2.2 %collective-permute-start.8 = (bf16[256,512]{1,0:T(8,128)(2,1)S(1)}, bf16[256,512]{1,0:T(8,128)(2,1)S(1)}, u32[]{:S(2)}, u32[]{:S(2)}) collective-permute-start(bf16[256,512]{1,0:T(8,128)(2,1)S(1)} %get-tuple-element.82), channel_id=1, source_target_pairs={{0,1},{1,0},{2,3},{3,2},{4,5},{5,4},{6,7},{7,6},{8,9},{9,8},{10,11... | collective-permute-start | bytes 786440 | tf_op jit(solution)/shard_map/ppermute | solution.py:266
  22.7 6.1 %collective-permute-done.5.refs_1_ = bf16[128,1536]{1,0:T(8,128)(2,1)S(1)} collective-permute-done((bf16[128,1536]{1,0:T(8,128)(2,1)S(1)}, bf16[128,1536]{1,0:T(8,128)(2,1)S(1)}, u32[]{:S(2)}, u32[]{:S(2)}) %collective-permute-start.5) | collective-permute-done | bytes 393248 | tf_op jit(solution)/shard_map/ppermute | solution.py:266
  28.9 5.2 %collective-permute-start.11 = (bf16[128,1536]{1,0:T(8,128)(2,1)S(1)}, bf16[128,1536]{1,0:T(8,128)(2,1)S(1)}, u32[]{:S(2)}, u32[]{:S(2)}) collective-permute-start(bf16[128,1536]{1,0:T(8,128)(2,1)S(1)} %shard_map.83.refs_0_), channel_id=1, source_target_pairs={{0,24},{1,25},{2,26},{3,27},{4,28},{5,29},{6,30},{7,31},{8,0},{9,1... | collective-permute-start | bytes 1179656 | tf_op jit(solution)/shard_map/ppermute | solution.py:266
  34.1 1.1 %collective-permute-start.13 = (s32[1,128]{1,0:T(1,128)S(1)}, s32[1,128]{1,0:T(1,128)S(1)}, u32[]{:S(2)}, u32[]{:S(2)}) collective-permute-start(s32[1,128]{1,0:T(1,128)S(1)} %get-tuple-element.54), channel_id=1, source_target_pairs={{0,1},{1,0},{2,3},{3,2},{4,5},{5,4},{6,7},{7,6},{8,9},{9,8},{10,11... | collective-permute-start | bytes 1544 | tf_op jit(solution)/shard_map/ppermute | solution.py:266
  35.2 0.8 collective-permute-done.13
  36.0 2.7 %collective-permute-done.14 = s32[2,128]{1,0:T(2,128)S(1)} collective-permute-done((s32[2,128]{1,0:T(2,128)S(1)}, s32[2,128]{1,0:T(2,128)S(1)}, u32[]{:S(2)}, u32[]{:S(2)}) %collective-permute-start.14) | collective-permute-done | bytes 1056 | tf_op jit(solution)/shard_map/ppermute | solution.py:266
  38.7 1.2 %collective-permute-start.15 = (bf16[512,1024]{1,0:T(8,128)(2,1)S(1)}, bf16[512,1024]{1,0:T(8,128)(2,1)S(1)}, u32[]{:S(2)}, u32[]{:S(2)}) collective-permute-start(bf16[512,1024]{1,0:T(8,128)(2,1)S(1)} %copy-done), channel_id=1, source_target_pairs={{0,1},{1,0},{2,3},{3,2},{4,5},{5,4},{6,7},{7,6},{8,9},{9,8},{10,11... | collective-permute-start | bytes 3145736 | tf_op jit(solution)/shard_map/ppermute | solution.py:266
  39.9 1.8 %collective-permute-done.11.refs_3_ = bf16[128,1536]{1,0:T(8,128)(2,1)S(1)} collective-permute-done((bf16[128,1536]{1,0:T(8,128)(2,1)S(1)}, bf16[128,1536]{1,0:T(8,128)(2,1)S(1)}, u32[]{:S(2)}, u32[]{:S(2)}) %collective-permute-start.11) | collective-permute-done | bytes 393248 | tf_op jit(solution)/shard_map/ppermute | solution.py:266
  41.8 1.7 %collective-permute-start.19 = (bf16[512,1024]{1,0:T(8,128)(2,1)S(1)}, bf16[512,1024]{1,0:T(8,128)(2,1)S(1)}, u32[]{:S(2)}, u32[]{:S(2)}) collective-permute-start(bf16[512,1024]{1,0:T(8,128)(2,1)S(1)} %collective-permute-done.12.refs_4_), channel_id=1, source_target_pairs={{0,1},{1,0},{2,3},{3,2},{4,5},{5,4},{6,7},{7,6},{8,9},{9,8},{10,11... | collective-permute-start | bytes 3145736 | tf_op jit(solution)/shard_map/ppermute | solution.py:266
  43.6 1.3 %collective-permute-start.17 = (bf16[128,1536]{1,0:T(8,128)(2,1)S(1)}, bf16[128,1536]{1,0:T(8,128)(2,1)S(1)}, u32[]{:S(2)}, u32[]{:S(2)}) collective-permute-start(bf16[128,1536]{1,0:T(8,128)(2,1)S(1)} %collective-permute-done.10.refs_0_), channel_id=1, source_target_pairs={{0,8},{1,9},{2,10},{3,11},{4,12},{5,13},{6,14},{7,15},{8,16},{9,17... | collective-permute-start | bytes 1179656 | tf_op jit(solution)/shard_map/ppermute | solution.py:266
  45.0 1.5 %collective-permute-start.21 = (bf16[512,512]{1,0:T(8,128)(2,1)S(1)}, bf16[512,512]{1,0:T(8,128)(2,1)S(1)}, u32[]{:S(2)}, u32[]{:S(2)}) collective-permute-start(bf16[512,512]{1,0:T(8,128)(2,1)S(1)} %pad_maximum_fusion), channel_id=1, source_target_pairs={{0,2},{1,3},{2,0},{3,1},{4,6},{5,7},{6,4},{7,5},{8,10},{9,11},{10,... | collective-permute-start | bytes 1572872 | tf_op jit(solution)/shard_map/ppermute | solution.py:266
  46.5 2.0 %collective-permute-start.20 = (bf16[512,1024]{1,0:T(8,128)(2,1)S(1)}, bf16[512,1024]{1,0:T(8,128)(2,1)S(1)}, u32[]{:S(2)}, u32[]{:S(2)}) collective-permute-start(bf16[512,1024]{1,0:T(8,128)(2,1)S(1)} %collective-permute-done.12.refs_4_), channel_id=1, source_target_pairs={{0,4},{1,5},{4,8},{5,9},{6,2},{7,3},{8,12},{9,13},{10,6},{11,7},{1... | collective-permute-start | bytes 3145736 | tf_op jit(solution)/shard_map/ppermute | solution.py:266
  48.5 5.7 %shard_map.84 = (f32[512,512]{1,0:T(8,128)S(1)}, f32[512,512]{1,0:T(8,128)S(1)}) custom-call(s32[4,128]{1,0:T(4,128)S(1)} %pad_add_fusion.meta, bf16[128,1536]{1,0:T(8,128)(2,1)S(1)} %shard_map.83.refs_0_, bf16[128,1536]{1,0:T(8,128)(2,1)S(1)} %collective-permute-done.5.refs_1_, bf16[128,1536]{1,0:T(8,128)(2,1)S(1)} %collective-permute-done.6.refs_2_, ...), custom_call_target="tpu_custom_call" | custom-call | flops 1000 | bytes 1000 | tf_op jit(solution)/shard_map/pallas_call | solution.py:78
  54.2 4.2 %shard_map.85 = (f32[512,512]{1,0:T(8,128)S(1)}, f32[512,512]{1,0:T(8,128)S(1)}) custom-call(s32[4,128]{1,0:T(4,128)S(1)} %pad_add_fusion.meta, bf16[128,1536]{1,0:T(8,128)(2,1)S(1)} %shard_map.83.refs_0_, bf16[128,1536]{1,0:T(8,128)(2,1)S(1)} %collective-permute-done.5.refs_1_, bf16[128,1536]{1,0:T(8,128)(2,1)S(1)} %collective-permute-done.6.refs_2_, ...), custom_call_target="tpu_custom_call" | custom-call | flops 1000 | bytes 1000 | tf_op jit(solution)/shard_map/pallas_call | solution.py:78
  58.4 6.9 %collective-permute-done.17.refs_2_ = bf16[128,1536]{1,0:T(8,128)(2,1)S(1)} collective-permute-done((bf16[128,1536]{1,0:T(8,128)(2,1)S(1)}, bf16[128,1536]{1,0:T(8,128)(2,1)S(1)}, u32[]{:S(2)}, u32[]{:S(2)}) %collective-permute-start.17) | collective-permute-done | bytes 393248 | tf_op jit(solution)/shard_map/ppermute | solution.py:266
  65.4 2.2 %shard_map.89 = bf16[512,512]{1,0:T(8,128)(2,1)S(1)} custom-call(s32[4,128]{1,0:T(4,128)S(1)} %pad_add_fusion.meta, bf16[128,1536]{1,0:T(8,128)(2,1)S(1)} %collective-permute-done.10.refs_0_, bf16[128,1536]{1,0:T(8,128)(2,1)S(1)} %collective-permute-done.16.refs_1_, bf16[128,1536]{1,0:T(8,128)(2,1)S(1)} %collective-permute-done.17.refs_2_, ...), custom_call_target="tpu_custom_call" | custom-call | flops 1000 | bytes 1000 | tf_op jit(solution)/shard_map/pallas_call | solution.py:78
  67.6 0.6 collective-permute-start.25
  68.3 2.0 %shard_map.88.one = f32[512,512]{1,0:T(8,128)S(1)} custom-call(s32[4,128]{1,0:T(4,128)S(1)} %pad_add_fusion.meta, bf16[128,1536]{1,0:T(8,128)(2,1)S(1)} %collective-permute-done.10.refs_0_, bf16[128,1536]{1,0:T(8,128)(2,1)S(1)} %collective-permute-done.16.refs_1_, bf16[128,1536]{1,0:T(8,128)(2,1)S(1)} %collective-permute-done.17.refs_2_, ...), custom_call_target="tpu_custom_call" | custom-call | flops 1000 | bytes 1000 | tf_op jit(solution)/shard_map/pallas_call | solution.py:78
  70.6 3.4 %shard_map.86 = (f32[512,512]{1,0:T(8,128)S(1)}, f32[512,512]{1,0:T(8,128)S(1)}) custom-call(s32[4,128]{1,0:T(4,128)S(1)} %pad_add_fusion.meta, bf16[128,1536]{1,0:T(8,128)(2,1)S(1)} %collective-permute-done.10.refs_0_, bf16[128,1536]{1,0:T(8,128)(2,1)S(1)} %collective-permute-done.16.refs_1_, bf16[128,1536]{1,0:T(8,128)(2,1)S(1)} %collective-permute-done.17.refs_2_, ...), custom_call_target="tpu_custom_call" | custom-call | flops 1000 | bytes 1000 | tf_op jit(solution)/shard_map/pallas_call | solution.py:78
  74.0 13.7 %collective-permute-done.20.ypts = bf16[512,1024]{1,0:T(8,128)(2,1)S(1)} collective-permute-done((bf16[512,1024]{1,0:T(8,128)(2,1)S(1)}, bf16[512,1024]{1,0:T(8,128)(2,1)S(1)}, u32[]{:S(2)}, u32[]{:S(2)}) %collective-permute-start.20) | collective-permute-done | bytes 1048608 | tf_op jit(solution)/shard_map/ppermute | solution.py:266
  87.7 0.9 %shard_map.87 = (f32[512,512]{1,0:T(8,128)S(1)}, bf16[256,512]{1,0:T(8,128)(2,1)S(1)}, bf16[256,512]{1,0:T(8,128)(2,1)S(1)}) custom-call(s32[4,128]{1,0:T(4,128)S(1)} %pad_add_fusion.meta, bf16[512,1024]{1,0:T(8,128)(2,1)S(1)} %copy-done, bf16[512,1024]{1,0:T(8,128)(2,1)S(1)} %collective-permute-done.15.refs_5_.other, ...), custom_call_target="tpu_custom_call" | custom-call | flops 1000 | bytes 1000 | tf_op jit(solution)/shard_map/pallas_call | solution.py:78
  88.7 0.6 collective-permute-start.24
  89.3 1.1 %collective-permute-done.24 = bf16[256,512]{1,0:T(8,128)(2,1)S(1)} collective-permute-done((bf16[256,512]{1,0:T(8,128)(2,1)S(1)}, bf16[256,512]{1,0:T(8,128)(2,1)S(1)}, u32[]{:S(2)}, u32[]{:S(2)}) %collective-permute-start.24) | collective-permute-done | bytes 262176 | tf_op jit(solution)/shard_map/ppermute | solution.py:266
  90.8 1.2 %convert_add_fusion = f32[512,512]{1,0:T(8,128)} fusion(bf16[512,512]{1,0:T(8,128)(2,1)S(1)} %collective-permute-done.26, f32[512,512]{1,0:T(8,128)S(1)} %get-tuple-element.76, bf16[256,512]{1,0:T(8,128)(2,1)S(1)} %collective-permute-done.24, bf16[256,512]{1,0:T(8,128)(2,1)S(1)} %collective-permute-done.23), kind=kLoop, calls=%fused_computation | loop fusion | flops 1835008 | bytes 3145728 | tf_op jit(solution)/shard_map/add | solution.py:356
  (50 shorter events, 2.9 us)
Async XLA Ops:
  0.7 0.7 copy-start.2
  0.7 0.7 copy-start.3
  1.4 1.0 %copy-start.1 = (bf16[512,512]{1,0:T(8,128)(2,1)S(1)}, bf16[512,512]{1,0:T(8,128)(2,1)}, u32[]{:S(2)}) copy-start(bf16[512,512]{1,0:T(8,128)(2,1)} %proj.1) | copy-start | bytes 1572868
  3.9 4.5 %collective-permute-start.3 = (bf16[64,512]{1,0:T(8,128)(2,1)S(1)}, bf16[64,512]{1,0:T(8,128)(2,1)S(1)}, u32[]{:S(2)}, u32[]{:S(2)}) collective-permute-start(bf16[64,512]{1,0:T(8,128)(2,1)S(1)} %get-tuple-element.47), channel_id=1, source_target_pairs={{0,1},{1,0},{2,3},{3,2},{4,5},{5,4},{6,7},{7,6},{8,9},{9,8},{10,11... | collective-permute-start | bytes 196616 | tf_op jit(solution)/shard_map/ppermute | solution.py:266
  4.6 3.8 %collective-permute-start.2 = (bf16[64,512]{1,0:T(8,128)(2,1)S(1)}, bf16[64,512]{1,0:T(8,128)(2,1)S(1)}, u32[]{:S(2)}, u32[]{:S(2)}) collective-permute-start(bf16[64,512]{1,0:T(8,128)(2,1)S(1)} %get-tuple-element.46), channel_id=1, source_target_pairs={{0,1},{1,0},{2,3},{3,2},{4,5},{5,4},{6,7},{7,6},{8,9},{9,8},{10,11... | collective-permute-start | bytes 196616 | tf_op jit(solution)/shard_map/ppermute | solution.py:266
  4.7 3.7 %collective-permute-start.1 = (bf16[64,512]{1,0:T(8,128)(2,1)S(1)}, bf16[64,512]{1,0:T(8,128)(2,1)S(1)}, u32[]{:S(2)}, u32[]{:S(2)}) collective-permute-start(bf16[64,512]{1,0:T(8,128)(2,1)S(1)} %get-tuple-element.45), channel_id=1, source_target_pairs={{0,1},{1,0},{2,3},{3,2},{4,5},{5,4},{6,7},{7,6},{8,9},{9,8},{10,11... | collective-permute-start | bytes 196616 | tf_op jit(solution)/shard_map/ppermute | solution.py:266
  5.1 3.3 %collective-permute-start = (bf16[64,512]{1,0:T(8,128)(2,1)S(1)}, bf16[64,512]{1,0:T(8,128)(2,1)S(1)}, u32[]{:S(2)}, u32[]{:S(2)}) collective-permute-start(bf16[64,512]{1,0:T(8,128)(2,1)S(1)} %get-tuple-element.44), channel_id=1, source_target_pairs={{0,1},{1,0},{2,3},{3,2},{4,5},{5,4},{6,7},{7,6},{8,9},{9,8},{10,11... | collective-permute-start | bytes 196616 | tf_op jit(solution)/shard_map/ppermute | solution.py:266
  5.2 15.2 %collective-permute-start.7 = (bf16[512,512]{1,0:T(8,128)(2,1)}, bf16[512,512]{1,0:T(8,128)(2,1)S(1)}, u32[]{:S(2)}, u32[]{:S(2)}) collective-permute-start(bf16[512,512]{1,0:T(8,128)(2,1)} %refs_7_.3), channel_id=1, source_target_pairs={{2,6},{3,7},{4,0},{5,1},{6,10},{7,11},{8,4},{9,5},{10,14},{11,15},... | collective-permute-start | bytes 1572872 | tf_op jit(solution)/shard_map/ppermute | solution.py:266
  8.4 4.6 %copy-start = (bf16[512,1024]{1,0:T(8,128)(2,1)S(1)}, bf16[512,1024]{1,0:T(8,128)(2,1)}, u32[]{:S(2)}) copy-start(bf16[512,1024]{1,0:T(8,128)(2,1)} %own.1) | copy-start | bytes 3145732
  8.6 4.4 %collective-permute-start.4 = (bf16[128,512]{1,0:T(8,128)(2,1)S(1)}, bf16[128,512]{1,0:T(8,128)(2,1)S(1)}, u32[]{:S(2)}, u32[]{:S(2)}) collective-permute-start(bf16[128,512]{1,0:T(8,128)(2,1)S(1)} %fusion.1), channel_id=1, source_target_pairs={{0,2},{1,3},{2,0},{3,1},{4,6},{5,7},{6,4},{7,5},{8,10},{9,11},{10,... | collective-permute-start | bytes 393224 | tf_op jit(solution)/shard_map/ppermute | solution.py:266
  13.0 0.7 copy-start.4
  13.0 28.8 %collective-permute-start.12 = (bf16[512,1024]{1,0:T(8,128)(2,1)S(1)}, bf16[512,1024]{1,0:T(8,128)(2,1)S(1)}, u32[]{:S(2)}, u32[]{:S(2)}) collective-permute-start(bf16[512,1024]{1,0:T(8,128)(2,1)S(1)} %copy-done), channel_id=1, source_target_pairs={{0,2},{1,3},{2,0},{3,1},{4,6},{5,7},{6,4},{7,5},{8,10},{9,11},{10,... | collective-permute-start | bytes 3145736 | tf_op jit(solution)/shard_map/ppermute | solution.py:266
  14.0 14.8 %collective-permute-start.5 = (bf16[128,1536]{1,0:T(8,128)(2,1)S(1)}, bf16[128,1536]{1,0:T(8,128)(2,1)S(1)}, u32[]{:S(2)}, u32[]{:S(2)}) collective-permute-start(bf16[128,1536]{1,0:T(8,128)(2,1)S(1)} %shard_map.83.refs_0_), channel_id=1, source_target_pairs={{0,4},{1,5},{2,6},{3,7},{4,0},{5,1},{6,2},{7,3},{8,12},{9,13},{10,... | collective-permute-start | bytes 1179656 | tf_op jit(solution)/shard_map/ppermute | solution.py:266
  14.3 14.5 %collective-permute-start.6 = (bf16[128,1536]{1,0:T(8,128)(2,1)S(1)}, bf16[128,1536]{1,0:T(8,128)(2,1)S(1)}, u32[]{:S(2)}, u32[]{:S(2)}) collective-permute-start(bf16[128,1536]{1,0:T(8,128)(2,1)S(1)} %shard_map.83.refs_0_), channel_id=1, source_target_pairs={{0,8},{1,9},{2,10},{3,11},{4,12},{5,13},{6,14},{7,15},{8,16},{9,17... | collective-permute-start | bytes 1179656 | tf_op jit(solution)/shard_map/ppermute | solution.py:266
  20.4 8.4 %collective-permute-start.8 = (bf16[256,512]{1,0:T(8,128)(2,1)S(1)}, bf16[256,512]{1,0:T(8,128)(2,1)S(1)}, u32[]{:S(2)}, u32[]{:S(2)}) collective-permute-start(bf16[256,512]{1,0:T(8,128)(2,1)S(1)} %get-tuple-element.82), channel_id=1, source_target_pairs={{0,1},{1,0},{2,3},{3,2},{4,5},{5,4},{6,7},{7,6},{8,9},{9,8},{10,11... | collective-permute-start | bytes 786440 | tf_op jit(solution)/shard_map/ppermute | solution.py:266
  22.6 6.2 %collective-permute-start.9 = (bf16[256,512]{1,0:T(8,128)(2,1)S(1)}, bf16[256,512]{1,0:T(8,128)(2,1)S(1)}, u32[]{:S(2)}, u32[]{:S(2)}) collective-permute-start(bf16[256,512]{1,0:T(8,128)(2,1)S(1)} %get-tuple-element.81), channel_id=1, source_target_pairs={{0,1},{1,0},{2,3},{3,2},{4,5},{5,4},{6,7},{7,6},{8,9},{9,8},{10,11... | collective-permute-start | bytes 786440 | tf_op jit(solution)/shard_map/ppermute | solution.py:266
  28.8 11.1 %collective-permute-start.10 = (bf16[128,1536]{1,0:T(8,128)(2,1)S(1)}, bf16[128,1536]{1,0:T(8,128)(2,1)S(1)}, u32[]{:S(2)}, u32[]{:S(2)}) collective-permute-start(bf16[128,1536]{1,0:T(8,128)(2,1)S(1)} %collective-permute-done.6.refs_2_), channel_id=1, source_target_pairs={{0,4},{1,5},{2,6},{3,7},{4,0},{5,1},{6,2},{7,3},{8,12},{9,13},{10,... | collective-permute-start | bytes 1179656 | tf_op jit(solution)/shard_map/ppermute | solution.py:266
  28.9 12.9 %collective-permute-start.11 = (bf16[128,1536]{1,0:T(8,128)(2,1)S(1)}, bf16[128,1536]{1,0:T(8,128)(2,1)S(1)}, u32[]{:S(2)}, u32[]{:S(2)}) collective-permute-start(bf16[128,1536]{1,0:T(8,128)(2,1)S(1)} %shard_map.83.refs_0_), channel_id=1, source_target_pairs={{0,24},{1,25},{2,26},{3,27},{4,28},{5,29},{6,30},{7,31},{8,0},{9,1... | collective-permute-start | bytes 1179656 | tf_op jit(solution)/shard_map/ppermute | solution.py:266
  34.1 1.9 %collective-permute-start.13 = (s32[1,128]{1,0:T(1,128)S(1)}, s32[1,128]{1,0:T(1,128)S(1)}, u32[]{:S(2)}, u32[]{:S(2)}) collective-permute-start(s32[1,128]{1,0:T(1,128)S(1)} %get-tuple-element.54), channel_id=1, source_target_pairs={{0,1},{1,0},{2,3},{3,2},{4,5},{5,4},{6,7},{7,6},{8,9},{9,8},{10,11... | collective-permute-start | bytes 1544 | tf_op jit(solution)/shard_map/ppermute | solution.py:266
  36.0 2.7 %collective-permute-start.14 = (s32[2,128]{1,0:T(2,128)S(1)}, s32[2,128]{1,0:T(2,128)S(1)}, u32[]{:S(2)}, u32[]{:S(2)}) collective-permute-start(s32[2,128]{1,0:T(2,128)S(1)} %pad_add_fusion.1), channel_id=1, source_target_pairs={{0,2},{1,3},{2,0},{3,1},{4,6},{5,7},{6,4},{7,5},{8,10},{9,11},{10,... | collective-permute-start | bytes 3080 | tf_op jit(solution)/shard_map/ppermute | solution.py:266
  38.7 6.3 %collective-permute-start.15 = (bf16[512,1024]{1,0:T(8,128)(2,1)S(1)}, bf16[512,1024]{1,0:T(8,128)(2,1)S(1)}, u32[]{:S(2)}, u32[]{:S(2)}) collective-permute-start(bf16[512,1024]{1,0:T(8,128)(2,1)S(1)} %copy-done), channel_id=1, source_target_pairs={{0,1},{1,0},{2,3},{3,2},{4,5},{5,4},{6,7},{7,6},{8,9},{9,8},{10,11... | collective-permute-start | bytes 3145736 | tf_op jit(solution)/shard_map/ppermute | solution.py:266
  41.8 4.7 %collective-permute-start.19 = (bf16[512,1024]{1,0:T(8,128)(2,1)S(1)}, bf16[512,1024]{1,0:T(8,128)(2,1)S(1)}, u32[]{:S(2)}, u32[]{:S(2)}) collective-permute-start(bf16[512,1024]{1,0:T(8,128)(2,1)S(1)} %collective-permute-done.12.refs_4_), channel_id=1, source_target_pairs={{0,1},{1,0},{2,3},{3,2},{4,5},{5,4},{6,7},{7,6},{8,9},{9,8},{10,11... | collective-permute-start | bytes 3145736 | tf_op jit(solution)/shard_map/ppermute | solution.py:266
  43.4 15.0 %collective-permute-start.16 = (bf16[128,1536]{1,0:T(8,128)(2,1)S(1)}, bf16[128,1536]{1,0:T(8,128)(2,1)S(1)}, u32[]{:S(2)}, u32[]{:S(2)}) collective-permute-start(bf16[128,1536]{1,0:T(8,128)(2,1)S(1)} %collective-permute-done.6.refs_2_), channel_id=1, source_target_pairs={{0,8},{1,9},{2,10},{3,11},{4,12},{5,13},{6,14},{7,15},{8,16},{9,17... | collective-permute-start | bytes 1179656 | tf_op jit(solution)/shard_map/ppermute | solution.py:266
  43.6 21.7 %collective-permute-start.17 = (bf16[128,1536]{1,0:T(8,128)(2,1)S(1)}, bf16[128,1536]{1,0:T(8,128)(2,1)S(1)}, u32[]{:S(2)}, u32[]{:S(2)}) collective-permute-start(bf16[128,1536]{1,0:T(8,128)(2,1)S(1)} %collective-permute-done.10.refs_0_), channel_id=1, source_target_pairs={{0,8},{1,9},{2,10},{3,11},{4,12},{5,13},{6,14},{7,15},{8,16},{9,17... | collective-permute-start | bytes 1179656 | tf_op jit(solution)/shard_map/ppermute | solution.py:266
  44.9 20.4 %collective-permute-start.18 = (bf16[128,1536]{1,0:T(8,128)(2,1)S(1)}, bf16[128,1536]{1,0:T(8,128)(2,1)S(1)}, u32[]{:S(2)}, u32[]{:S(2)}) collective-permute-start(bf16[128,1536]{1,0:T(8,128)(2,1)S(1)} %collective-permute-done.11.refs_3_), channel_id=1, source_target_pairs={{0,4},{1,5},{2,6},{3,7},{4,0},{5,1},{6,2},{7,3},{8,12},{9,13},{10,... | collective-permute-start | bytes 1179656 | tf_op jit(solution)/shard_map/ppermute | solution.py:266
  45.0 23.2 %collective-permute-start.21 = (bf16[512,512]{1,0:T(8,128)(2,1)S(1)}, bf16[512,512]{1,0:T(8,128)(2,1)S(1)}, u32[]{:S(2)}, u32[]{:S(2)}) collective-permute-start(bf16[512,512]{1,0:T(8,128)(2,1)S(1)} %pad_maximum_fusion), channel_id=1, source_target_pairs={{0,2},{1,3},{2,0},{3,1},{4,6},{5,7},{6,4},{7,5},{8,10},{9,11},{10,... | collective-permute-start | bytes 1572872 | tf_op jit(solution)/shard_map/ppermute | solution.py:266
  46.5 41.2 %collective-permute-start.20 = (bf16[512,1024]{1,0:T(8,128)(2,1)S(1)}, bf16[512,1024]{1,0:T(8,128)(2,1)S(1)}, u32[]{:S(2)}, u32[]{:S(2)}) collective-permute-start(bf16[512,1024]{1,0:T(8,128)(2,1)S(1)} %collective-permute-done.12.refs_4_), channel_id=1, source_target_pairs={{0,4},{1,5},{4,8},{5,9},{6,2},{7,3},{8,12},{9,13},{10,6},{11,7},{1... | collective-permute-start | bytes 3145736 | tf_op jit(solution)/shard_map/ppermute | solution.py:266
  67.6 2.8 %collective-permute-start.25 = (bf16[512,512]{1,0:T(8,128)(2,1)S(1)}, bf16[512,512]{1,0:T(8,128)(2,1)S(1)}, u32[]{:S(2)}, u32[]{:S(2)}) collective-permute-start(bf16[512,512]{1,0:T(8,128)(2,1)S(1)} %shard_map.89), channel_id=1, source_target_pairs={{0,1},{1,0},{2,3},{3,2},{4,5},{5,4},{6,7},{7,6},{8,9},{9,8},{10,11... | collective-permute-start | bytes 1572872 | tf_op jit(solution)/shard_map/ppermute | solution.py:266
  68.3 5.7 %collective-permute-start.22 = (bf16[512,512]{1,0:T(8,128)(2,1)S(1)}, bf16[512,512]{1,0:T(8,128)(2,1)S(1)}, u32[]{:S(2)}, u32[]{:S(2)}) collective-permute-start(bf16[512,512]{1,0:T(8,128)(2,1)S(1)} %collective-permute-done.21), channel_id=1, source_target_pairs={{0,1},{1,0},{2,3},{3,2},{4,5},{5,4},{6,7},{7,6},{8,9},{9,8},{10,11... | collective-permute-start | bytes 1572872 | tf_op jit(solution)/shard_map/ppermute | solution.py:266
  70.5 20.2 %collective-permute-start.26 = (bf16[512,512]{1,0:T(8,128)(2,1)S(1)}, bf16[512,512]{1,0:T(8,128)(2,1)S(1)}, u32[]{:S(2)}, u32[]{:S(2)}) collective-permute-start(bf16[512,512]{1,0:T(8,128)(2,1)S(1)} %shard_map.90), channel_id=1, source_target_pairs={{0,2},{1,3},{2,0},{3,1},{4,6},{5,7},{6,4},{7,5},{8,10},{9,11},{10,... | collective-permute-start | bytes 1572872 | tf_op jit(solution)/shard_map/ppermute | solution.py:266
  88.7 1.7 %collective-permute-start.24 = (bf16[256,512]{1,0:T(8,128)(2,1)S(1)}, bf16[256,512]{1,0:T(8,128)(2,1)S(1)}, u32[]{:S(2)}, u32[]{:S(2)}) collective-permute-start(bf16[256,512]{1,0:T(8,128)(2,1)S(1)} %get-tuple-element.78), channel_id=1, source_target_pairs={{0,1},{1,0},{2,3},{3,2},{4,5},{5,4},{6,7},{7,6},{8,9},{9,8},{10,11... | collective-permute-start | bytes 786440 | tf_op jit(solution)/shard_map/ppermute | solution.py:266
  89.2 1.5 %collective-permute-start.23 = (bf16[256,512]{1,0:T(8,128)(2,1)S(1)}, bf16[256,512]{1,0:T(8,128)(2,1)S(1)}, u32[]{:S(2)}, u32[]{:S(2)}) collective-permute-start(bf16[256,512]{1,0:T(8,128)(2,1)S(1)} %get-tuple-element.77), channel_id=1, source_target_pairs={{0,1},{1,0},{2,3},{3,2},{4,5},{5,4},{6,7},{7,6},{8,9},{9,8},{10,11... | collective-permute-start | bytes 786440 | tf_op jit(solution)/shard_map/ppermute | solution.py:266

commit v4 on v3

--- a/solution.py
+++ b/solution.py
@@ -20,8 +20,8 @@
 FAR_LIST = NEAR + 1
 FAR_COUNT = FAR_LIST + FAR
 LEAF = FAR_COUNT + 1
-META = 128
-PIECES = 4
+META = 16
+CUTS = 4
 
 
 def vmem():
@@ -32,8 +32,8 @@
     return pl.BlockSpec(memory_space=pltpu.SMEM)
 
 
-def params():
-    return pltpu.CompilerParams(vmem_limit_bytes=24 * MIB)
+def params(limit=24):
+    return pltpu.CompilerParams(vmem_limit_bytes=limit * MIB)
 
 
 def norm_column(points, scale):
@@ -74,70 +74,83 @@
     return jnp.dot(kern.astype(BF16), wts, preferred_element_type=F32)
 
 
-def call(body, kinds, scalars, arrays, scratch=()):
+def call(body, kinds, scalars, arrays, scratch=(), outside=(), limit=24):
     return pl.pallas_call(
         body,
         out_shape=kinds,
-        in_specs=[smem()] * len(scalars) + [vmem()] * len(arrays),
+        in_specs=[smem()] * len(scalars)
+        + [vmem()] * len(arrays)
+        + [pl.BlockSpec(memory_space=pltpu.HBM)] * len(outside),
         out_specs=jax.tree.map(lambda _: vmem(), kinds),
         scratch_shapes=scratch,
-        compiler_params=params(),
+        compiler_params=params(limit),
         cost_estimate=pl.CostEstimate(flops=1000, bytes_accessed=1000, transcendentals=0),
-    )(*scalars, *arrays)
-
-
-def project_body(near_list, near_count, far_list, far_count, wts, proj, keep, meta, *pieces):
+    )(*scalars, *arrays, *outside)
+
+
+def project_body(wts, proj, keep, *outs):
+    *gives, wts_here, proj_here, sems = outs
+    copies = []
+    for source, target in ((wts, wts_here), (proj, proj_here)):
+        rows = source.shape[0] // CUTS
+        for cut in range(CUTS):
+            part = pl.ds(cut * rows, rows)
+            copies.append(pltpu.make_async_copy(source.at[part], target.at[part], sems.at[len(copies)]))
+    for copy in copies:
+        copy.start()
+    for copy in copies:
+        copy.wait()
     leaf = lax.axis_index("pts")
-    core = leaf % 2
-    fields = [near_list[0, slot] for slot in range(NEAR)] + [near_count[0]]
-    fields += [far_list[0, slot] for slot in range(FAR)] + [far_count[0], leaf]
-    lane = lax.broadcasted_iota(jnp.int32, meta.shape, 1)
-    row = jnp.zeros(meta.shape, jnp.int32)
-    for place, field in enumerate(fields):
-        row = jnp.where(lane == place, field, row)
-    meta[...] = row
-    whole = jnp.dot(proj[...], wts[...], preferred_element_type=F32)
-    pairs, count, wcols = keep.shape
-    whole = whole.reshape(pairs, 2, count, wcols)
-    other = jnp.where(core == 0, whole[:, 1], whole[:, 0])
-    keep[...] = jnp.where(core == 0, whole[:, 0], whole[:, 1])
-    other = other.reshape(pairs * count, wcols).astype(BF16)
-    first = 0
-    for piece in pieces:
-        piece[...] = other[first : first + piece.shape[0]]
-        first += piece.shape[0]
-
-
-def project(group, lists, wts, proj):
-    count, wcols = proj.shape[0] // group, wts.shape[1]
-    pairs = group // 2
-    piece = jax.ShapeDtypeStruct((pairs * count // PIECES, wcols), BF16)
-    kinds = (
-        jax.ShapeDtypeStruct((pairs, count, wcols), F32),
-        jax.ShapeDtypeStruct((1, META), jnp.int32),
-    ) + (piece,) * PIECES
-    return call(project_body, kinds, lists, (wts, proj))
-
-
-def pack_body(idx, pts, keep, got, packed):
+    groups, count, wcols = keep.shape
+    whole = jnp.dot(proj_here[...], wts_here[...], preferred_element_type=F32)
+    whole = whole.reshape(groups, QUAD, count, wcols)
+    for turn in range(QUAD):
+        block = whole[:, QUAD - 1]
+        for place in range(QUAD - 1):
+            block = jnp.where((leaf ^ turn) % QUAD == place, whole[:, place], block)
+        if turn == 0:
+            keep[...] = block
+        else:
+            gives[turn - 1][...] = block.astype(BF16)
+
+
+def project(group, wts, proj):
+    shape = (group // QUAD, proj.shape[0] // group, wts.shape[1])
+    kinds = (jax.ShapeDtypeStruct(shape, F32),) + (jax.ShapeDtypeStruct(shape, BF16),) * (QUAD - 1)
+    scratch = [
+        pltpu.VMEM(wts.shape, BF16),
+        pltpu.VMEM(proj.shape, BF16),
+        pltpu.SemaphoreType.DMA((2 * CUTS,)),
+    ]
+    return call(project_body, kinds, (), (), scratch, (wts, proj), 54)
+
+
+def pack_body(idx, pts, keep, *refs):
+    *got, packed = refs
     rows, dim = pts.shape
     place = lax.broadcasted_iota(jnp.int32, (rows, idx.shape[1]), 0)
     pick = (place == idx[...]).astype(F32).astype(BF16)
     packed[:, :dim] = lax.dot_general(
         pick, pts[...], (((0,), (0,)), ((), ())), preferred_element_type=F32
     ).astype(BF16)
-    packed[:, dim:] = (keep[0] + got[0].astype(F32)).astype(BF16)
+    total = keep[0]
+    for part in got:
+        total = total + part[0].astype(F32)
+    packed[:, dim:] = total.astype(BF16)
 
 
 def pack(idx, pts, keep, got):
     shape = (idx.shape[1], pts.shape[1] + keep.shape[2])
-    return call(pack_body, jax.ShapeDtypeStruct(shape, BF16), (), (idx, pts, keep, got))
-
-
-def quad_body(group, places, targets, own, meta, *refs):
+    return call(pack_body, jax.ShapeDtypeStruct(shape, BF16), (), (idx, pts, keep, *got))
+
+
+def quad_body(group, places, targets, cuts, own, meta, *refs):
     packed, refs = refs[: len(places)], refs[len(places) :]
     many = len(targets)
-    xpts, refs = refs[:many], refs[many:]
+    xpts = []
+    for size in cuts:
+        xpts.append(refs[0][...] if size == 1 else jnp.concatenate([ref[...] for ref in refs[:size]], axis=0))
+        refs = refs[size:]
     if own:
         mine, mine_w, *outs = refs
     else:
@@ -162,15 +175,15 @@
         some = functools.reduce(jnp.logical_or, hits)
         away = [jnp.full((1, count), jnp.where(hit, 0.0, 1e30), F32) for hit in hits]
         far_sq = ysq + jnp.concatenate(away, axis=1)
-        xsq = norm_column(xpts[place][...], scale)
+        xsq = norm_column(xpts[place], scale)
 
         def far(place=place, xsq=xsq, far_sq=far_sq):
-            return kernel_sum(xpts[place][...], xsq, ypts, far_sq, wts)
+            return kernel_sum(xpts[place], xsq, ypts, far_sq, wts)
 
         out = outs[place]
         if own:
             def near(place=place, xsq=xsq):
-                return kernel_sum(xpts[place][...], xsq, mine[...], own_sq, mine_w[...])
+                return kernel_sum(xpts[place], xsq, mine[...], own_sq, mine_w[...])
 
             if target == 0:
                 out[...] = near()
@@ -199,11 +212,12 @@
 
 
 def quad_terms(group, places, targets, meta, packed, xpts, mine, start, kinds):
-    rows = xpts[0].shape[0]
-    wcols = packed[0].shape[1] - xpts[0].shape[1]
-    body = functools.partial(quad_body, group, tuple(places), targets, bool(mine))
+    rows = sum(part.shape[0] for part in xpts[0])
+    wcols = packed[0].shape[1] - xpts[0][0].shape[1]
+    cuts = tuple(len(parts) for parts in xpts)
+    body = functools.partial(quad_body, group, tuple(places), targets, cuts, bool(mine))
     shapes = tuple(jax.ShapeDtypeStruct((rows, wcols), kind) for kind in kinds)
-    return call(body, shapes, (meta,), (*packed, *xpts, *mine, *start))
+    return call(body, shapes, (meta,), (*packed, *sum(xpts, ()), *mine, *start))
 
 
 def sum_body(one, two, out):
@@ -214,44 +228,31 @@
     return call(sum_body, jax.ShapeDtypeStruct(one.shape, BF16), (), (one, two))
 
 
-def cross_body(meta, own, other, start, start_other, ypts, wts, acc, *halves):
+def cross_body(row, meta, xpts, start, ypts, wts, *outs):
     leaf = meta[0, LEAF]
-    away = leaf + 4 * (leaf // 2 % 2) - 2
-    scale = half_scale(own.shape[1])
-    ysq = norm_row(ypts[...], scale)
-
-    def term(xpts):
-        return kernel_sum(xpts[...], norm_column(xpts[...], scale), ypts[...], ysq, wts[...])
-
-    acc[...] = start[...]
-    hit = near_hit(meta, 0, away)
+    scale = half_scale(xpts.shape[1])
+    hit = near_hit(meta, row, leaf + 4 * (leaf // 2 % 2) - 2)
+
+    def put(value):
+        first = 0
+        for out in outs:
+            out[...] = value[first : first + out.shape[0]].astype(out.dtype)
+            first += out.shape[0]
 
     @pl.when(hit)
     def _():
-        acc[...] += term(own)
-
-    def put(value):
-        first = 0
-        for half in halves:
-            half[...] = value[first : first + half.shape[0]].astype(BF16)
-            first += half.shape[0]
-
-    hit = near_hit(meta, 1, away)
-
-    @pl.when(hit)
-    def _():
-        put(start_other[...] + term(other))
+        xsq, ysq = norm_column(xpts[...], scale), norm_row(ypts[...], scale)
+        put(start[...] + kernel_sum(xpts[...], xsq, ypts[...], ysq, wts[...]))
 
     @pl.when(jnp.logical_not(hit))
     def _():
-        put(start_other[...])
-
-
-def cross_terms(meta, xpts, start, ypts, wts):
-    rows, wcols = start[0].shape
-    half = jax.ShapeDtypeStruct((rows // 2, wcols), BF16)
-    shapes = (jax.ShapeDtypeStruct((rows, wcols), F32), half, half)
-    return call(cross_body, shapes, (meta,), (*xpts, *start, ypts, wts))
+        put(start[...])
+
+
+def cross_terms(row, meta, xpts, start, ypts, wts, kind, cuts):
+    rows, wcols = start.shape
+    shapes = (jax.ShapeDtypeStruct((rows // cuts, wcols), kind),) * cuts
+    return call(functools.partial(cross_body, row), shapes, (meta,), (xpts, start, ypts, wts))
 
 
 def shards(points, weights, node_proj, skel_idx, near_list, near_count, far_list, far_count):
@@ -288,23 +289,22 @@
 
     core, side, row = bit(0), bit(1), bit(2)
 
-    lists = (near_list, near_count, far_list, far_count)
-    keep, meta, *give = project(group, lists, weights, node_proj)
-    level = 0
-    while True:
-        got = [move(piece, bit(level)) for piece in give]
-        got = jnp.concatenate(got, axis=0).reshape(keep.shape)
-        level += 1
-        if keep.shape[0] == 1:
-            break
+    keep, *give = project(group, weights, node_proj)
+    got = [move(block, lambda source, turn=turn: source ^ turn) for turn, block in enumerate(give, 1)]
+    level = 2
+    while keep.shape[0] > 1:
+        for part in got:
+            keep = keep + part.astype(F32)
         count = keep.shape[0]
-        keep = (keep + got.astype(F32)).reshape(count // 2, 2, *keep.shape[1:])
+        keep = keep.reshape(count // 2, 2, *keep.shape[1:])
         upper = (me >> level) % 2 == 1
         give = jnp.where(upper, keep[:, 0], keep[:, 1]).astype(BF16)
-        give = [give.reshape(-1, give.shape[-1])]
         keep = jnp.where(upper, keep[:, 1], keep[:, 0])
+        got = [move(give, bit(level))]
+        level += 1
     cross_w = move(weights, along(-1))
-    cross_w = [move(half, core) for half in jnp.split(cross_w, 2)]
+    cut = weights.shape[0] * 11 // 256 * 16
+    cross_w = [move(part, core) for part in jnp.split(cross_w, [cut])]
     got, pts_later = after((got, points))
     packed = pack(skel_idx, points, keep, got)
 
@@ -319,12 +319,14 @@
     if depth > 2:
         gathered[depth - 1, 0] = move(packed, down)
     gathered[1, 1] = move(gathered[1, 0], row)
+    meta = [near_list[0], near_count, far_list[0], far_count, me[None]]
+    meta = jnp.concatenate(meta + [jnp.zeros((META - LEAF - 1,), jnp.int32)])[None]
     for hop in (core, side):
         meta = jnp.concatenate([meta, move(meta, hop)], axis=0)
     gathered, pts_side, meta = after((gathered, pts_side, meta))
     cross_w = move(move(jnp.concatenate(cross_w, axis=0), side), core)
     cross_p = move(pts_side, along(1))
-    pts_both = move(pts_side, core)
+    pts_both = (move(pts_side, core),)
     first_places = sorted(set(gathered) - {(1, 1)})
     if depth > 2:
         gathered[depth - 1, 1] = move(gathered[depth - 1, 0], row)
@@ -335,8 +337,8 @@
             gathered[turn, flip] = move(gathered[turn + 1, flip], down)
 
     mine = (points, weights)
-    near_x = (points, pts_core)
-    side_x = (pts_side, pts_both)
+    near_x = ((points,), (pts_core,))
+    side_x = ((pts_side,), pts_both)
     some = [gathered[place] for place in first_places]
     acc0, acc1 = quad_terms(group, first_places, (0, 1), meta, some, near_x, mine, (), (F32, F32))
     acc2, acc3 = quad_terms(group, first_places, (2, 3), meta, some, side_x, mine, (), (F32, F32))
@@ -346,12 +348,13 @@
     rest = [gathered[place] for place in last_places]
     (out3,) = quad_terms(group, last_places, (3,), meta, rest, (pts_both,), (), (acc3,), (BF16,))
     got3 = move(out3, core)
-    (acc2,) = quad_terms(group, last_places, (2,), meta, rest, (pts_side,), (), (acc2,), (F32,))
+    (acc2,) = quad_terms(group, last_places, (2,), meta, rest, ((pts_side,),), (), (acc2,), (F32,))
     last = move(sum_terms(acc2, got3), side)
     acc0, acc1 = quad_terms(
         group, last_places, (0, 1), meta, rest, near_x, (), (acc0, acc1), (F32, F32)
     )
-    acc0, *out1 = cross_terms(meta, near_x, (acc0, acc1), cross_p, cross_w)
+    out1 = cross_terms(1, meta, pts_core, acc1, cross_p, cross_w, BF16, 2)
+    (acc0,) = cross_terms(0, meta, points, acc0, cross_p, cross_w, F32, 1)
     extra = jnp.concatenate([move(half, core) for half in out1], axis=0)
     return acc0 + extra.astype(F32) + last.astype(F32)
 

time: 93.5 us -> 90.8 us (0.971)
  waiting for transfers between devices: 42.8 us -> 38.4 us
  Pallas kernels: 20.4 us -> 22.3 us
    ppermute x27 -> x25, waiting for transfers between devices: 42.8 us -> 38.4 us  [move(): lax.ppermute(value, 'pts', [(a, b) for a, b in pairs if b is not None])]
    pallas_call x9 -> x10, Pallas kernels: 20.4 us -> 22.3 us  [call(): pl.pallas_call(body, out_shape=kinds, in_specs=[smem()] * len(scalars) +...]
    concatenate x1, other arithmetic: 0.03 us -> 1.02 us  [shards(): cross_w = move(move(jnp.concatenate(cross_w, axis=0), side), core)]
    ppermute x27 -> x25, starting transfers between devices: 24.4 us -> 24 us  [move(): lax.ppermute(value, 'pts', [(a, b) for a, b in pairs if b is not None])]
  transfers between devices with their start and end apart: 27 -> 25, of which waited for: 10 -> 10; matrix products, arithmetic and copies ran while one was open for 0% -> 1% of each run, Pallas kernels for 21% -> 25%
where the time goes in v4:
time: 90.8 us; the launch traced here: 90.2 us
  waiting for transfers between devices  38.4 us (42%)
  starting transfers between devices  24 us (26%)
  Pallas kernels  22.3 us (25%)
  other arithmetic  2.24 us (2%)
  local copies, waits for them, and re-layouts  1.72 us (2%)
  between operations  1.52 us (2%)
    ppermute x25, waiting for transfers between devices, move(): lax.ppermute(value, 'pts', [(a, b) for a, b in pairs if b is not None])  38.4 us
    ppermute x25, starting transfers between devices, move(): lax.ppermute(value, 'pts', [(a, b) for a, b in pairs if b is not None])  24 us
    pallas_call x10, Pallas kernels, call(): pl.pallas_call(body, out_shape=kinds, in_specs=[smem()] * len(scalars) +...  22.3 us
  transfers between devices with their start and end apart: 25, of which 10 were waited for; matrix products, arithmetic and copies ran while one was open for 1% of the time, Pallas kernels for 25%

profile of v4, /device:TPU:7, one launch (start us, length us, event | category | flops | bytes accessed | tf_op | source)
XLA Modules:
  0.0 90.2 jit_solution(15176286372689726532)
XLA Ops:
  0.0 3.3 %collective-permute-start.5 = (bf16[512,512]{1,0:T(8,128)(2,1)}, bf16[512,512]{1,0:T(8,128)(2,1)S(1)}, u32[]{:S(2)}, u32[]{:S(2)}) collective-permute-start(bf16[512,512]{1,0:T(8,128)(2,1)} %refs_7_.3), channel_id=1, source_target_pairs={{2,6},{3,7},{4,0},{5,1},{6,10},{7,11},{8,4},{9,5},{10,14},{11,15},... | collective-permute-start | bytes 1572872 | tf_op jit(solution)/shard_map/ppermute | solution.py:267
  3.3 2.7 %shard_map.82 = (f32[1,128,512]{2,1,0:T(8,128)}, bf16[1,128,512]{2,1,0:T(8,128)(2,1)}, bf16[1,128,512]{2,1,0:T(8,128)(2,1)}, bf16[1,128,512]{2,1,0:T(8,128)(2,1)}) custom-call(bf16[512,512]{1,0:T(8,128)(2,1)} %refs_7_.3, bf16[512,512]{1,0:T(8,128)(2,1)} %proj.1), custom_call_target="tpu_custom_call" | custom-call | flops 1000 | bytes 1000 | tf_op jit(solution)/shard_map/pallas_call | solution.py:78
  6.0 1.0 %collective-permute-start = (bf16[1,128,512]{2,1,0:T(8,128)(2,1)}, bf16[1,128,512]{2,1,0:T(8,128)(2,1)S(1)}, u32[]{:S(2)}, u32[]{:S(2)}) collective-permute-start(bf16[1,128,512]{2,1,0:T(8,128)(2,1)} %get-tuple-element.43), channel_id=1, source_target_pairs={{0,1},{1,0},{2,3},{3,2},{4,5},{5,4},{6,7},{7,6},{8,9},{9,8},{10,11... | collective-permute-start | bytes 393224 | tf_op jit(solution)/shard_map/ppermute | solution.py:267
  7.0 1.7 %collective-permute-start.2 = (bf16[1,128,512]{2,1,0:T(8,128)(2,1)}, bf16[1,128,512]{2,1,0:T(8,128)(2,1)S(1)}, u32[]{:S(2)}, u32[]{:S(2)}) collective-permute-start(bf16[1,128,512]{2,1,0:T(8,128)(2,1)} %get-tuple-element.45), channel_id=1, source_target_pairs={{0,3},{1,2},{2,1},{3,0},{4,7},{5,6},{6,5},{7,4},{8,11},{9,10},{10,... | collective-permute-start | bytes 393224 | tf_op jit(solution)/shard_map/ppermute | solution.py:267
  8.7 3.6 %collective-permute-done.1.refs_1_ = bf16[1,128,512]{2,1,0:T(8,128)(2,1)S(1)} collective-permute-done((bf16[1,128,512]{2,1,0:T(8,128)(2,1)}, bf16[1,128,512]{2,1,0:T(8,128)(2,1)S(1)}, u32[]{:S(2)}, u32[]{:S(2)}) %collective-permute-start.1) | collective-permute-done | bytes 131104 | tf_op jit(solution)/shard_map/ppermute | solution.py:267
  12.3 3.3 %collective-permute-done.2.refs_2_ = bf16[1,128,512]{2,1,0:T(8,128)(2,1)S(1)} collective-permute-done((bf16[1,128,512]{2,1,0:T(8,128)(2,1)}, bf16[1,128,512]{2,1,0:T(8,128)(2,1)S(1)}, u32[]{:S(2)}, u32[]{:S(2)}) %collective-permute-start.2) | collective-permute-done | bytes 131104 | tf_op jit(solution)/shard_map/ppermute | solution.py:267
  15.6 0.9 %copy-done.2 = f32[1,128,512]{2,1,0:T(8,128)S(1)} copy-done((f32[1,128,512]{2,1,0:T(8,128)S(1)}, f32[1,128,512]{2,1,0:T(8,128)}, u32[]{:S(2)}) %copy-start.2) | copy-done | bytes 262168
  17.2 1.4 %collective-permute-start.4 = (bf16[128,1536]{1,0:T(8,128)(2,1)S(1)}, bf16[128,1536]{1,0:T(8,128)(2,1)}, u32[]{:S(2)}, u32[]{:S(2)}) collective-permute-start(bf16[128,1536]{1,0:T(8,128)(2,1)S(1)} %shard_map.83.refs_0_), channel_id=1, source_target_pairs={{0,8},{1,9},{2,10},{3,11},{4,12},{5,13},{6,14},{7,15},{8,16},{9,17... | collective-permute-start | bytes 1179656 | tf_op jit(solution)/shard_map/ppermute | solution.py:267
  18.6 0.8 collective-permute-start.6
  19.6 7.7 %collective-permute-done.3.refs_1_ = bf16[128,1536]{1,0:T(8,128)(2,1)S(1)} collective-permute-done((bf16[128,1536]{1,0:T(8,128)(2,1)S(1)}, bf16[128,1536]{1,0:T(8,128)(2,1)S(1)}, u32[]{:S(2)}, u32[]{:S(2)}) %collective-permute-start.3) | collective-permute-done | bytes 393248 | tf_op jit(solution)/shard_map/ppermute | solution.py:267
  27.3 2.1 %collective-permute-done.4.refs_2_ = bf16[128,1536]{1,0:T(8,128)(2,1)} collective-permute-done((bf16[128,1536]{1,0:T(8,128)(2,1)S(1)}, bf16[128,1536]{1,0:T(8,128)(2,1)}, u32[]{:S(2)}, u32[]{:S(2)}) %collective-permute-start.4) | collective-permute-done | bytes 393248 | tf_op jit(solution)/shard_map/ppermute | solution.py:267
  29.4 0.8 collective-permute-start.8
  30.3 1.0 %collective-permute-start.9 = (bf16[128,1536]{1,0:T(8,128)(2,1)S(1)}, bf16[128,1536]{1,0:T(8,128)(2,1)}, u32[]{:S(2)}, u32[]{:S(2)}) collective-permute-start(bf16[128,1536]{1,0:T(8,128)(2,1)S(1)} %shard_map.83.refs_0_), channel_id=1, source_target_pairs={{0,24},{1,25},{2,26},{3,27},{4,28},{5,29},{6,30},{7,31},{8,0},{9,1... | collective-permute-start | bytes 1179656 | tf_op jit(solution)/shard_map/ppermute | solution.py:267
  33.4 1.6 %collective-permute-start.11 = (s32[1,16]{1,0:T(1,128)S(1)}, s32[1,16]{1,0:T(1,128)S(1)}, u32[]{:S(2)}, u32[]{:S(2)}) collective-permute-start(s32[1,16]{1,0:T(1,128)S(1)} %bitcast.4), channel_id=1, source_target_pairs={{0,1},{1,0},{2,3},{3,2},{4,5},{5,4},{6,7},{7,6},{8,9},{9,8},{10,11... | collective-permute-start | bytes 200 | tf_op jit(solution)/shard_map/ppermute | solution.py:267
  35.0 0.8 collective-permute-done.11
  35.8 1.3 %collective-permute-start.12 = (s32[2,16]{1,0:T(2,128)S(1)}, s32[2,16]{1,0:T(2,128)S(1)}, u32[]{:S(2)}, u32[]{:S(2)}) collective-permute-start(s32[2,16]{1,0:T(2,128)S(1)} %pad_add_fusion.1), channel_id=1, source_target_pairs={{0,2},{1,3},{2,0},{3,1},{4,6},{5,7},{6,4},{7,5},{8,10},{9,11},{10,... | collective-permute-start | bytes 392 | tf_op jit(solution)/shard_map/ppermute | solution.py:267
  37.1 3.4 %collective-permute-done.12 = s32[2,16]{1,0:T(2,128)S(1)} collective-permute-done((s32[2,16]{1,0:T(2,128)S(1)}, s32[2,16]{1,0:T(2,128)S(1)}, u32[]{:S(2)}, u32[]{:S(2)}) %collective-permute-start.12) | collective-permute-done | bytes 160 | tf_op jit(solution)/shard_map/ppermute | solution.py:267
  40.6 0.7 collective-permute-start.16
  41.9 0.8 collective-permute-start.13
  42.7 1.3 %collective-permute-start.14 = (bf16[128,1536]{1,0:T(8,128)(2,1)S(1)}, bf16[128,1536]{1,0:T(8,128)(2,1)S(1)}, u32[]{:S(2)}, u32[]{:S(2)}) collective-permute-start(bf16[128,1536]{1,0:T(8,128)(2,1)S(1)} %collective-permute-done.8.refs_0_), channel_id=1, source_target_pairs={{0,8},{1,9},{2,10},{3,11},{4,12},{5,13},{6,14},{7,15},{8,16},{9,17... | collective-permute-start | bytes 1179656 | tf_op jit(solution)/shard_map/ppermute | solution.py:267
  44.2 1.0 %pad_maximum_fusion = bf16[512,512]{1,0:T(8,128)(2,1)S(1)} fusion(bf16[160,512]{1,0:T(8,128)(2,1)S(1)} %collective-permute-done.7, bf16[352,512]{1,0:T(8,128)(2,1)} %collective-permute-done.6), kind=kLoop, calls=%fused_computation.1 | loop fusion | flops 1048576 | bytes 1048576 | tf_op jit(solution)/shard_map/concatenate | solution.py:327
  45.9 3.0 %collective-permute-start.18 = (bf16[512,1024]{1,0:T(8,128)(2,1)S(1)}, bf16[512,1024]{1,0:T(8,128)(2,1)S(1)}, u32[]{:S(2)}, u32[]{:S(2)}) collective-permute-start(bf16[512,1024]{1,0:T(8,128)(2,1)S(1)} %collective-permute-done.10.refs_4_), channel_id=1, source_target_pairs={{0,4},{1,5},{4,8},{5,9},{6,2},{7,3},{8,12},{9,13},{10,6},{11,7},{1... | collective-permute-start | bytes 3145736 | tf_op jit(solution)/shard_map/ppermute | solution.py:267
  48.9 4.7 %shard_map.84 = (f32[512,512]{1,0:T(8,128)S(1)}, f32[512,512]{1,0:T(8,128)S(1)}) custom-call(s32[4,16]{1,0:T(4,128)S(1)} %pad_add_fusion.meta, bf16[128,1536]{1,0:T(8,128)(2,1)S(1)} %shard_map.83.refs_0_, bf16[128,1536]{1,0:T(8,128)(2,1)S(1)} %collective-permute-done.3.refs_1_, bf16[128,1536]{1,0:T(8,128)(2,1)} %collective-permute-done.4.refs_2_, ...), custom_call_target="tpu_custom_call" | custom-call | flops 1000 | bytes 1000 | tf_op jit(solution)/shard_map/pallas_call | solution.py:78
  53.6 5.4 %shard_map.85 = (f32[512,512]{1,0:T(8,128)S(1)}, f32[512,512]{1,0:T(8,128)S(1)}) custom-call(s32[4,16]{1,0:T(4,128)S(1)} %pad_add_fusion.meta, bf16[128,1536]{1,0:T(8,128)(2,1)S(1)} %shard_map.83.refs_0_, bf16[128,1536]{1,0:T(8,128)(2,1)S(1)} %collective-permute-done.3.refs_1_, bf16[128,1536]{1,0:T(8,128)(2,1)} %collective-permute-done.4.refs_2_, ...), custom_call_target="tpu_custom_call" | custom-call | flops 1000 | bytes 1000 | tf_op jit(solution)/shard_map/pallas_call | solution.py:78
  59.1 4.0 %collective-permute-done.14.refs_2_ = bf16[128,1536]{1,0:T(8,128)(2,1)S(1)} collective-permute-done((bf16[128,1536]{1,0:T(8,128)(2,1)S(1)}, bf16[128,1536]{1,0:T(8,128)(2,1)S(1)}, u32[]{:S(2)}, u32[]{:S(2)}) %collective-permute-start.14) | collective-permute-done | bytes 393248 | tf_op jit(solution)/shard_map/ppermute | solution.py:267
  63.1 2.2 %shard_map.90 = bf16[512,512]{1,0:T(8,128)(2,1)S(1)} custom-call(s32[4,16]{1,0:T(4,128)S(1)} %pad_add_fusion.meta, bf16[128,1536]{1,0:T(8,128)(2,1)S(1)} %collective-permute-done.8.refs_0_, bf16[128,1536]{1,0:T(8,128)(2,1)S(1)} %collective-permute-done.13.refs_1_, bf16[128,1536]{1,0:T(8,128)(2,1)S(1)} %collective-permute-done.14.refs_2_, ...), custom_call_target="tpu_custom_call" | custom-call | flops 1000 | bytes 1000 | tf_op jit(solution)/shard_map/pallas_call | solution.py:78
  65.3 0.8 collective-permute-start.23
  66.3 2.0 %shard_map.89.one = f32[512,512]{1,0:T(8,128)S(1)} custom-call(s32[4,16]{1,0:T(4,128)S(1)} %pad_add_fusion.meta, bf16[128,1536]{1,0:T(8,128)(2,1)S(1)} %collective-permute-done.8.refs_0_, bf16[128,1536]{1,0:T(8,128)(2,1)S(1)} %collective-permute-done.13.refs_1_, bf16[128,1536]{1,0:T(8,128)(2,1)S(1)} %collective-permute-done.14.refs_2_, ...), custom_call_target="tpu_custom_call" | custom-call | flops 1000 | bytes 1000 | tf_op jit(solution)/shard_map/pallas_call | solution.py:78
  68.4 1.8 %collective-permute-start.24 = (bf16[512,512]{1,0:T(8,128)(2,1)S(1)}, bf16[512,512]{1,0:T(8,128)(2,1)S(1)}, u32[]{:S(2)}, u32[]{:S(2)}) collective-permute-start(bf16[512,512]{1,0:T(8,128)(2,1)S(1)} %shard_map.91), channel_id=1, source_target_pairs={{0,2},{1,3},{2,0},{3,1},{4,6},{5,7},{6,4},{7,5},{8,10},{9,11},{10,... | collective-permute-start | bytes 1572872 | tf_op jit(solution)/shard_map/ppermute | solution.py:267
  70.2 3.4 %shard_map.86 = (f32[512,512]{1,0:T(8,128)S(1)}, f32[512,512]{1,0:T(8,128)S(1)}) custom-call(s32[4,16]{1,0:T(4,128)S(1)} %pad_add_fusion.meta, bf16[128,1536]{1,0:T(8,128)(2,1)S(1)} %collective-permute-done.8.refs_0_, bf16[128,1536]{1,0:T(8,128)(2,1)S(1)} %collective-permute-done.13.refs_1_, bf16[128,1536]{1,0:T(8,128)(2,1)S(1)} %collective-permute-done.14.refs_2_, ...), custom_call_target="tpu_custom_call" | custom-call | flops 1000 | bytes 1000 | tf_op jit(solution)/shard_map/pallas_call | solution.py:78
  73.6 12.6 %collective-permute-done.18.ypts = bf16[512,1024]{1,0:T(8,128)(2,1)S(1)} collective-permute-done((bf16[512,1024]{1,0:T(8,128)(2,1)S(1)}, bf16[512,1024]{1,0:T(8,128)(2,1)S(1)}, u32[]{:S(2)}, u32[]{:S(2)}) %collective-permute-start.18) | collective-permute-done | bytes 1048608 | tf_op jit(solution)/shard_map/ppermute | solution.py:267
  89.0 1.2 %convert_add_fusion = f32[512,512]{1,0:T(8,128)} fusion(bf16[512,512]{1,0:T(8,128)(2,1)S(1)} %collective-permute-done.24, f32[512,512]{1,0:T(8,128)S(1)} %shard_map.87, bf16[256,512]{1,0:T(8,128)(2,1)S(1)} %collective-permute-done.22, bf16[256,512]{1,0:T(8,128)(2,1)S(1)} %collective-permute-done.21), kind=kLoop, calls=%fused_computation | loop fusion | flops 1835008 | bytes 3145728 | tf_op jit(solution)/shard_map/add | solution.py:359
  (48 shorter events, 5.9 us)
Async XLA Ops:
  0.0 15.6 %copy-start = (bf16[512,1024]{1,0:T(8,128)(2,1)S(1)}, bf16[512,1024]{1,0:T(8,128)(2,1)}, u32[]{:S(2)}) copy-start(bf16[512,1024]{1,0:T(8,128)(2,1)} %xpts.1) | copy-start | bytes 3145732
  0.0 18.6 %collective-permute-start.5 = (bf16[512,512]{1,0:T(8,128)(2,1)}, bf16[512,512]{1,0:T(8,128)(2,1)S(1)}, u32[]{:S(2)}, u32[]{:S(2)}) collective-permute-start(bf16[512,512]{1,0:T(8,128)(2,1)} %refs_7_.3), channel_id=1, source_target_pairs={{2,6},{3,7},{4,0},{5,1},{6,10},{7,11},{8,4},{9,5},{10,14},{11,15},... | collective-permute-start | bytes 1572872 | tf_op jit(solution)/shard_map/ppermute | solution.py:267
  6.0 2.7 %collective-permute-start = (bf16[1,128,512]{2,1,0:T(8,128)(2,1)}, bf16[1,128,512]{2,1,0:T(8,128)(2,1)S(1)}, u32[]{:S(2)}, u32[]{:S(2)}) collective-permute-start(bf16[1,128,512]{2,1,0:T(8,128)(2,1)} %get-tuple-element.43), channel_id=1, source_target_pairs={{0,1},{1,0},{2,3},{3,2},{4,5},{5,4},{6,7},{7,6},{8,9},{9,8},{10,11... | collective-permute-start | bytes 393224 | tf_op jit(solution)/shard_map/ppermute | solution.py:267
  7.0 5.3 %collective-permute-start.1 = (bf16[1,128,512]{2,1,0:T(8,128)(2,1)}, bf16[1,128,512]{2,1,0:T(8,128)(2,1)S(1)}, u32[]{:S(2)}, u32[]{:S(2)}) collective-permute-start(bf16[1,128,512]{2,1,0:T(8,128)(2,1)} %get-tuple-element.44), channel_id=1, source_target_pairs={{0,2},{1,3},{2,0},{3,1},{4,6},{5,7},{6,4},{7,5},{8,10},{9,11},{10,... | collective-permute-start | bytes 393224 | tf_op jit(solution)/shard_map/ppermute | solution.py:267
  7.0 8.6 %copy-start.3 = (s32[1,128]{1,0:T(1,128)S(1)}, s32[1,128]{1,0:T(1,128)}, u32[]{:S(2)}) copy-start(s32[1,128]{1,0:T(1,128)} %idx.1) | copy-start | bytes 1540
  7.0 8.5 %collective-permute-start.2 = (bf16[1,128,512]{2,1,0:T(8,128)(2,1)}, bf16[1,128,512]{2,1,0:T(8,128)(2,1)S(1)}, u32[]{:S(2)}, u32[]{:S(2)}) collective-permute-start(bf16[1,128,512]{2,1,0:T(8,128)(2,1)} %get-tuple-element.45), channel_id=1, source_target_pairs={{0,3},{1,2},{2,1},{3,0},{4,7},{5,6},{6,5},{7,4},{8,11},{9,10},{10,... | collective-permute-start | bytes 393224 | tf_op jit(solution)/shard_map/ppermute | solution.py:267
  15.6 25.7 %collective-permute-start.10 = (bf16[512,1024]{1,0:T(8,128)(2,1)S(1)}, bf16[512,1024]{1,0:T(8,128)(2,1)S(1)}, u32[]{:S(2)}, u32[]{:S(2)}) collective-permute-start(bf16[512,1024]{1,0:T(8,128)(2,1)S(1)} %copy-done), channel_id=1, source_target_pairs={{0,2},{1,3},{2,0},{3,1},{4,6},{5,7},{6,4},{7,5},{8,10},{9,11},{10,... | collective-permute-start | bytes 3145736 | tf_op jit(solution)/shard_map/ppermute | solution.py:267
  15.6 1.0 %copy-start.2 = (f32[1,128,512]{2,1,0:T(8,128)S(1)}, f32[1,128,512]{2,1,0:T(8,128)}, u32[]{:S(2)}) copy-start(f32[1,128,512]{2,1,0:T(8,128)} %get-tuple-element.42.keep) | copy-start | bytes 786436
  16.9 10.4 %collective-permute-start.3 = (bf16[128,1536]{1,0:T(8,128)(2,1)S(1)}, bf16[128,1536]{1,0:T(8,128)(2,1)S(1)}, u32[]{:S(2)}, u32[]{:S(2)}) collective-permute-start(bf16[128,1536]{1,0:T(8,128)(2,1)S(1)} %shard_map.83.refs_0_), channel_id=1, source_target_pairs={{0,4},{1,5},{2,6},{3,7},{4,0},{5,1},{6,2},{7,3},{8,12},{9,13},{10,... | collective-permute-start | bytes 1179656 | tf_op jit(solution)/shard_map/ppermute | solution.py:267
  17.2 12.3 %collective-permute-start.4 = (bf16[128,1536]{1,0:T(8,128)(2,1)S(1)}, bf16[128,1536]{1,0:T(8,128)(2,1)}, u32[]{:S(2)}, u32[]{:S(2)}) collective-permute-start(bf16[128,1536]{1,0:T(8,128)(2,1)S(1)} %shard_map.83.refs_0_), channel_id=1, source_target_pairs={{0,8},{1,9},{2,10},{3,11},{4,12},{5,13},{6,14},{7,15},{8,16},{9,17... | collective-permute-start | bytes 1179656 | tf_op jit(solution)/shard_map/ppermute | solution.py:267
  18.6 10.8 %collective-permute-start.6 = (bf16[352,512]{1,0:T(8,128)(2,1)S(1)}, bf16[352,512]{1,0:T(8,128)(2,1)}, u32[]{:S(2)}, u32[]{:S(2)}) collective-permute-start(bf16[352,512]{1,0:T(8,128)(2,1)S(1)} %split.8), channel_id=1, source_target_pairs={{0,1},{1,0},{2,3},{3,2},{4,5},{5,4},{6,7},{7,6},{8,9},{9,8},{10,11... | collective-permute-start | bytes 1081352 | tf_op jit(solution)/shard_map/ppermute | solution.py:267
  19.5 9.9 %collective-permute-start.7 = (bf16[160,512]{1,0:T(8,128)(2,1)S(1)}, bf16[160,512]{1,0:T(8,128)(2,1)S(1)}, u32[]{:S(2)}, u32[]{:S(2)}) collective-permute-start(bf16[160,512]{1,0:T(8,128)(2,1)S(1)} %split.9), channel_id=1, source_target_pairs={{0,1},{1,0},{2,3},{3,2},{4,5},{5,4},{6,7},{7,6},{8,9},{9,8},{10,11... | collective-permute-start | bytes 491528 | tf_op jit(solution)/shard_map/ppermute | solution.py:267
  29.4 11.9 %collective-permute-start.8 = (bf16[128,1536]{1,0:T(8,128)(2,1)}, bf16[128,1536]{1,0:T(8,128)(2,1)S(1)}, u32[]{:S(2)}, u32[]{:S(2)}) collective-permute-start(bf16[128,1536]{1,0:T(8,128)(2,1)} %collective-permute-done.4.refs_2_), channel_id=1, source_target_pairs={{0,4},{1,5},{2,6},{3,7},{4,0},{5,1},{6,2},{7,3},{8,12},{9,13},{10,... | collective-permute-start | bytes 1179656 | tf_op jit(solution)/shard_map/ppermute | solution.py:267
  30.3 11.0 %collective-permute-start.9 = (bf16[128,1536]{1,0:T(8,128)(2,1)S(1)}, bf16[128,1536]{1,0:T(8,128)(2,1)}, u32[]{:S(2)}, u32[]{:S(2)}) collective-permute-start(bf16[128,1536]{1,0:T(8,128)(2,1)S(1)} %shard_map.83.refs_0_), channel_id=1, source_target_pairs={{0,24},{1,25},{2,26},{3,27},{4,28},{5,29},{6,30},{7,31},{8,0},{9,1... | collective-permute-start | bytes 1179656 | tf_op jit(solution)/shard_map/ppermute | solution.py:267
  32.6 0.7 copy-start.4
  32.6 0.7 copy-start.5
  33.4 2.4 %collective-permute-start.11 = (s32[1,16]{1,0:T(1,128)S(1)}, s32[1,16]{1,0:T(1,128)S(1)}, u32[]{:S(2)}, u32[]{:S(2)}) collective-permute-start(s32[1,16]{1,0:T(1,128)S(1)} %bitcast.4), channel_id=1, source_target_pairs={{0,1},{1,0},{2,3},{3,2},{4,5},{5,4},{6,7},{7,6},{8,9},{9,8},{10,11... | collective-permute-start | bytes 200 | tf_op jit(solution)/shard_map/ppermute | solution.py:267
  35.8 4.8 %collective-permute-start.12 = (s32[2,16]{1,0:T(2,128)S(1)}, s32[2,16]{1,0:T(2,128)S(1)}, u32[]{:S(2)}, u32[]{:S(2)}) collective-permute-start(s32[2,16]{1,0:T(2,128)S(1)} %pad_add_fusion.1), channel_id=1, source_target_pairs={{0,2},{1,3},{2,0},{3,1},{4,6},{5,7},{6,4},{7,5},{8,10},{9,11},{10,... | collective-permute-start | bytes 392 | tf_op jit(solution)/shard_map/ppermute | solution.py:267
  40.6 8.3 %copy-start.1 = (bf16[512,512]{1,0:T(8,128)(2,1)S(1)}, bf16[512,512]{1,0:T(8,128)(2,1)}, u32[]{:S(2)}) copy-start(bf16[512,512]{1,0:T(8,128)(2,1)} %refs_7_.3) | copy-start | bytes 1572868
  40.6 4.7 %collective-permute-start.16 = (bf16[512,1024]{1,0:T(8,128)(2,1)S(1)}, bf16[512,1024]{1,0:T(8,128)(2,1)S(1)}, u32[]{:S(2)}, u32[]{:S(2)}) collective-permute-start(bf16[512,1024]{1,0:T(8,128)(2,1)S(1)} %copy-done), channel_id=1, source_target_pairs={{0,1},{1,0},{2,3},{3,2},{4,5},{5,4},{6,7},{7,6},{8,9},{9,8},{10,11... | collective-permute-start | bytes 3145736 | tf_op jit(solution)/shard_map/ppermute | solution.py:267
  41.3 4.6 %collective-permute-start.17 = (bf16[512,1024]{1,0:T(8,128)(2,1)S(1)}, bf16[512,1024]{1,0:T(8,128)(2,1)S(1)}, u32[]{:S(2)}, u32[]{:S(2)}) collective-permute-start(bf16[512,1024]{1,0:T(8,128)(2,1)S(1)} %collective-permute-done.10.refs_4_), channel_id=1, source_target_pairs={{0,1},{1,0},{2,3},{3,2},{4,5},{5,4},{6,7},{7,6},{8,9},{9,8},{10,11... | collective-permute-start | bytes 3145736 | tf_op jit(solution)/shard_map/ppermute | solution.py:267
  41.9 17.1 %collective-permute-start.13 = (bf16[128,1536]{1,0:T(8,128)(2,1)}, bf16[128,1536]{1,0:T(8,128)(2,1)S(1)}, u32[]{:S(2)}, u32[]{:S(2)}) collective-permute-start(bf16[128,1536]{1,0:T(8,128)(2,1)} %collective-permute-done.4.refs_2_), channel_id=1, source_target_pairs={{0,8},{1,9},{2,10},{3,11},{4,12},{5,13},{6,14},{7,15},{8,16},{9,17... | collective-permute-start | bytes 1179656 | tf_op jit(solution)/shard_map/ppermute | solution.py:267
  42.7 20.4 %collective-permute-start.14 = (bf16[128,1536]{1,0:T(8,128)(2,1)S(1)}, bf16[128,1536]{1,0:T(8,128)(2,1)S(1)}, u32[]{:S(2)}, u32[]{:S(2)}) collective-permute-start(bf16[128,1536]{1,0:T(8,128)(2,1)S(1)} %collective-permute-done.8.refs_0_), channel_id=1, source_target_pairs={{0,8},{1,9},{2,10},{3,11},{4,12},{5,13},{6,14},{7,15},{8,16},{9,17... | collective-permute-start | bytes 1179656 | tf_op jit(solution)/shard_map/ppermute | solution.py:267
  44.0 19.1 %collective-permute-start.15 = (bf16[128,1536]{1,0:T(8,128)(2,1)}, bf16[128,1536]{1,0:T(8,128)(2,1)S(1)}, u32[]{:S(2)}, u32[]{:S(2)}) collective-permute-start(bf16[128,1536]{1,0:T(8,128)(2,1)} %collective-permute-done.9.refs_3_), channel_id=1, source_target_pairs={{0,4},{1,5},{2,6},{3,7},{4,0},{5,1},{6,2},{7,3},{8,12},{9,13},{10,... | collective-permute-start | bytes 1179656 | tf_op jit(solution)/shard_map/ppermute | solution.py:267
  45.3 20.9 %collective-permute-start.19 = (bf16[512,512]{1,0:T(8,128)(2,1)S(1)}, bf16[512,512]{1,0:T(8,128)(2,1)S(1)}, u32[]{:S(2)}, u32[]{:S(2)}) collective-permute-start(bf16[512,512]{1,0:T(8,128)(2,1)S(1)} %pad_maximum_fusion), channel_id=1, source_target_pairs={{0,2},{1,3},{2,0},{3,1},{4,6},{5,7},{6,4},{7,5},{8,10},{9,11},{10,... | collective-permute-start | bytes 1572872 | tf_op jit(solution)/shard_map/ppermute | solution.py:267
  45.9 40.3 %collective-permute-start.18 = (bf16[512,1024]{1,0:T(8,128)(2,1)S(1)}, bf16[512,1024]{1,0:T(8,128)(2,1)S(1)}, u32[]{:S(2)}, u32[]{:S(2)}) collective-permute-start(bf16[512,1024]{1,0:T(8,128)(2,1)S(1)} %collective-permute-done.10.refs_4_), channel_id=1, source_target_pairs={{0,4},{1,5},{4,8},{5,9},{6,2},{7,3},{8,12},{9,13},{10,6},{11,7},{1... | collective-permute-start | bytes 3145736 | tf_op jit(solution)/shard_map/ppermute | solution.py:267
  65.3 3.0 %collective-permute-start.23 = (bf16[512,512]{1,0:T(8,128)(2,1)S(1)}, bf16[512,512]{1,0:T(8,128)(2,1)S(1)}, u32[]{:S(2)}, u32[]{:S(2)}) collective-permute-start(bf16[512,512]{1,0:T(8,128)(2,1)S(1)} %shard_map.90), channel_id=1, source_target_pairs={{0,1},{1,0},{2,3},{3,2},{4,5},{5,4},{6,7},{7,6},{8,9},{9,8},{10,11... | collective-permute-start | bytes 1572872 | tf_op jit(solution)/shard_map/ppermute | solution.py:267
  66.2 7.4 %collective-permute-start.20 = (bf16[512,512]{1,0:T(8,128)(2,1)S(1)}, bf16[512,512]{1,0:T(8,128)(2,1)S(1)}, u32[]{:S(2)}, u32[]{:S(2)}) collective-permute-start(bf16[512,512]{1,0:T(8,128)(2,1)S(1)} %collective-permute-done.19), channel_id=1, source_target_pairs={{0,1},{1,0},{2,3},{3,2},{4,5},{5,4},{6,7},{7,6},{8,9},{9,8},{10,11... | collective-permute-start | bytes 1572872 | tf_op jit(solution)/shard_map/ppermute | solution.py:267
  68.4 20.5 %collective-permute-start.24 = (bf16[512,512]{1,0:T(8,128)(2,1)S(1)}, bf16[512,512]{1,0:T(8,128)(2,1)S(1)}, u32[]{:S(2)}, u32[]{:S(2)}) collective-permute-start(bf16[512,512]{1,0:T(8,128)(2,1)S(1)} %shard_map.91), channel_id=1, source_target_pairs={{0,2},{1,3},{2,0},{3,1},{4,6},{5,7},{6,4},{7,5},{8,10},{9,11},{10,... | collective-permute-start | bytes 1572872 | tf_op jit(solution)/shard_map/ppermute | solution.py:267
  86.9 1.7 %collective-permute-start.22 = (bf16[256,512]{1,0:T(8,128)(2,1)S(1)}, bf16[256,512]{1,0:T(8,128)(2,1)S(1)}, u32[]{:S(2)}, u32[]{:S(2)}) collective-permute-start(bf16[256,512]{1,0:T(8,128)(2,1)S(1)} %get-tuple-element.76), channel_id=1, source_target_pairs={{0,1},{1,0},{2,3},{3,2},{4,5},{5,4},{6,7},{7,6},{8,9},{9,8},{10,11... | collective-permute-start | bytes 786440 | tf_op jit(solution)/shard_map/ppermute | solution.py:267
  87.4 1.5 %collective-permute-start.21 = (bf16[256,512]{1,0:T(8,128)(2,1)S(1)}, bf16[256,512]{1,0:T(8,128)(2,1)S(1)}, u32[]{:S(2)}, u32[]{:S(2)}) collective-permute-start(bf16[256,512]{1,0:T(8,128)(2,1)S(1)} %get-tuple-element.75), channel_id=1, source_target_pairs={{0,1},{1,0},{2,3},{3,2},{4,5},{5,4},{6,7},{7,6},{8,9},{9,8},{10,11... | collective-permute-start | bytes 786440 | tf_op jit(solution)/shard_map/ppermute | solution.py:267

commit v5 on v4

--- a/solution.py
+++ b/solution.py
@@ -21,7 +21,6 @@
 FAR_COUNT = FAR_LIST + FAR
 LEAF = FAR_COUNT + 1
 META = 16
-CUTS = 4
 
 
 def vmem():
@@ -32,8 +31,8 @@
     return pl.BlockSpec(memory_space=pltpu.SMEM)
 
 
-def params(limit=24):
-    return pltpu.CompilerParams(vmem_limit_bytes=limit * MIB)
+def params():
+    return pltpu.CompilerParams(vmem_limit_bytes=16 * MIB)
 
 
 def norm_column(points, scale):
@@ -74,35 +73,22 @@
     return jnp.dot(kern.astype(BF16), wts, preferred_element_type=F32)
 
 
-def call(body, kinds, scalars, arrays, scratch=(), outside=(), limit=24):
+def call(body, kinds, scalars, arrays):
     return pl.pallas_call(
         body,
         out_shape=kinds,
         in_specs=[smem()] * len(scalars)
-        + [vmem()] * len(arrays)
-        + [pl.BlockSpec(memory_space=pltpu.HBM)] * len(outside),
+        + [vmem()] * len(arrays),
         out_specs=jax.tree.map(lambda _: vmem(), kinds),
-        scratch_shapes=scratch,
-        compiler_params=params(limit),
+        compiler_params=params(),
         cost_estimate=pl.CostEstimate(flops=1000, bytes_accessed=1000, transcendentals=0),
-    )(*scalars, *arrays, *outside)
-
-
-def project_body(wts, proj, keep, *outs):
-    *gives, wts_here, proj_here, sems = outs
-    copies = []
-    for source, target in ((wts, wts_here), (proj, proj_here)):
-        rows = source.shape[0] // CUTS
-        for cut in range(CUTS):
-            part = pl.ds(cut * rows, rows)
-            copies.append(pltpu.make_async_copy(source.at[part], target.at[part], sems.at[len(copies)]))
-    for copy in copies:
-        copy.start()
-    for copy in copies:
-        copy.wait()
+    )(*scalars, *arrays)
+
+
+def project_body(wts, proj, keep, *gives):
     leaf = lax.axis_index("pts")
     groups, count, wcols = keep.shape
-    whole = jnp.dot(proj_here[...], wts_here[...], preferred_element_type=F32)
+    whole = jnp.dot(proj[...], wts[...], preferred_element_type=F32)
     whole = whole.reshape(groups, QUAD, count, wcols)
     for turn in range(QUAD):
         block = whole[:, QUAD - 1]
@@ -117,12 +103,7 @@
 def project(group, wts, proj):
     shape = (group // QUAD, proj.shape[0] // group, wts.shape[1])
     kinds = (jax.ShapeDtypeStruct(shape, F32),) + (jax.ShapeDtypeStruct(shape, BF16),) * (QUAD - 1)
-    scratch = [
-        pltpu.VMEM(wts.shape, BF16),
-        pltpu.VMEM(proj.shape, BF16),
-        pltpu.SemaphoreType.DMA((2 * CUTS,)),
-    ]
-    return call(project_body, kinds, (), (), scratch, (wts, proj), 54)
+    return call(project_body, kinds, (), (wts, proj))
 
 
 def pack_body(idx, pts, keep, *refs):

time: 90.8 us -> 90.2 us (level)
  Pallas kernels: 22.3 us -> 20.2 us
  local copies, waits for them, and re-layouts: 1.72 us -> 2.86 us
    pallas_call x10, Pallas kernels: 22.3 us -> 20.2 us  [call(): pl.pallas_call(body, out_shape=kinds, in_specs=[smem()] * len(scalars) +...]
    unnamed x12 -> x14, local copies, waits for them, and re-layouts: 1.61 us -> 2.75 us
  transfers between devices with their start and end apart: 25 -> 25, of which waited for: 10 -> 8; matrix products, arithmetic and copies ran while one was open for 1% -> 1% of each run, Pallas kernels for 25% -> 22%
where the time goes in v5:
time: 90.2 us; the launch traced here: 90.4 us
  waiting for transfers between devices  38.8 us (43%)
  starting transfers between devices  24.8 us (27%)
  Pallas kernels  20.2 us (22%)
  local copies, waits for them, and re-layouts  2.86 us (3%)
  other arithmetic  2.22 us (2%)
  between operations  1.54 us (2%)
    ppermute x25, waiting for transfers between devices, move(): lax.ppermute(value, 'pts', [(a, b) for a, b in pairs if b is not None])  38.8 us
    ppermute x25, starting transfers between devices, move(): lax.ppermute(value, 'pts', [(a, b) for a, b in pairs if b is not None])  24.8 us
    pallas_call x10, Pallas kernels, call(): pl.pallas_call(body, out_shape=kinds, in_specs=[smem()] * len(scalars) +...  20.2 us
    unnamed x14, local copies, waits for them, and re-layouts  2.75 us
  transfers between devices with their start and end apart: 25, of which 8 were waited for; matrix products, arithmetic and copies ran while one was open for 1% of the time, Pallas kernels for 22%

profile of v5, /device:TPU:7, one launch (start us, length us, event | category | flops | bytes accessed | tf_op | source)
XLA Modules:
  0.0 90.4 jit_solution(4439601866464438309)
XLA Ops:
  0.0 3.3 %collective-permute-start.5 = (bf16[512,512]{1,0:T(8,128)(2,1)}, bf16[512,512]{1,0:T(8,128)(2,1)S(1)}, u32[]{:S(2)}, u32[]{:S(2)}) collective-permute-start(bf16[512,512]{1,0:T(8,128)(2,1)} %refs_7_.3), channel_id=1, source_target_pairs={{2,6},{3,7},{4,0},{5,1},{6,10},{7,11},{8,4},{9,5},{10,14},{11,15},... | collective-permute-start | bytes 1572872 | tf_op jit(solution)/shard_map/ppermute | solution.py:248
  3.3 1.0 %copy-done.1 = bf16[512,512]{1,0:T(8,128)(2,1)S(1)} copy-done((bf16[512,512]{1,0:T(8,128)(2,1)S(1)}, bf16[512,512]{1,0:T(8,128)(2,1)}, u32[]{:S(2)}) %copy-start.1) | copy-done | bytes 524312
  4.3 1.0 %copy-done.3 = bf16[512,512]{1,0:T(8,128)(2,1)S(1)} copy-done((bf16[512,512]{1,0:T(8,128)(2,1)S(1)}, bf16[512,512]{1,0:T(8,128)(2,1)}, u32[]{:S(2)}) %copy-start.3) | copy-done | bytes 524312
  5.9 1.0 %collective-permute-start = (bf16[1,128,512]{2,1,0:T(8,128)(2,1)S(1)}, bf16[1,128,512]{2,1,0:T(8,128)(2,1)S(1)}, u32[]{:S(2)}, u32[]{:S(2)}) collective-permute-start(bf16[1,128,512]{2,1,0:T(8,128)(2,1)S(1)} %get-tuple-element.43), channel_id=1, source_target_pairs={{0,1},{1,0},{2,3},{3,2},{4,5},{5,4},{6,7},{7,6},{8,9},{9,8},{10,11... | collective-permute-start | bytes 393224 | tf_op jit(solution)/shard_map/ppermute | solution.py:248
  6.9 1.7 %collective-permute-start.2 = (bf16[1,128,512]{2,1,0:T(8,128)(2,1)S(1)}, bf16[1,128,512]{2,1,0:T(8,128)(2,1)S(1)}, u32[]{:S(2)}, u32[]{:S(2)}) collective-permute-start(bf16[1,128,512]{2,1,0:T(8,128)(2,1)S(1)} %get-tuple-element.45), channel_id=1, source_target_pairs={{0,3},{1,2},{2,1},{3,0},{4,7},{5,6},{6,5},{7,4},{8,11},{9,10},{10,... | collective-permute-start | bytes 393224 | tf_op jit(solution)/shard_map/ppermute | solution.py:248
  8.6 3.4 %collective-permute-done.1.refs_1_ = bf16[1,128,512]{2,1,0:T(8,128)(2,1)S(1)} collective-permute-done((bf16[1,128,512]{2,1,0:T(8,128)(2,1)S(1)}, bf16[1,128,512]{2,1,0:T(8,128)(2,1)S(1)}, u32[]{:S(2)}, u32[]{:S(2)}) %collective-permute-start.1) | collective-permute-done | bytes 131104 | tf_op jit(solution)/shard_map/ppermute | solution.py:248
  12.0 3.3 %collective-permute-done.2.refs_2_ = bf16[1,128,512]{2,1,0:T(8,128)(2,1)S(1)} collective-permute-done((bf16[1,128,512]{2,1,0:T(8,128)(2,1)S(1)}, bf16[1,128,512]{2,1,0:T(8,128)(2,1)S(1)}, u32[]{:S(2)}, u32[]{:S(2)}) %collective-permute-start.2) | collective-permute-done | bytes 131104 | tf_op jit(solution)/shard_map/ppermute | solution.py:248
  15.9 1.4 %collective-permute-start.4 = (bf16[128,1536]{1,0:T(8,128)(2,1)S(1)}, bf16[128,1536]{1,0:T(8,128)(2,1)}, u32[]{:S(2)}, u32[]{:S(2)}) collective-permute-start(bf16[128,1536]{1,0:T(8,128)(2,1)S(1)} %shard_map.83.refs_0_), channel_id=1, source_target_pairs={{0,8},{1,9},{2,10},{3,11},{4,12},{5,13},{6,14},{7,15},{8,16},{9,17... | collective-permute-start | bytes 1179656 | tf_op jit(solution)/shard_map/ppermute | solution.py:248
  17.4 0.8 collective-permute-start.6
  18.3 7.8 %collective-permute-done.3.refs_1_ = bf16[128,1536]{1,0:T(8,128)(2,1)S(1)} collective-permute-done((bf16[128,1536]{1,0:T(8,128)(2,1)S(1)}, bf16[128,1536]{1,0:T(8,128)(2,1)S(1)}, u32[]{:S(2)}, u32[]{:S(2)}) %collective-permute-start.3) | collective-permute-done | bytes 393248 | tf_op jit(solution)/shard_map/ppermute | solution.py:248
  26.1 2.1 %collective-permute-done.4.refs_2_ = bf16[128,1536]{1,0:T(8,128)(2,1)} collective-permute-done((bf16[128,1536]{1,0:T(8,128)(2,1)S(1)}, bf16[128,1536]{1,0:T(8,128)(2,1)}, u32[]{:S(2)}, u32[]{:S(2)}) %collective-permute-start.4) | collective-permute-done | bytes 393248 | tf_op jit(solution)/shard_map/ppermute | solution.py:248
  28.2 0.9 collective-permute-start.8
  29.0 1.0 %collective-permute-start.9 = (bf16[128,1536]{1,0:T(8,128)(2,1)S(1)}, bf16[128,1536]{1,0:T(8,128)(2,1)}, u32[]{:S(2)}, u32[]{:S(2)}) collective-permute-start(bf16[128,1536]{1,0:T(8,128)(2,1)S(1)} %shard_map.83.refs_0_), channel_id=1, source_target_pairs={{0,24},{1,25},{2,26},{3,27},{4,28},{5,29},{6,30},{7,31},{8,0},{9,1... | collective-permute-start | bytes 1179656 | tf_op jit(solution)/shard_map/ppermute | solution.py:248
  32.1 1.6 %collective-permute-start.11 = (s32[1,16]{1,0:T(1,128)S(1)}, s32[1,16]{1,0:T(1,128)S(1)}, u32[]{:S(2)}, u32[]{:S(2)}) collective-permute-start(s32[1,16]{1,0:T(1,128)S(1)} %bitcast.4), channel_id=1, source_target_pairs={{0,1},{1,0},{2,3},{3,2},{4,5},{5,4},{6,7},{7,6},{8,9},{9,8},{10,11... | collective-permute-start | bytes 200 | tf_op jit(solution)/shard_map/ppermute | solution.py:248
  34.6 1.3 %collective-permute-start.12 = (s32[2,16]{1,0:T(2,128)S(1)}, s32[2,16]{1,0:T(2,128)S(1)}, u32[]{:S(2)}, u32[]{:S(2)}) collective-permute-start(s32[2,16]{1,0:T(2,128)S(1)} %pad_add_fusion.1), channel_id=1, source_target_pairs={{0,2},{1,3},{2,0},{3,1},{4,6},{5,7},{6,4},{7,5},{8,10},{9,11},{10,... | collective-permute-start | bytes 392 | tf_op jit(solution)/shard_map/ppermute | solution.py:248
  35.9 4.4 %collective-permute-done.12 = s32[2,16]{1,0:T(2,128)S(1)} collective-permute-done((s32[2,16]{1,0:T(2,128)S(1)}, s32[2,16]{1,0:T(2,128)S(1)}, u32[]{:S(2)}, u32[]{:S(2)}) %collective-permute-start.12) | collective-permute-done | bytes 160 | tf_op jit(solution)/shard_map/ppermute | solution.py:248
  41.1 1.3 %collective-permute-start.13 = (bf16[128,1536]{1,0:T(8,128)(2,1)}, bf16[128,1536]{1,0:T(8,128)(2,1)S(1)}, u32[]{:S(2)}, u32[]{:S(2)}) collective-permute-start(bf16[128,1536]{1,0:T(8,128)(2,1)} %collective-permute-done.4.refs_2_), channel_id=1, source_target_pairs={{0,8},{1,9},{2,10},{3,11},{4,12},{5,13},{6,14},{7,15},{8,16},{9,17... | collective-permute-start | bytes 1179656 | tf_op jit(solution)/shard_map/ppermute | solution.py:248
  42.4 1.3 %collective-permute-start.14 = (bf16[128,1536]{1,0:T(8,128)(2,1)S(1)}, bf16[128,1536]{1,0:T(8,128)(2,1)S(1)}, u32[]{:S(2)}, u32[]{:S(2)}) collective-permute-start(bf16[128,1536]{1,0:T(8,128)(2,1)S(1)} %collective-permute-done.8.refs_0_), channel_id=1, source_target_pairs={{0,8},{1,9},{2,10},{3,11},{4,12},{5,13},{6,14},{7,15},{8,16},{9,17... | collective-permute-start | bytes 1179656 | tf_op jit(solution)/shard_map/ppermute | solution.py:248
  44.0 1.0 %pad_maximum_fusion = bf16[512,512]{1,0:T(8,128)(2,1)S(1)} fusion(bf16[160,512]{1,0:T(8,128)(2,1)S(1)} %collective-permute-done.7, bf16[352,512]{1,0:T(8,128)(2,1)} %collective-permute-done.6), kind=kLoop, calls=%fused_computation.1 | loop fusion | flops 1048576 | bytes 1048576 | tf_op jit(solution)/shard_map/concatenate | solution.py:308
  45.2 3.0 %collective-permute-start.18 = (bf16[512,1024]{1,0:T(8,128)(2,1)S(1)}, bf16[512,1024]{1,0:T(8,128)(2,1)S(1)}, u32[]{:S(2)}, u32[]{:S(2)}) collective-permute-start(bf16[512,1024]{1,0:T(8,128)(2,1)S(1)} %collective-permute-done.10.refs_4_), channel_id=1, source_target_pairs={{0,4},{1,5},{4,8},{5,9},{6,2},{7,3},{8,12},{9,13},{10,6},{11,7},{1... | collective-permute-start | bytes 3145736 | tf_op jit(solution)/shard_map/ppermute | solution.py:248
  48.2 5.8 %shard_map.84 = (f32[512,512]{1,0:T(8,128)S(1)}, f32[512,512]{1,0:T(8,128)S(1)}) custom-call(s32[4,16]{1,0:T(4,128)S(1)} %pad_add_fusion.meta, bf16[128,1536]{1,0:T(8,128)(2,1)S(1)} %shard_map.83.refs_0_, bf16[128,1536]{1,0:T(8,128)(2,1)S(1)} %collective-permute-done.3.refs_1_, bf16[128,1536]{1,0:T(8,128)(2,1)} %collective-permute-done.4.refs_2_, ...), custom_call_target="tpu_custom_call" | custom-call | flops 1000 | bytes 1000 | tf_op jit(solution)/shard_map/pallas_call | solution.py:77
  54.0 3.4 %shard_map.85 = (f32[512,512]{1,0:T(8,128)S(1)}, f32[512,512]{1,0:T(8,128)S(1)}) custom-call(s32[4,16]{1,0:T(4,128)S(1)} %pad_add_fusion.meta, bf16[128,1536]{1,0:T(8,128)(2,1)S(1)} %shard_map.83.refs_0_, bf16[128,1536]{1,0:T(8,128)(2,1)S(1)} %collective-permute-done.3.refs_1_, bf16[128,1536]{1,0:T(8,128)(2,1)} %collective-permute-done.4.refs_2_, ...), custom_call_target="tpu_custom_call" | custom-call | flops 1000 | bytes 1000 | tf_op jit(solution)/shard_map/pallas_call | solution.py:77
  57.4 4.4 %collective-permute-done.14.refs_2_ = bf16[128,1536]{1,0:T(8,128)(2,1)S(1)} collective-permute-done((bf16[128,1536]{1,0:T(8,128)(2,1)S(1)}, bf16[128,1536]{1,0:T(8,128)(2,1)S(1)}, u32[]{:S(2)}, u32[]{:S(2)}) %collective-permute-start.14) | collective-permute-done | bytes 393248 | tf_op jit(solution)/shard_map/ppermute | solution.py:248
  61.8 2.2 %shard_map.90 = bf16[512,512]{1,0:T(8,128)(2,1)S(1)} custom-call(s32[4,16]{1,0:T(4,128)S(1)} %pad_add_fusion.meta, bf16[128,1536]{1,0:T(8,128)(2,1)S(1)} %collective-permute-done.8.refs_0_, bf16[128,1536]{1,0:T(8,128)(2,1)S(1)} %collective-permute-done.13.refs_1_, bf16[128,1536]{1,0:T(8,128)(2,1)S(1)} %collective-permute-done.14.refs_2_, ...), custom_call_target="tpu_custom_call" | custom-call | flops 1000 | bytes 1000 | tf_op jit(solution)/shard_map/pallas_call | solution.py:77
  64.1 1.4 %collective-permute-start.23 = (bf16[512,512]{1,0:T(8,128)(2,1)S(1)}, bf16[512,512]{1,0:T(8,128)(2,1)S(1)}, u32[]{:S(2)}, u32[]{:S(2)}) collective-permute-start(bf16[512,512]{1,0:T(8,128)(2,1)S(1)} %shard_map.90), channel_id=1, source_target_pairs={{0,1},{1,0},{2,3},{3,2},{4,5},{5,4},{6,7},{7,6},{8,9},{9,8},{10,11... | collective-permute-start | bytes 1572872 | tf_op jit(solution)/shard_map/ppermute | solution.py:248
  65.5 2.0 %shard_map.89.one = f32[512,512]{1,0:T(8,128)S(1)} custom-call(s32[4,16]{1,0:T(4,128)S(1)} %pad_add_fusion.meta, bf16[128,1536]{1,0:T(8,128)(2,1)S(1)} %collective-permute-done.8.refs_0_, bf16[128,1536]{1,0:T(8,128)(2,1)S(1)} %collective-permute-done.13.refs_1_, bf16[128,1536]{1,0:T(8,128)(2,1)S(1)} %collective-permute-done.14.refs_2_, ...), custom_call_target="tpu_custom_call" | custom-call | flops 1000 | bytes 1000 | tf_op jit(solution)/shard_map/pallas_call | solution.py:77
  67.7 1.3 %collective-permute-start.24 = (bf16[512,512]{1,0:T(8,128)(2,1)S(1)}, bf16[512,512]{1,0:T(8,128)(2,1)S(1)}, u32[]{:S(2)}, u32[]{:S(2)}) collective-permute-start(bf16[512,512]{1,0:T(8,128)(2,1)S(1)} %shard_map.91), channel_id=1, source_target_pairs={{0,2},{1,3},{2,0},{3,1},{4,6},{5,7},{6,4},{7,5},{8,10},{9,11},{10,... | collective-permute-start | bytes 1572872 | tf_op jit(solution)/shard_map/ppermute | solution.py:248
  68.9 3.4 %shard_map.86 = (f32[512,512]{1,0:T(8,128)S(1)}, f32[512,512]{1,0:T(8,128)S(1)}) custom-call(s32[4,16]{1,0:T(4,128)S(1)} %pad_add_fusion.meta, bf16[128,1536]{1,0:T(8,128)(2,1)S(1)} %collective-permute-done.8.refs_0_, bf16[128,1536]{1,0:T(8,128)(2,1)S(1)} %collective-permute-done.13.refs_1_, bf16[128,1536]{1,0:T(8,128)(2,1)S(1)} %collective-permute-done.14.refs_2_, ...), custom_call_target="tpu_custom_call" | custom-call | flops 1000 | bytes 1000 | tf_op jit(solution)/shard_map/pallas_call | solution.py:77
  72.4 12.7 %collective-permute-done.18.ypts = bf16[512,1024]{1,0:T(8,128)(2,1)S(1)} collective-permute-done((bf16[512,1024]{1,0:T(8,128)(2,1)S(1)}, bf16[512,1024]{1,0:T(8,128)(2,1)S(1)}, u32[]{:S(2)}, u32[]{:S(2)}) %collective-permute-start.18) | collective-permute-done | bytes 1048608 | tf_op jit(solution)/shard_map/ppermute | solution.py:248
  85.7 1.6 %collective-permute-start.22 = (bf16[256,512]{1,0:T(8,128)(2,1)S(1)}, bf16[256,512]{1,0:T(8,128)(2,1)S(1)}, u32[]{:S(2)}, u32[]{:S(2)}) collective-permute-start(bf16[256,512]{1,0:T(8,128)(2,1)S(1)} %get-tuple-element.76), channel_id=1, source_target_pairs={{0,1},{1,0},{2,3},{3,2},{4,5},{5,4},{6,7},{7,6},{8,9},{9,8},{10,11... | collective-permute-start | bytes 786440 | tf_op jit(solution)/shard_map/ppermute | solution.py:248
  87.5 1.7 %shard_map.87 = f32[512,512]{1,0:T(8,128)S(1)} custom-call(s32[4,16]{1,0:T(4,128)S(1)} %pad_add_fusion.meta, bf16[512,1024]{1,0:T(8,128)(2,1)S(1)} %copy-done, f32[512,512]{1,0:T(8,128)S(1)} %get-tuple-element.71.start, bf16[512,1024]{1,0:T(8,128)(2,1)S(1)} %collective-permute-done.18.ypts, bf16[512,512]{1,0:T(8,128)(2,1)S(1)} %collective-permute-done.20.wts), custom_call_target="tpu_custom_call" | custom-call | flops 1000 | bytes 1000 | tf_op jit(solution)/shard_map/pallas_call | solution.py:77
  89.2 1.2 %convert_add_fusion = f32[512,512]{1,0:T(8,128)} fusion(bf16[512,512]{1,0:T(8,128)(2,1)S(1)} %collective-permute-done.24, f32[512,512]{1,0:T(8,128)S(1)} %shard_map.87, bf16[256,512]{1,0:T(8,128)(2,1)S(1)} %collective-permute-done.22, bf16[256,512]{1,0:T(8,128)(2,1)S(1)} %collective-permute-done.21), kind=kLoop, calls=%fused_computation | loop fusion | flops 1835008 | bytes 3145728 | tf_op jit(solution)/shard_map/add | solution.py:340
  (50 shorter events, 5.1 us)
Async XLA Ops:
  0.0 15.3 %copy-start = (bf16[512,1024]{1,0:T(8,128)(2,1)S(1)}, bf16[512,1024]{1,0:T(8,128)(2,1)}, u32[]{:S(2)}) copy-start(bf16[512,1024]{1,0:T(8,128)(2,1)} %xpts.1) | copy-start | bytes 3145732
  0.0 17.4 %collective-permute-start.5 = (bf16[512,512]{1,0:T(8,128)(2,1)}, bf16[512,512]{1,0:T(8,128)(2,1)S(1)}, u32[]{:S(2)}, u32[]{:S(2)}) collective-permute-start(bf16[512,512]{1,0:T(8,128)(2,1)} %refs_7_.3), channel_id=1, source_target_pairs={{2,6},{3,7},{4,0},{5,1},{6,10},{7,11},{8,4},{9,5},{10,14},{11,15},... | collective-permute-start | bytes 1572872 | tf_op jit(solution)/shard_map/ppermute | solution.py:248
  3.3 1.1 %copy-start.1 = (bf16[512,512]{1,0:T(8,128)(2,1)S(1)}, bf16[512,512]{1,0:T(8,128)(2,1)}, u32[]{:S(2)}) copy-start(bf16[512,512]{1,0:T(8,128)(2,1)} %refs_7_.3) | copy-start | bytes 1572868
  4.3 1.0 %copy-start.3 = (bf16[512,512]{1,0:T(8,128)(2,1)S(1)}, bf16[512,512]{1,0:T(8,128)(2,1)}, u32[]{:S(2)}) copy-start(bf16[512,512]{1,0:T(8,128)(2,1)} %proj.1) | copy-start | bytes 1572868
  5.9 2.7 %collective-permute-start = (bf16[1,128,512]{2,1,0:T(8,128)(2,1)S(1)}, bf16[1,128,512]{2,1,0:T(8,128)(2,1)S(1)}, u32[]{:S(2)}, u32[]{:S(2)}) collective-permute-start(bf16[1,128,512]{2,1,0:T(8,128)(2,1)S(1)} %get-tuple-element.43), channel_id=1, source_target_pairs={{0,1},{1,0},{2,3},{3,2},{4,5},{5,4},{6,7},{7,6},{8,9},{9,8},{10,11... | collective-permute-start | bytes 393224 | tf_op jit(solution)/shard_map/ppermute | solution.py:248
  6.9 5.1 %collective-permute-start.1 = (bf16[1,128,512]{2,1,0:T(8,128)(2,1)S(1)}, bf16[1,128,512]{2,1,0:T(8,128)(2,1)S(1)}, u32[]{:S(2)}, u32[]{:S(2)}) collective-permute-start(bf16[1,128,512]{2,1,0:T(8,128)(2,1)S(1)} %get-tuple-element.44), channel_id=1, source_target_pairs={{0,2},{1,3},{2,0},{3,1},{4,6},{5,7},{6,4},{7,5},{8,10},{9,11},{10,... | collective-permute-start | bytes 393224 | tf_op jit(solution)/shard_map/ppermute | solution.py:248
  6.9 8.3 %copy-start.4 = (s32[1,128]{1,0:T(1,128)S(1)}, s32[1,128]{1,0:T(1,128)}, u32[]{:S(2)}) copy-start(s32[1,128]{1,0:T(1,128)} %idx.1) | copy-start | bytes 1540
  6.9 8.3 %collective-permute-start.2 = (bf16[1,128,512]{2,1,0:T(8,128)(2,1)S(1)}, bf16[1,128,512]{2,1,0:T(8,128)(2,1)S(1)}, u32[]{:S(2)}, u32[]{:S(2)}) collective-permute-start(bf16[1,128,512]{2,1,0:T(8,128)(2,1)S(1)} %get-tuple-element.45), channel_id=1, source_target_pairs={{0,3},{1,2},{2,1},{3,0},{4,7},{5,6},{6,5},{7,4},{8,11},{9,10},{10,... | collective-permute-start | bytes 393224 | tf_op jit(solution)/shard_map/ppermute | solution.py:248
  15.3 25.7 %collective-permute-start.10 = (bf16[512,1024]{1,0:T(8,128)(2,1)S(1)}, bf16[512,1024]{1,0:T(8,128)(2,1)S(1)}, u32[]{:S(2)}, u32[]{:S(2)}) collective-permute-start(bf16[512,1024]{1,0:T(8,128)(2,1)S(1)} %copy-done), channel_id=1, source_target_pairs={{0,2},{1,3},{2,0},{3,1},{4,6},{5,7},{6,4},{7,5},{8,10},{9,11},{10,... | collective-permute-start | bytes 3145736 | tf_op jit(solution)/shard_map/ppermute | solution.py:248
  15.6 10.5 %collective-permute-start.3 = (bf16[128,1536]{1,0:T(8,128)(2,1)S(1)}, bf16[128,1536]{1,0:T(8,128)(2,1)S(1)}, u32[]{:S(2)}, u32[]{:S(2)}) collective-permute-start(bf16[128,1536]{1,0:T(8,128)(2,1)S(1)} %shard_map.83.refs_0_), channel_id=1, source_target_pairs={{0,4},{1,5},{2,6},{3,7},{4,0},{5,1},{6,2},{7,3},{8,12},{9,13},{10,... | collective-permute-start | bytes 1179656 | tf_op jit(solution)/shard_map/ppermute | solution.py:248
  15.9 12.2 %collective-permute-start.4 = (bf16[128,1536]{1,0:T(8,128)(2,1)S(1)}, bf16[128,1536]{1,0:T(8,128)(2,1)}, u32[]{:S(2)}, u32[]{:S(2)}) collective-permute-start(bf16[128,1536]{1,0:T(8,128)(2,1)S(1)} %shard_map.83.refs_0_), channel_id=1, source_target_pairs={{0,8},{1,9},{2,10},{3,11},{4,12},{5,13},{6,14},{7,15},{8,16},{9,17... | collective-permute-start | bytes 1179656 | tf_op jit(solution)/shard_map/ppermute | solution.py:248
  17.4 10.8 %collective-permute-start.6 = (bf16[352,512]{1,0:T(8,128)(2,1)S(1)}, bf16[352,512]{1,0:T(8,128)(2,1)}, u32[]{:S(2)}, u32[]{:S(2)}) collective-permute-start(bf16[352,512]{1,0:T(8,128)(2,1)S(1)} %split.8), channel_id=1, source_target_pairs={{0,1},{1,0},{2,3},{3,2},{4,5},{5,4},{6,7},{7,6},{8,9},{9,8},{10,11... | collective-permute-start | bytes 1081352 | tf_op jit(solution)/shard_map/ppermute | solution.py:248
  18.2 9.9 %collective-permute-start.7 = (bf16[160,512]{1,0:T(8,128)(2,1)S(1)}, bf16[160,512]{1,0:T(8,128)(2,1)S(1)}, u32[]{:S(2)}, u32[]{:S(2)}) collective-permute-start(bf16[160,512]{1,0:T(8,128)(2,1)S(1)} %split.9), channel_id=1, source_target_pairs={{0,1},{1,0},{2,3},{3,2},{4,5},{5,4},{6,7},{7,6},{8,9},{9,8},{10,11... | collective-permute-start | bytes 491528 | tf_op jit(solution)/shard_map/ppermute | solution.py:248
  28.2 12.8 %collective-permute-start.8 = (bf16[128,1536]{1,0:T(8,128)(2,1)}, bf16[128,1536]{1,0:T(8,128)(2,1)S(1)}, u32[]{:S(2)}, u32[]{:S(2)}) collective-permute-start(bf16[128,1536]{1,0:T(8,128)(2,1)} %collective-permute-done.4.refs_2_), channel_id=1, source_target_pairs={{0,4},{1,5},{2,6},{3,7},{4,0},{5,1},{6,2},{7,3},{8,12},{9,13},{10,... | collective-permute-start | bytes 1179656 | tf_op jit(solution)/shard_map/ppermute | solution.py:248
  29.0 12.0 %collective-permute-start.9 = (bf16[128,1536]{1,0:T(8,128)(2,1)S(1)}, bf16[128,1536]{1,0:T(8,128)(2,1)}, u32[]{:S(2)}, u32[]{:S(2)}) collective-permute-start(bf16[128,1536]{1,0:T(8,128)(2,1)S(1)} %shard_map.83.refs_0_), channel_id=1, source_target_pairs={{0,24},{1,25},{2,26},{3,27},{4,28},{5,29},{6,30},{7,31},{8,0},{9,1... | collective-permute-start | bytes 1179656 | tf_op jit(solution)/shard_map/ppermute | solution.py:248
  31.4 0.7 copy-start.5
  31.4 0.7 copy-start.6
  32.1 2.4 %collective-permute-start.11 = (s32[1,16]{1,0:T(1,128)S(1)}, s32[1,16]{1,0:T(1,128)S(1)}, u32[]{:S(2)}, u32[]{:S(2)}) collective-permute-start(s32[1,16]{1,0:T(1,128)S(1)} %bitcast.4), channel_id=1, source_target_pairs={{0,1},{1,0},{2,3},{3,2},{4,5},{5,4},{6,7},{7,6},{8,9},{9,8},{10,11... | collective-permute-start | bytes 200 | tf_op jit(solution)/shard_map/ppermute | solution.py:248
  34.6 5.7 %collective-permute-start.12 = (s32[2,16]{1,0:T(2,128)S(1)}, s32[2,16]{1,0:T(2,128)S(1)}, u32[]{:S(2)}, u32[]{:S(2)}) collective-permute-start(s32[2,16]{1,0:T(2,128)S(1)} %pad_add_fusion.1), channel_id=1, source_target_pairs={{0,2},{1,3},{2,0},{3,1},{4,6},{5,7},{6,4},{7,5},{8,10},{9,11},{10,... | collective-permute-start | bytes 392 | tf_op jit(solution)/shard_map/ppermute | solution.py:248
  40.3 8.0 %copy-start.2 = (bf16[512,512]{1,0:T(8,128)(2,1)S(1)}, bf16[512,512]{1,0:T(8,128)(2,1)}, u32[]{:S(2)}) copy-start(bf16[512,512]{1,0:T(8,128)(2,1)} %refs_7_.3) | copy-start | bytes 1572868
  40.3 4.7 %collective-permute-start.16 = (bf16[512,1024]{1,0:T(8,128)(2,1)S(1)}, bf16[512,1024]{1,0:T(8,128)(2,1)S(1)}, u32[]{:S(2)}, u32[]{:S(2)}) collective-permute-start(bf16[512,1024]{1,0:T(8,128)(2,1)S(1)} %copy-done), channel_id=1, source_target_pairs={{0,1},{1,0},{2,3},{3,2},{4,5},{5,4},{6,7},{7,6},{8,9},{9,8},{10,11... | collective-permute-start | bytes 3145736 | tf_op jit(solution)/shard_map/ppermute | solution.py:248
  41.0 4.2 %collective-permute-start.17 = (bf16[512,1024]{1,0:T(8,128)(2,1)S(1)}, bf16[512,1024]{1,0:T(8,128)(2,1)S(1)}, u32[]{:S(2)}, u32[]{:S(2)}) collective-permute-start(bf16[512,1024]{1,0:T(8,128)(2,1)S(1)} %collective-permute-done.10.refs_4_), channel_id=1, source_target_pairs={{0,1},{1,0},{2,3},{3,2},{4,5},{5,4},{6,7},{7,6},{8,9},{9,8},{10,11... | collective-permute-start | bytes 3145736 | tf_op jit(solution)/shard_map/ppermute | solution.py:248
  41.1 16.3 %collective-permute-start.13 = (bf16[128,1536]{1,0:T(8,128)(2,1)}, bf16[128,1536]{1,0:T(8,128)(2,1)S(1)}, u32[]{:S(2)}, u32[]{:S(2)}) collective-permute-start(bf16[128,1536]{1,0:T(8,128)(2,1)} %collective-permute-done.4.refs_2_), channel_id=1, source_target_pairs={{0,8},{1,9},{2,10},{3,11},{4,12},{5,13},{6,14},{7,15},{8,16},{9,17... | collective-permute-start | bytes 1179656 | tf_op jit(solution)/shard_map/ppermute | solution.py:248
  42.4 19.4 %collective-permute-start.14 = (bf16[128,1536]{1,0:T(8,128)(2,1)S(1)}, bf16[128,1536]{1,0:T(8,128)(2,1)S(1)}, u32[]{:S(2)}, u32[]{:S(2)}) collective-permute-start(bf16[128,1536]{1,0:T(8,128)(2,1)S(1)} %collective-permute-done.8.refs_0_), channel_id=1, source_target_pairs={{0,8},{1,9},{2,10},{3,11},{4,12},{5,13},{6,14},{7,15},{8,16},{9,17... | collective-permute-start | bytes 1179656 | tf_op jit(solution)/shard_map/ppermute | solution.py:248
  43.7 18.1 %collective-permute-start.15 = (bf16[128,1536]{1,0:T(8,128)(2,1)}, bf16[128,1536]{1,0:T(8,128)(2,1)S(1)}, u32[]{:S(2)}, u32[]{:S(2)}) collective-permute-start(bf16[128,1536]{1,0:T(8,128)(2,1)} %collective-permute-done.9.refs_3_), channel_id=1, source_target_pairs={{0,4},{1,5},{2,6},{3,7},{4,0},{5,1},{6,2},{7,3},{8,12},{9,13},{10,... | collective-permute-start | bytes 1179656 | tf_op jit(solution)/shard_map/ppermute | solution.py:248
  45.0 20.4 %collective-permute-start.19 = (bf16[512,512]{1,0:T(8,128)(2,1)S(1)}, bf16[512,512]{1,0:T(8,128)(2,1)S(1)}, u32[]{:S(2)}, u32[]{:S(2)}) collective-permute-start(bf16[512,512]{1,0:T(8,128)(2,1)S(1)} %pad_maximum_fusion), channel_id=1, source_target_pairs={{0,2},{1,3},{2,0},{3,1},{4,6},{5,7},{6,4},{7,5},{8,10},{9,11},{10,... | collective-permute-start | bytes 1572872 | tf_op jit(solution)/shard_map/ppermute | solution.py:248
  45.2 39.9 %collective-permute-start.18 = (bf16[512,1024]{1,0:T(8,128)(2,1)S(1)}, bf16[512,1024]{1,0:T(8,128)(2,1)S(1)}, u32[]{:S(2)}, u32[]{:S(2)}) collective-permute-start(bf16[512,1024]{1,0:T(8,128)(2,1)S(1)} %collective-permute-done.10.refs_4_), channel_id=1, source_target_pairs={{0,4},{1,5},{4,8},{5,9},{6,2},{7,3},{8,12},{9,13},{10,6},{11,7},{1... | collective-permute-start | bytes 3145736 | tf_op jit(solution)/shard_map/ppermute | solution.py:248
  64.1 3.5 %collective-permute-start.23 = (bf16[512,512]{1,0:T(8,128)(2,1)S(1)}, bf16[512,512]{1,0:T(8,128)(2,1)S(1)}, u32[]{:S(2)}, u32[]{:S(2)}) collective-permute-start(bf16[512,512]{1,0:T(8,128)(2,1)S(1)} %shard_map.90), channel_id=1, source_target_pairs={{0,1},{1,0},{2,3},{3,2},{4,5},{5,4},{6,7},{7,6},{8,9},{9,8},{10,11... | collective-permute-start | bytes 1572872 | tf_op jit(solution)/shard_map/ppermute | solution.py:248
  65.4 7.0 %collective-permute-start.20 = (bf16[512,512]{1,0:T(8,128)(2,1)S(1)}, bf16[512,512]{1,0:T(8,128)(2,1)S(1)}, u32[]{:S(2)}, u32[]{:S(2)}) collective-permute-start(bf16[512,512]{1,0:T(8,128)(2,1)S(1)} %collective-permute-done.19), channel_id=1, source_target_pairs={{0,1},{1,0},{2,3},{3,2},{4,5},{5,4},{6,7},{7,6},{8,9},{9,8},{10,11... | collective-permute-start | bytes 1572872 | tf_op jit(solution)/shard_map/ppermute | solution.py:248
  67.7 21.5 %collective-permute-start.24 = (bf16[512,512]{1,0:T(8,128)(2,1)S(1)}, bf16[512,512]{1,0:T(8,128)(2,1)S(1)}, u32[]{:S(2)}, u32[]{:S(2)}) collective-permute-start(bf16[512,512]{1,0:T(8,128)(2,1)S(1)} %shard_map.91), channel_id=1, source_target_pairs={{0,2},{1,3},{2,0},{3,1},{4,6},{5,7},{6,4},{7,5},{8,10},{9,11},{10,... | collective-permute-start | bytes 1572872 | tf_op jit(solution)/shard_map/ppermute | solution.py:248
  85.7 3.4 %collective-permute-start.22 = (bf16[256,512]{1,0:T(8,128)(2,1)S(1)}, bf16[256,512]{1,0:T(8,128)(2,1)S(1)}, u32[]{:S(2)}, u32[]{:S(2)}) collective-permute-start(bf16[256,512]{1,0:T(8,128)(2,1)S(1)} %get-tuple-element.76), channel_id=1, source_target_pairs={{0,1},{1,0},{2,3},{3,2},{4,5},{5,4},{6,7},{7,6},{8,9},{9,8},{10,11... | collective-permute-start | bytes 786440 | tf_op jit(solution)/shard_map/ppermute | solution.py:248
  87.4 1.8 %collective-permute-start.21 = (bf16[256,512]{1,0:T(8,128)(2,1)S(1)}, bf16[256,512]{1,0:T(8,128)(2,1)S(1)}, u32[]{:S(2)}, u32[]{:S(2)}) collective-permute-start(bf16[256,512]{1,0:T(8,128)(2,1)S(1)} %get-tuple-element.75), channel_id=1, source_target_pairs={{0,1},{1,0},{2,3},{3,2},{4,5},{5,4},{6,7},{7,6},{8,9},{9,8},{10,11... | collective-permute-start | bytes 786440 | tf_op jit(solution)/shard_map/ppermute | solution.py:248

commit v6 on v5

--- a/solution.py
+++ b/solution.py
@@ -21,6 +21,7 @@
 FAR_COUNT = FAR_LIST + FAR
 LEAF = FAR_COUNT + 1
 META = 16
+PIECES = 4
 
 
 def vmem():
@@ -209,12 +210,15 @@
     return call(sum_body, jax.ShapeDtypeStruct(one.shape, BF16), (), (one, two))
 
 
-def cross_body(row, meta, xpts, start, ypts, wts, *outs):
+def cross_body(row, more, meta, xpts, start, ypts, wts, *refs):
+    extras, outs = refs[:more], refs[more:]
     leaf = meta[0, LEAF]
     scale = half_scale(xpts.shape[1])
     hit = near_hit(meta, row, leaf + 4 * (leaf // 2 % 2) - 2)
 
     def put(value):
+        for extra in extras:
+            value = value + extra[...].astype(F32)
         first = 0
         for out in outs:
             out[...] = value[first : first + out.shape[0]].astype(out.dtype)
@@ -230,10 +234,38 @@
         put(start[...])
 
 
-def cross_terms(row, meta, xpts, start, ypts, wts, kind, cuts):
+def cross_terms(row, meta, xpts, start, ypts, wts, kind, cuts, extras=()):
     rows, wcols = start.shape
     shapes = (jax.ShapeDtypeStruct((rows // cuts, wcols), kind),) * cuts
-    return call(functools.partial(cross_body, row), shapes, (meta,), (xpts, start, ypts, wts))
+    body = functools.partial(cross_body, row, len(extras))
+    return call(body, shapes, (meta,), (xpts, start, ypts, wts, *extras))
+
+
+def finish_body(acc, upper, lower, out, here, sems):
+    rows = acc.shape[0] // PIECES
+    copies = []
+    for piece in range(PIECES):
+        part = pl.ds(piece * rows, rows)
+        half, first = divmod(piece * rows, upper.shape[0])
+        other = (upper, lower)[half][first : first + rows]
+        here[part, :] = acc[part, :] + other.astype(F32)
+        copy = pltpu.make_async_copy(here.at[part], out.at[part], sems.at[piece])
+        copy.start()
+        copies.append(copy)
+    for copy in copies:
+        copy.wait()
+
+
+def finish(acc, upper, lower):
+    return pl.pallas_call(
+        finish_body,
+        out_shape=jax.ShapeDtypeStruct(acc.shape, F32),
+        in_specs=[vmem()] * 3,
+        out_specs=pl.BlockSpec(memory_space=pl.ANY),
+        scratch_shapes=[pltpu.VMEM(acc.shape, F32), pltpu.SemaphoreType.DMA((PIECES,))],
+        compiler_params=params(),
+        cost_estimate=pl.CostEstimate(flops=1000, bytes_accessed=1000, transcendentals=0),
+    )(acc, upper, lower)
 
 
 def shards(points, weights, node_proj, skel_idx, near_list, near_count, far_list, far_count):
@@ -335,9 +367,8 @@
         group, last_places, (0, 1), meta, rest, near_x, (), (acc0, acc1), (F32, F32)
     )
     out1 = cross_terms(1, meta, pts_core, acc1, cross_p, cross_w, BF16, 2)
-    (acc0,) = cross_terms(0, meta, points, acc0, cross_p, cross_w, F32, 1)
-    extra = jnp.concatenate([move(half, core) for half in out1], axis=0)
-    return acc0 + extra.astype(F32) + last.astype(F32)
+    (acc0,) = cross_terms(0, meta, points, acc0, cross_p, cross_w, F32, 1, (last,))
+    return finish(acc0, *[move(half, core) for half in out1])
 
 
 def solution(mesh):

time: 90.2 us -> 89.8 us (level)
  other arithmetic: 2.22 us -> 1.04 us
  Pallas kernels: 20.2 us -> 21.3 us
  starting transfers between devices: 24.8 us -> 23.7 us
    add x1 -> x0, other arithmetic: 1.19 us -> none  [shards(): return acc0 + extra.astype(F32) + last.astype(F32)]
    ppermute x25, starting transfers between devices: 24.8 us -> 23.7 us  [move(): lax.ppermute(value, 'pts', [(a, b) for a, b in pairs if b is not None])]
    pallas_call x0 -> x1, Pallas kernels: none -> 1.02 us  [finish(): pl.pallas_call(finish_body, out_shape=jax.ShapeDtypeStruct(acc.shape, F32...]
  transfers between devices with their start and end apart: 25 -> 25, of which waited for: 8 -> 8; matrix products, arithmetic and copies ran while one was open for 1% -> 1% of each run, Pallas kernels for 22% -> 23%
where the time goes in v6:
time: 89.8 us; the launch traced here: 89.3 us
  waiting for transfers between devices  38.7 us (43%)
  starting transfers between devices  23.7 us (26%)
  Pallas kernels  21.3 us (24%)
  local copies, waits for them, and re-layouts  2.86 us (3%)
  between operations  1.69 us (2%)
  other arithmetic  1.04 us (1%)
    ppermute x25, waiting for transfers between devices, move(): lax.ppermute(value, 'pts', [(a, b) for a, b in pairs if b is not None])  38.7 us
    ppermute x25, starting transfers between devices, move(): lax.ppermute(value, 'pts', [(a, b) for a, b in pairs if b is not None])  23.7 us
    pallas_call x10, Pallas kernels, call(): pl.pallas_call(body, out_shape=kinds, in_specs=[smem()] * len(scalars) +...  20.3 us
    unnamed x14, local copies, waits for them, and re-layouts  2.75 us
  transfers between devices with their start and end apart: 25, of which 8 were waited for; matrix products, arithmetic and copies ran while one was open for 1% of the time, Pallas kernels for 23%

profile of v6, /device:TPU:7, one launch (start us, length us, event | category | flops | bytes accessed | tf_op | source)
XLA Modules:
  0.0 89.3 jit_solution(11144662899270132071)
XLA Ops:
  0.0 3.3 %collective-permute-start.5 = (bf16[512,512]{1,0:T(8,128)(2,1)}, bf16[512,512]{1,0:T(8,128)(2,1)S(1)}, u32[]{:S(2)}, u32[]{:S(2)}) collective-permute-start(bf16[512,512]{1,0:T(8,128)(2,1)} %refs_7_.3), channel_id=1, source_target_pairs={{2,6},{3,7},{4,0},{5,1},{6,10},{7,11},{8,4},{9,5},{10,14},{11,15},... | collective-permute-start | bytes 1572872 | tf_op jit(solution)/shard_map/ppermute | solution.py:280
  3.3 1.0 %copy-done.1 = bf16[512,512]{1,0:T(8,128)(2,1)S(1)} copy-done((bf16[512,512]{1,0:T(8,128)(2,1)S(1)}, bf16[512,512]{1,0:T(8,128)(2,1)}, u32[]{:S(2)}) %copy-start.1) | copy-done | bytes 524312
  4.3 1.0 %copy-done.3 = bf16[512,512]{1,0:T(8,128)(2,1)S(1)} copy-done((bf16[512,512]{1,0:T(8,128)(2,1)S(1)}, bf16[512,512]{1,0:T(8,128)(2,1)}, u32[]{:S(2)}) %copy-start.3) | copy-done | bytes 524312
  5.9 1.0 %collective-permute-start = (bf16[1,128,512]{2,1,0:T(8,128)(2,1)S(1)}, bf16[1,128,512]{2,1,0:T(8,128)(2,1)S(1)}, u32[]{:S(2)}, u32[]{:S(2)}) collective-permute-start(bf16[1,128,512]{2,1,0:T(8,128)(2,1)S(1)} %get-tuple-element.43), channel_id=1, source_target_pairs={{0,1},{1,0},{2,3},{3,2},{4,5},{5,4},{6,7},{7,6},{8,9},{9,8},{10,11... | collective-permute-start | bytes 393224 | tf_op jit(solution)/shard_map/ppermute | solution.py:280
  6.9 1.7 %collective-permute-start.2 = (bf16[1,128,512]{2,1,0:T(8,128)(2,1)S(1)}, bf16[1,128,512]{2,1,0:T(8,128)(2,1)S(1)}, u32[]{:S(2)}, u32[]{:S(2)}) collective-permute-start(bf16[1,128,512]{2,1,0:T(8,128)(2,1)S(1)} %get-tuple-element.45), channel_id=1, source_target_pairs={{0,3},{1,2},{2,1},{3,0},{4,7},{5,6},{6,5},{7,4},{8,11},{9,10},{10,... | collective-permute-start | bytes 393224 | tf_op jit(solution)/shard_map/ppermute | solution.py:280
  8.6 3.4 %collective-permute-done.1.refs_1_ = bf16[1,128,512]{2,1,0:T(8,128)(2,1)S(1)} collective-permute-done((bf16[1,128,512]{2,1,0:T(8,128)(2,1)S(1)}, bf16[1,128,512]{2,1,0:T(8,128)(2,1)S(1)}, u32[]{:S(2)}, u32[]{:S(2)}) %collective-permute-start.1) | collective-permute-done | bytes 131104 | tf_op jit(solution)/shard_map/ppermute | solution.py:280
  12.0 3.3 %collective-permute-done.2.refs_2_ = bf16[1,128,512]{2,1,0:T(8,128)(2,1)S(1)} collective-permute-done((bf16[1,128,512]{2,1,0:T(8,128)(2,1)S(1)}, bf16[1,128,512]{2,1,0:T(8,128)(2,1)S(1)}, u32[]{:S(2)}, u32[]{:S(2)}) %collective-permute-start.2) | collective-permute-done | bytes 131104 | tf_op jit(solution)/shard_map/ppermute | solution.py:280
  15.9 1.4 %collective-permute-start.4 = (bf16[128,1536]{1,0:T(8,128)(2,1)S(1)}, bf16[128,1536]{1,0:T(8,128)(2,1)}, u32[]{:S(2)}, u32[]{:S(2)}) collective-permute-start(bf16[128,1536]{1,0:T(8,128)(2,1)S(1)} %shard_map.83.refs_0_), channel_id=1, source_target_pairs={{0,8},{1,9},{2,10},{3,11},{4,12},{5,13},{6,14},{7,15},{8,16},{9,17... | collective-permute-start | bytes 1179656 | tf_op jit(solution)/shard_map/ppermute | solution.py:280
  17.4 0.8 collective-permute-start.6
  18.3 7.8 %collective-permute-done.3.refs_1_ = bf16[128,1536]{1,0:T(8,128)(2,1)S(1)} collective-permute-done((bf16[128,1536]{1,0:T(8,128)(2,1)S(1)}, bf16[128,1536]{1,0:T(8,128)(2,1)S(1)}, u32[]{:S(2)}, u32[]{:S(2)}) %collective-permute-start.3) | collective-permute-done | bytes 393248 | tf_op jit(solution)/shard_map/ppermute | solution.py:280
  26.1 2.1 %collective-permute-done.4.refs_2_ = bf16[128,1536]{1,0:T(8,128)(2,1)} collective-permute-done((bf16[128,1536]{1,0:T(8,128)(2,1)S(1)}, bf16[128,1536]{1,0:T(8,128)(2,1)}, u32[]{:S(2)}, u32[]{:S(2)}) %collective-permute-start.4) | collective-permute-done | bytes 393248 | tf_op jit(solution)/shard_map/ppermute | solution.py:280
  28.2 0.9 collective-permute-start.8
  29.0 1.0 %collective-permute-start.9 = (bf16[128,1536]{1,0:T(8,128)(2,1)S(1)}, bf16[128,1536]{1,0:T(8,128)(2,1)}, u32[]{:S(2)}, u32[]{:S(2)}) collective-permute-start(bf16[128,1536]{1,0:T(8,128)(2,1)S(1)} %shard_map.83.refs_0_), channel_id=1, source_target_pairs={{0,24},{1,25},{2,26},{3,27},{4,28},{5,29},{6,30},{7,31},{8,0},{9,1... | collective-permute-start | bytes 1179656 | tf_op jit(solution)/shard_map/ppermute | solution.py:280
  32.1 1.6 %collective-permute-start.11 = (s32[1,16]{1,0:T(1,128)S(1)}, s32[1,16]{1,0:T(1,128)S(1)}, u32[]{:S(2)}, u32[]{:S(2)}) collective-permute-start(s32[1,16]{1,0:T(1,128)S(1)} %bitcast.4), channel_id=1, source_target_pairs={{0,1},{1,0},{2,3},{3,2},{4,5},{5,4},{6,7},{7,6},{8,9},{9,8},{10,11... | collective-permute-start | bytes 200 | tf_op jit(solution)/shard_map/ppermute | solution.py:280
  33.7 0.8 collective-permute-done.11
  34.6 1.3 %collective-permute-start.12 = (s32[2,16]{1,0:T(2,128)S(1)}, s32[2,16]{1,0:T(2,128)S(1)}, u32[]{:S(2)}, u32[]{:S(2)}) collective-permute-start(s32[2,16]{1,0:T(2,128)S(1)} %pad_add_fusion.1), channel_id=1, source_target_pairs={{0,2},{1,3},{2,0},{3,1},{4,6},{5,7},{6,4},{7,5},{8,10},{9,11},{10,... | collective-permute-start | bytes 392 | tf_op jit(solution)/shard_map/ppermute | solution.py:280
  35.9 4.4 %collective-permute-done.12 = s32[2,16]{1,0:T(2,128)S(1)} collective-permute-done((s32[2,16]{1,0:T(2,128)S(1)}, s32[2,16]{1,0:T(2,128)S(1)}, u32[]{:S(2)}, u32[]{:S(2)}) %collective-permute-start.12) | collective-permute-done | bytes 160 | tf_op jit(solution)/shard_map/ppermute | solution.py:280
  41.1 1.3 %collective-permute-start.13 = (bf16[128,1536]{1,0:T(8,128)(2,1)}, bf16[128,1536]{1,0:T(8,128)(2,1)S(1)}, u32[]{:S(2)}, u32[]{:S(2)}) collective-permute-start(bf16[128,1536]{1,0:T(8,128)(2,1)} %collective-permute-done.4.refs_2_), channel_id=1, source_target_pairs={{0,8},{1,9},{2,10},{3,11},{4,12},{5,13},{6,14},{7,15},{8,16},{9,17... | collective-permute-start | bytes 1179656 | tf_op jit(solution)/shard_map/ppermute | solution.py:280
  42.4 1.3 %collective-permute-start.14 = (bf16[128,1536]{1,0:T(8,128)(2,1)S(1)}, bf16[128,1536]{1,0:T(8,128)(2,1)S(1)}, u32[]{:S(2)}, u32[]{:S(2)}) collective-permute-start(bf16[128,1536]{1,0:T(8,128)(2,1)S(1)} %collective-permute-done.8.refs_0_), channel_id=1, source_target_pairs={{0,8},{1,9},{2,10},{3,11},{4,12},{5,13},{6,14},{7,15},{8,16},{9,17... | collective-permute-start | bytes 1179656 | tf_op jit(solution)/shard_map/ppermute | solution.py:280
  44.0 1.0 %pad_maximum_fusion = bf16[512,512]{1,0:T(8,128)(2,1)S(1)} fusion(bf16[160,512]{1,0:T(8,128)(2,1)S(1)} %collective-permute-done.7, bf16[352,512]{1,0:T(8,128)(2,1)} %collective-permute-done.6), kind=kLoop, calls=%fused_computation | loop fusion | flops 1048576 | bytes 1048576 | tf_op jit(solution)/shard_map/concatenate | solution.py:340
  45.2 3.0 %collective-permute-start.18 = (bf16[512,1024]{1,0:T(8,128)(2,1)S(1)}, bf16[512,1024]{1,0:T(8,128)(2,1)S(1)}, u32[]{:S(2)}, u32[]{:S(2)}) collective-permute-start(bf16[512,1024]{1,0:T(8,128)(2,1)S(1)} %collective-permute-done.10.refs_4_), channel_id=1, source_target_pairs={{0,4},{1,5},{4,8},{5,9},{6,2},{7,3},{8,12},{9,13},{10,6},{11,7},{1... | collective-permute-start | bytes 3145736 | tf_op jit(solution)/shard_map/ppermute | solution.py:280
  48.2 5.8 %shard_map.84 = (f32[512,512]{1,0:T(8,128)S(1)}, f32[512,512]{1,0:T(8,128)S(1)}) custom-call(s32[4,16]{1,0:T(4,128)S(1)} %pad_add_fusion.meta, bf16[128,1536]{1,0:T(8,128)(2,1)S(1)} %shard_map.83.refs_0_, bf16[128,1536]{1,0:T(8,128)(2,1)S(1)} %collective-permute-done.3.refs_1_, bf16[128,1536]{1,0:T(8,128)(2,1)} %collective-permute-done.4.refs_2_, ...), custom_call_target="tpu_custom_call" | custom-call | flops 1000 | bytes 1000 | tf_op jit(solution)/shard_map/pallas_call | solution.py:78
  54.0 4.4 %shard_map.85 = (f32[512,512]{1,0:T(8,128)S(1)}, f32[512,512]{1,0:T(8,128)S(1)}) custom-call(s32[4,16]{1,0:T(4,128)S(1)} %pad_add_fusion.meta, bf16[128,1536]{1,0:T(8,128)(2,1)S(1)} %shard_map.83.refs_0_, bf16[128,1536]{1,0:T(8,128)(2,1)S(1)} %collective-permute-done.3.refs_1_, bf16[128,1536]{1,0:T(8,128)(2,1)} %collective-permute-done.4.refs_2_, ...), custom_call_target="tpu_custom_call" | custom-call | flops 1000 | bytes 1000 | tf_op jit(solution)/shard_map/pallas_call | solution.py:78
  58.5 3.3 %collective-permute-done.14.refs_2_ = bf16[128,1536]{1,0:T(8,128)(2,1)S(1)} collective-permute-done((bf16[128,1536]{1,0:T(8,128)(2,1)S(1)}, bf16[128,1536]{1,0:T(8,128)(2,1)S(1)}, u32[]{:S(2)}, u32[]{:S(2)}) %collective-permute-start.14) | collective-permute-done | bytes 393248 | tf_op jit(solution)/shard_map/ppermute | solution.py:280
  61.8 2.2 %shard_map.88 = bf16[512,512]{1,0:T(8,128)(2,1)S(1)} custom-call(s32[4,16]{1,0:T(4,128)S(1)} %pad_add_fusion.meta, bf16[128,1536]{1,0:T(8,128)(2,1)S(1)} %collective-permute-done.8.refs_0_, bf16[128,1536]{1,0:T(8,128)(2,1)S(1)} %collective-permute-done.13.refs_1_, bf16[128,1536]{1,0:T(8,128)(2,1)S(1)} %collective-permute-done.14.refs_2_, ...), custom_call_target="tpu_custom_call" | custom-call | flops 1000 | bytes 1000 | tf_op jit(solution)/shard_map/pallas_call | solution.py:78
  64.1 1.4 %collective-permute-start.21 = (bf16[512,512]{1,0:T(8,128)(2,1)S(1)}, bf16[512,512]{1,0:T(8,128)(2,1)S(1)}, u32[]{:S(2)}, u32[]{:S(2)}) collective-permute-start(bf16[512,512]{1,0:T(8,128)(2,1)S(1)} %shard_map.88), channel_id=1, source_target_pairs={{0,1},{1,0},{2,3},{3,2},{4,5},{5,4},{6,7},{7,6},{8,9},{9,8},{10,11... | collective-permute-start | bytes 1572872 | tf_op jit(solution)/shard_map/ppermute | solution.py:280
  65.5 2.0 %shard_map.87.one = f32[512,512]{1,0:T(8,128)S(1)} custom-call(s32[4,16]{1,0:T(4,128)S(1)} %pad_add_fusion.meta, bf16[128,1536]{1,0:T(8,128)(2,1)S(1)} %collective-permute-done.8.refs_0_, bf16[128,1536]{1,0:T(8,128)(2,1)S(1)} %collective-permute-done.13.refs_1_, bf16[128,1536]{1,0:T(8,128)(2,1)S(1)} %collective-permute-done.14.refs_2_, ...), custom_call_target="tpu_custom_call" | custom-call | flops 1000 | bytes 1000 | tf_op jit(solution)/shard_map/pallas_call | solution.py:78
  67.7 1.3 %collective-permute-start.22 = (bf16[512,512]{1,0:T(8,128)(2,1)S(1)}, bf16[512,512]{1,0:T(8,128)(2,1)S(1)}, u32[]{:S(2)}, u32[]{:S(2)}) collective-permute-start(bf16[512,512]{1,0:T(8,128)(2,1)S(1)} %shard_map.89), channel_id=1, source_target_pairs={{0,2},{1,3},{2,0},{3,1},{4,6},{5,7},{6,4},{7,5},{8,10},{9,11},{10,... | collective-permute-start | bytes 1572872 | tf_op jit(solution)/shard_map/ppermute | solution.py:280
  69.0 2.5 %shard_map.86 = (f32[512,512]{1,0:T(8,128)S(1)}, f32[512,512]{1,0:T(8,128)S(1)}) custom-call(s32[4,16]{1,0:T(4,128)S(1)} %pad_add_fusion.meta, bf16[128,1536]{1,0:T(8,128)(2,1)S(1)} %collective-permute-done.8.refs_0_, bf16[128,1536]{1,0:T(8,128)(2,1)S(1)} %collective-permute-done.13.refs_1_, bf16[128,1536]{1,0:T(8,128)(2,1)S(1)} %collective-permute-done.14.refs_2_, ...), custom_call_target="tpu_custom_call" | custom-call | flops 1000 | bytes 1000 | tf_op jit(solution)/shard_map/pallas_call | solution.py:78
  71.4 13.7 %collective-permute-done.18.ypts = bf16[512,1024]{1,0:T(8,128)(2,1)S(1)} collective-permute-done((bf16[512,1024]{1,0:T(8,128)(2,1)S(1)}, bf16[512,1024]{1,0:T(8,128)(2,1)S(1)}, u32[]{:S(2)}, u32[]{:S(2)}) %collective-permute-start.18) | collective-permute-done | bytes 1048608 | tf_op jit(solution)/shard_map/ppermute | solution.py:280
  86.4 1.7 %shard_map.90.acc = f32[512,512]{1,0:T(8,128)S(1)} custom-call(s32[4,16]{1,0:T(4,128)S(1)} %pad_add_fusion.meta, bf16[512,1024]{1,0:T(8,128)(2,1)S(1)} %copy-done, f32[512,512]{1,0:T(8,128)S(1)} %get-tuple-element.71.start, bf16[512,1024]{1,0:T(8,128)(2,1)S(1)} %collective-permute-done.18.ypts, bf16[512,512]{1,0:T(8,128)(2,1)S(1)} %collective-permute-done.20.wts, ...), custom_call_target="tpu_custom_call" | custom-call | flops 1000 | bytes 1000 | tf_op jit(solution)/shard_map/pallas_call | solution.py:78
  88.1 1.0 %shard_map.92 = f32[512,512]{1,0:T(8,128)} custom-call(f32[512,512]{1,0:T(8,128)S(1)} %shard_map.90.acc, bf16[256,512]{1,0:T(8,128)(2,1)S(1)} %collective-permute-done.23.upper, bf16[256,512]{1,0:T(8,128)(2,1)S(1)} %collective-permute-done.24.lower), custom_call_target="tpu_custom_call" | custom-call | flops 1000 | bytes 1000 | tf_op jit(solution)/shard_map/pallas_call | solution.py:260
  (50 shorter events, 4.8 us)
Async XLA Ops:
  0.0 15.3 %copy-start = (bf16[512,1024]{1,0:T(8,128)(2,1)S(1)}, bf16[512,1024]{1,0:T(8,128)(2,1)}, u32[]{:S(2)}) copy-start(bf16[512,1024]{1,0:T(8,128)(2,1)} %xpts.1) | copy-start | bytes 3145732
  0.0 17.4 %collective-permute-start.5 = (bf16[512,512]{1,0:T(8,128)(2,1)}, bf16[512,512]{1,0:T(8,128)(2,1)S(1)}, u32[]{:S(2)}, u32[]{:S(2)}) collective-permute-start(bf16[512,512]{1,0:T(8,128)(2,1)} %refs_7_.3), channel_id=1, source_target_pairs={{2,6},{3,7},{4,0},{5,1},{6,10},{7,11},{8,4},{9,5},{10,14},{11,15},... | collective-permute-start | bytes 1572872 | tf_op jit(solution)/shard_map/ppermute | solution.py:280
  3.3 1.1 %copy-start.1 = (bf16[512,512]{1,0:T(8,128)(2,1)S(1)}, bf16[512,512]{1,0:T(8,128)(2,1)}, u32[]{:S(2)}) copy-start(bf16[512,512]{1,0:T(8,128)(2,1)} %refs_7_.3) | copy-start | bytes 1572868
  4.3 1.0 %copy-start.3 = (bf16[512,512]{1,0:T(8,128)(2,1)S(1)}, bf16[512,512]{1,0:T(8,128)(2,1)}, u32[]{:S(2)}) copy-start(bf16[512,512]{1,0:T(8,128)(2,1)} %proj.1) | copy-start | bytes 1572868
  5.9 2.7 %collective-permute-start = (bf16[1,128,512]{2,1,0:T(8,128)(2,1)S(1)}, bf16[1,128,512]{2,1,0:T(8,128)(2,1)S(1)}, u32[]{:S(2)}, u32[]{:S(2)}) collective-permute-start(bf16[1,128,512]{2,1,0:T(8,128)(2,1)S(1)} %get-tuple-element.43), channel_id=1, source_target_pairs={{0,1},{1,0},{2,3},{3,2},{4,5},{5,4},{6,7},{7,6},{8,9},{9,8},{10,11... | collective-permute-start | bytes 393224 | tf_op jit(solution)/shard_map/ppermute | solution.py:280
  6.9 5.1 %collective-permute-start.1 = (bf16[1,128,512]{2,1,0:T(8,128)(2,1)S(1)}, bf16[1,128,512]{2,1,0:T(8,128)(2,1)S(1)}, u32[]{:S(2)}, u32[]{:S(2)}) collective-permute-start(bf16[1,128,512]{2,1,0:T(8,128)(2,1)S(1)} %get-tuple-element.44), channel_id=1, source_target_pairs={{0,2},{1,3},{2,0},{3,1},{4,6},{5,7},{6,4},{7,5},{8,10},{9,11},{10,... | collective-permute-start | bytes 393224 | tf_op jit(solution)/shard_map/ppermute | solution.py:280
  6.9 8.3 %copy-start.4 = (s32[1,128]{1,0:T(1,128)S(1)}, s32[1,128]{1,0:T(1,128)}, u32[]{:S(2)}) copy-start(s32[1,128]{1,0:T(1,128)} %idx.1) | copy-start | bytes 1540
  6.9 8.3 %collective-permute-start.2 = (bf16[1,128,512]{2,1,0:T(8,128)(2,1)S(1)}, bf16[1,128,512]{2,1,0:T(8,128)(2,1)S(1)}, u32[]{:S(2)}, u32[]{:S(2)}) collective-permute-start(bf16[1,128,512]{2,1,0:T(8,128)(2,1)S(1)} %get-tuple-element.45), channel_id=1, source_target_pairs={{0,3},{1,2},{2,1},{3,0},{4,7},{5,6},{6,5},{7,4},{8,11},{9,10},{10,... | collective-permute-start | bytes 393224 | tf_op jit(solution)/shard_map/ppermute | solution.py:280
  15.3 25.7 %collective-permute-start.10 = (bf16[512,1024]{1,0:T(8,128)(2,1)S(1)}, bf16[512,1024]{1,0:T(8,128)(2,1)S(1)}, u32[]{:S(2)}, u32[]{:S(2)}) collective-permute-start(bf16[512,1024]{1,0:T(8,128)(2,1)S(1)} %copy-done), channel_id=1, source_target_pairs={{0,2},{1,3},{2,0},{3,1},{4,6},{5,7},{6,4},{7,5},{8,10},{9,11},{10,... | collective-permute-start | bytes 3145736 | tf_op jit(solution)/shard_map/ppermute | solution.py:280
  15.6 10.5 %collective-permute-start.3 = (bf16[128,1536]{1,0:T(8,128)(2,1)S(1)}, bf16[128,1536]{1,0:T(8,128)(2,1)S(1)}, u32[]{:S(2)}, u32[]{:S(2)}) collective-permute-start(bf16[128,1536]{1,0:T(8,128)(2,1)S(1)} %shard_map.83.refs_0_), channel_id=1, source_target_pairs={{0,4},{1,5},{2,6},{3,7},{4,0},{5,1},{6,2},{7,3},{8,12},{9,13},{10,... | collective-permute-start | bytes 1179656 | tf_op jit(solution)/shard_map/ppermute | solution.py:280
  15.9 12.2 %collective-permute-start.4 = (bf16[128,1536]{1,0:T(8,128)(2,1)S(1)}, bf16[128,1536]{1,0:T(8,128)(2,1)}, u32[]{:S(2)}, u32[]{:S(2)}) collective-permute-start(bf16[128,1536]{1,0:T(8,128)(2,1)S(1)} %shard_map.83.refs_0_), channel_id=1, source_target_pairs={{0,8},{1,9},{2,10},{3,11},{4,12},{5,13},{6,14},{7,15},{8,16},{9,17... | collective-permute-start | bytes 1179656 | tf_op jit(solution)/shard_map/ppermute | solution.py:280
  17.4 10.8 %collective-permute-start.6 = (bf16[352,512]{1,0:T(8,128)(2,1)S(1)}, bf16[352,512]{1,0:T(8,128)(2,1)}, u32[]{:S(2)}, u32[]{:S(2)}) collective-permute-start(bf16[352,512]{1,0:T(8,128)(2,1)S(1)} %split.8), channel_id=1, source_target_pairs={{0,1},{1,0},{2,3},{3,2},{4,5},{5,4},{6,7},{7,6},{8,9},{9,8},{10,11... | collective-permute-start | bytes 1081352 | tf_op jit(solution)/shard_map/ppermute | solution.py:280
  18.2 9.9 %collective-permute-start.7 = (bf16[160,512]{1,0:T(8,128)(2,1)S(1)}, bf16[160,512]{1,0:T(8,128)(2,1)S(1)}, u32[]{:S(2)}, u32[]{:S(2)}) collective-permute-start(bf16[160,512]{1,0:T(8,128)(2,1)S(1)} %split.9), channel_id=1, source_target_pairs={{0,1},{1,0},{2,3},{3,2},{4,5},{5,4},{6,7},{7,6},{8,9},{9,8},{10,11... | collective-permute-start | bytes 491528 | tf_op jit(solution)/shard_map/ppermute | solution.py:280
  28.2 12.8 %collective-permute-start.8 = (bf16[128,1536]{1,0:T(8,128)(2,1)}, bf16[128,1536]{1,0:T(8,128)(2,1)S(1)}, u32[]{:S(2)}, u32[]{:S(2)}) collective-permute-start(bf16[128,1536]{1,0:T(8,128)(2,1)} %collective-permute-done.4.refs_2_), channel_id=1, source_target_pairs={{0,4},{1,5},{2,6},{3,7},{4,0},{5,1},{6,2},{7,3},{8,12},{9,13},{10,... | collective-permute-start | bytes 1179656 | tf_op jit(solution)/shard_map/ppermute | solution.py:280
  29.0 12.0 %collective-permute-start.9 = (bf16[128,1536]{1,0:T(8,128)(2,1)S(1)}, bf16[128,1536]{1,0:T(8,128)(2,1)}, u32[]{:S(2)}, u32[]{:S(2)}) collective-permute-start(bf16[128,1536]{1,0:T(8,128)(2,1)S(1)} %shard_map.83.refs_0_), channel_id=1, source_target_pairs={{0,24},{1,25},{2,26},{3,27},{4,28},{5,29},{6,30},{7,31},{8,0},{9,1... | collective-permute-start | bytes 1179656 | tf_op jit(solution)/shard_map/ppermute | solution.py:280
  31.4 0.7 copy-start.5
  31.4 0.7 copy-start.6
  32.1 2.4 %collective-permute-start.11 = (s32[1,16]{1,0:T(1,128)S(1)}, s32[1,16]{1,0:T(1,128)S(1)}, u32[]{:S(2)}, u32[]{:S(2)}) collective-permute-start(s32[1,16]{1,0:T(1,128)S(1)} %bitcast.4), channel_id=1, source_target_pairs={{0,1},{1,0},{2,3},{3,2},{4,5},{5,4},{6,7},{7,6},{8,9},{9,8},{10,11... | collective-permute-start | bytes 200 | tf_op jit(solution)/shard_map/ppermute | solution.py:280
  34.6 5.7 %collective-permute-start.12 = (s32[2,16]{1,0:T(2,128)S(1)}, s32[2,16]{1,0:T(2,128)S(1)}, u32[]{:S(2)}, u32[]{:S(2)}) collective-permute-start(s32[2,16]{1,0:T(2,128)S(1)} %pad_add_fusion.1), channel_id=1, source_target_pairs={{0,2},{1,3},{2,0},{3,1},{4,6},{5,7},{6,4},{7,5},{8,10},{9,11},{10,... | collective-permute-start | bytes 392 | tf_op jit(solution)/shard_map/ppermute | solution.py:280
  40.3 8.0 %copy-start.2 = (bf16[512,512]{1,0:T(8,128)(2,1)S(1)}, bf16[512,512]{1,0:T(8,128)(2,1)}, u32[]{:S(2)}) copy-start(bf16[512,512]{1,0:T(8,128)(2,1)} %refs_7_.3) | copy-start | bytes 1572868
  40.3 4.7 %collective-permute-start.16 = (bf16[512,1024]{1,0:T(8,128)(2,1)S(1)}, bf16[512,1024]{1,0:T(8,128)(2,1)S(1)}, u32[]{:S(2)}, u32[]{:S(2)}) collective-permute-start(bf16[512,1024]{1,0:T(8,128)(2,1)S(1)} %copy-done), channel_id=1, source_target_pairs={{0,1},{1,0},{2,3},{3,2},{4,5},{5,4},{6,7},{7,6},{8,9},{9,8},{10,11... | collective-permute-start | bytes 3145736 | tf_op jit(solution)/shard_map/ppermute | solution.py:280
  41.0 4.2 %collective-permute-start.17 = (bf16[512,1024]{1,0:T(8,128)(2,1)S(1)}, bf16[512,1024]{1,0:T(8,128)(2,1)S(1)}, u32[]{:S(2)}, u32[]{:S(2)}) collective-permute-start(bf16[512,1024]{1,0:T(8,128)(2,1)S(1)} %collective-permute-done.10.refs_4_), channel_id=1, source_target_pairs={{0,1},{1,0},{2,3},{3,2},{4,5},{5,4},{6,7},{7,6},{8,9},{9,8},{10,11... | collective-permute-start | bytes 3145736 | tf_op jit(solution)/shard_map/ppermute | solution.py:280
  41.1 17.4 %collective-permute-start.13 = (bf16[128,1536]{1,0:T(8,128)(2,1)}, bf16[128,1536]{1,0:T(8,128)(2,1)S(1)}, u32[]{:S(2)}, u32[]{:S(2)}) collective-permute-start(bf16[128,1536]{1,0:T(8,128)(2,1)} %collective-permute-done.4.refs_2_), channel_id=1, source_target_pairs={{0,8},{1,9},{2,10},{3,11},{4,12},{5,13},{6,14},{7,15},{8,16},{9,17... | collective-permute-start | bytes 1179656 | tf_op jit(solution)/shard_map/ppermute | solution.py:280
  42.4 19.4 %collective-permute-start.14 = (bf16[128,1536]{1,0:T(8,128)(2,1)S(1)}, bf16[128,1536]{1,0:T(8,128)(2,1)S(1)}, u32[]{:S(2)}, u32[]{:S(2)}) collective-permute-start(bf16[128,1536]{1,0:T(8,128)(2,1)S(1)} %collective-permute-done.8.refs_0_), channel_id=1, source_target_pairs={{0,8},{1,9},{2,10},{3,11},{4,12},{5,13},{6,14},{7,15},{8,16},{9,17... | collective-permute-start | bytes 1179656 | tf_op jit(solution)/shard_map/ppermute | solution.py:280
  43.7 18.1 %collective-permute-start.15 = (bf16[128,1536]{1,0:T(8,128)(2,1)}, bf16[128,1536]{1,0:T(8,128)(2,1)S(1)}, u32[]{:S(2)}, u32[]{:S(2)}) collective-permute-start(bf16[128,1536]{1,0:T(8,128)(2,1)} %collective-permute-done.9.refs_3_), channel_id=1, source_target_pairs={{0,4},{1,5},{2,6},{3,7},{4,0},{5,1},{6,2},{7,3},{8,12},{9,13},{10,... | collective-permute-start | bytes 1179656 | tf_op jit(solution)/shard_map/ppermute | solution.py:280
  45.0 20.4 %collective-permute-start.19 = (bf16[512,512]{1,0:T(8,128)(2,1)S(1)}, bf16[512,512]{1,0:T(8,128)(2,1)S(1)}, u32[]{:S(2)}, u32[]{:S(2)}) collective-permute-start(bf16[512,512]{1,0:T(8,128)(2,1)S(1)} %pad_maximum_fusion), channel_id=1, source_target_pairs={{0,2},{1,3},{2,0},{3,1},{4,6},{5,7},{6,4},{7,5},{8,10},{9,11},{10,... | collective-permute-start | bytes 1572872 | tf_op jit(solution)/shard_map/ppermute | solution.py:280
  45.2 39.9 %collective-permute-start.18 = (bf16[512,1024]{1,0:T(8,128)(2,1)S(1)}, bf16[512,1024]{1,0:T(8,128)(2,1)S(1)}, u32[]{:S(2)}, u32[]{:S(2)}) collective-permute-start(bf16[512,1024]{1,0:T(8,128)(2,1)S(1)} %collective-permute-done.10.refs_4_), channel_id=1, source_target_pairs={{0,4},{1,5},{4,8},{5,9},{6,2},{7,3},{8,12},{9,13},{10,6},{11,7},{1... | collective-permute-start | bytes 3145736 | tf_op jit(solution)/shard_map/ppermute | solution.py:280
  64.1 3.5 %collective-permute-start.21 = (bf16[512,512]{1,0:T(8,128)(2,1)S(1)}, bf16[512,512]{1,0:T(8,128)(2,1)S(1)}, u32[]{:S(2)}, u32[]{:S(2)}) collective-permute-start(bf16[512,512]{1,0:T(8,128)(2,1)S(1)} %shard_map.88), channel_id=1, source_target_pairs={{0,1},{1,0},{2,3},{3,2},{4,5},{5,4},{6,7},{7,6},{8,9},{9,8},{10,11... | collective-permute-start | bytes 1572872 | tf_op jit(solution)/shard_map/ppermute | solution.py:280
  65.4 6.0 %collective-permute-start.20 = (bf16[512,512]{1,0:T(8,128)(2,1)S(1)}, bf16[512,512]{1,0:T(8,128)(2,1)S(1)}, u32[]{:S(2)}, u32[]{:S(2)}) collective-permute-start(bf16[512,512]{1,0:T(8,128)(2,1)S(1)} %collective-permute-done.19), channel_id=1, source_target_pairs={{0,1},{1,0},{2,3},{3,2},{4,5},{5,4},{6,7},{7,6},{8,9},{9,8},{10,11... | collective-permute-start | bytes 1572872 | tf_op jit(solution)/shard_map/ppermute | solution.py:280
  67.7 18.7 %collective-permute-start.22 = (bf16[512,512]{1,0:T(8,128)(2,1)S(1)}, bf16[512,512]{1,0:T(8,128)(2,1)S(1)}, u32[]{:S(2)}, u32[]{:S(2)}) collective-permute-start(bf16[512,512]{1,0:T(8,128)(2,1)S(1)} %shard_map.89), channel_id=1, source_target_pairs={{0,2},{1,3},{2,0},{3,1},{4,6},{5,7},{6,4},{7,5},{8,10},{9,11},{10,... | collective-permute-start | bytes 1572872 | tf_op jit(solution)/shard_map/ppermute | solution.py:280
  85.7 2.4 %collective-permute-start.23 = (bf16[256,512]{1,0:T(8,128)(2,1)S(1)}, bf16[256,512]{1,0:T(8,128)(2,1)S(1)}, u32[]{:S(2)}, u32[]{:S(2)}) collective-permute-start(bf16[256,512]{1,0:T(8,128)(2,1)S(1)} %get-tuple-element.77), channel_id=1, source_target_pairs={{0,1},{1,0},{2,3},{3,2},{4,5},{5,4},{6,7},{7,6},{8,9},{9,8},{10,11... | collective-permute-start | bytes 786440 | tf_op jit(solution)/shard_map/ppermute | solution.py:280
  86.3 1.8 %collective-permute-start.24 = (bf16[256,512]{1,0:T(8,128)(2,1)S(1)}, bf16[256,512]{1,0:T(8,128)(2,1)S(1)}, u32[]{:S(2)}, u32[]{:S(2)}) collective-permute-start(bf16[256,512]{1,0:T(8,128)(2,1)S(1)} %get-tuple-element.78), channel_id=1, source_target_pairs={{0,1},{1,0},{2,3},{3,2},{4,5},{5,4},{6,7},{7,6},{8,9},{9,8},{10,11... | collective-permute-start | bytes 786440 | tf_op jit(solution)/shard_map/ppermute | solution.py:280

commit v7 on v6

--- a/solution.py
+++ b/solution.py
@@ -21,7 +21,7 @@
 FAR_COUNT = FAR_LIST + FAR
 LEAF = FAR_COUNT + 1
 META = 16
-PIECES = 4
+PIECES = 8
 
 
 def vmem():

time: 89.8 us -> 90.6 us (level)
  starting transfers between devices: 23.7 us -> 24.8 us
    ppermute x25, starting transfers between devices: 23.7 us -> 24.8 us  [move(): lax.ppermute(value, 'pts', [(a, b) for a, b in pairs if b is not None])]
  transfers between devices with their start and end apart: 25 -> 25, of which waited for: 8 -> 8; matrix products, arithmetic and copies ran while one was open for 1% -> 1% of each run, Pallas kernels for 23% -> 22%
where the time goes in v7:
time: 90.6 us; the launch traced here: 90.4 us
  waiting for transfers between devices  38.8 us (43%)
  starting transfers between devices  24.8 us (27%)
  Pallas kernels  21.2 us (23%)
  local copies, waits for them, and re-layouts  2.86 us (3%)
  between operations  1.69 us (2%)
  other arithmetic  1.04 us (1%)
    ppermute x25, waiting for transfers between devices, move(): lax.ppermute(value, 'pts', [(a, b) for a, b in pairs if b is not None])  38.8 us
    ppermute x25, starting transfers between devices, move(): lax.ppermute(value, 'pts', [(a, b) for a, b in pairs if b is not None])  24.8 us
    pallas_call x10, Pallas kernels, call(): pl.pallas_call(body, out_shape=kinds, in_specs=[smem()] * len(scalars) +...  20.2 us
    unnamed x14, local copies, waits for them, and re-layouts  2.75 us
  transfers between devices with their start and end apart: 25, of which 8 were waited for; matrix products, arithmetic and copies ran while one was open for 1% of the time, Pallas kernels for 22%

profile of v7, /device:TPU:7, one launch (start us, length us, event | category | flops | bytes accessed | tf_op | source)
XLA Modules:
  0.0 90.4 jit_solution(10552868286537376027)
XLA Ops:
  0.0 3.3 %collective-permute-start.5 = (bf16[512,512]{1,0:T(8,128)(2,1)}, bf16[512,512]{1,0:T(8,128)(2,1)S(1)}, u32[]{:S(2)}, u32[]{:S(2)}) collective-permute-start(bf16[512,512]{1,0:T(8,128)(2,1)} %refs_7_.3), channel_id=1, source_target_pairs={{2,6},{3,7},{4,0},{5,1},{6,10},{7,11},{8,4},{9,5},{10,14},{11,15},... | collective-permute-start | bytes 1572872 | tf_op jit(solution)/shard_map/ppermute | solution.py:280
  3.3 1.0 %copy-done.1 = bf16[512,512]{1,0:T(8,128)(2,1)S(1)} copy-done((bf16[512,512]{1,0:T(8,128)(2,1)S(1)}, bf16[512,512]{1,0:T(8,128)(2,1)}, u32[]{:S(2)}) %copy-start.1) | copy-done | bytes 524312
  4.3 1.0 %copy-done.3 = bf16[512,512]{1,0:T(8,128)(2,1)S(1)} copy-done((bf16[512,512]{1,0:T(8,128)(2,1)S(1)}, bf16[512,512]{1,0:T(8,128)(2,1)}, u32[]{:S(2)}) %copy-start.3) | copy-done | bytes 524312
  5.9 1.0 %collective-permute-start = (bf16[1,128,512]{2,1,0:T(8,128)(2,1)S(1)}, bf16[1,128,512]{2,1,0:T(8,128)(2,1)S(1)}, u32[]{:S(2)}, u32[]{:S(2)}) collective-permute-start(bf16[1,128,512]{2,1,0:T(8,128)(2,1)S(1)} %get-tuple-element.43), channel_id=1, source_target_pairs={{0,1},{1,0},{2,3},{3,2},{4,5},{5,4},{6,7},{7,6},{8,9},{9,8},{10,11... | collective-permute-start | bytes 393224 | tf_op jit(solution)/shard_map/ppermute | solution.py:280
  6.9 1.7 %collective-permute-start.2 = (bf16[1,128,512]{2,1,0:T(8,128)(2,1)S(1)}, bf16[1,128,512]{2,1,0:T(8,128)(2,1)S(1)}, u32[]{:S(2)}, u32[]{:S(2)}) collective-permute-start(bf16[1,128,512]{2,1,0:T(8,128)(2,1)S(1)} %get-tuple-element.45), channel_id=1, source_target_pairs={{0,3},{1,2},{2,1},{3,0},{4,7},{5,6},{6,5},{7,4},{8,11},{9,10},{10,... | collective-permute-start | bytes 393224 | tf_op jit(solution)/shard_map/ppermute | solution.py:280
  8.6 3.4 %collective-permute-done.1.refs_1_ = bf16[1,128,512]{2,1,0:T(8,128)(2,1)S(1)} collective-permute-done((bf16[1,128,512]{2,1,0:T(8,128)(2,1)S(1)}, bf16[1,128,512]{2,1,0:T(8,128)(2,1)S(1)}, u32[]{:S(2)}, u32[]{:S(2)}) %collective-permute-start.1) | collective-permute-done | bytes 131104 | tf_op jit(solution)/shard_map/ppermute | solution.py:280
  12.0 3.3 %collective-permute-done.2.refs_2_ = bf16[1,128,512]{2,1,0:T(8,128)(2,1)S(1)} collective-permute-done((bf16[1,128,512]{2,1,0:T(8,128)(2,1)S(1)}, bf16[1,128,512]{2,1,0:T(8,128)(2,1)S(1)}, u32[]{:S(2)}, u32[]{:S(2)}) %collective-permute-start.2) | collective-permute-done | bytes 131104 | tf_op jit(solution)/shard_map/ppermute | solution.py:280
  15.9 1.4 %collective-permute-start.4 = (bf16[128,1536]{1,0:T(8,128)(2,1)S(1)}, bf16[128,1536]{1,0:T(8,128)(2,1)}, u32[]{:S(2)}, u32[]{:S(2)}) collective-permute-start(bf16[128,1536]{1,0:T(8,128)(2,1)S(1)} %shard_map.83.refs_0_), channel_id=1, source_target_pairs={{0,8},{1,9},{2,10},{3,11},{4,12},{5,13},{6,14},{7,15},{8,16},{9,17... | collective-permute-start | bytes 1179656 | tf_op jit(solution)/shard_map/ppermute | solution.py:280
  17.4 0.8 collective-permute-start.6
  18.3 7.8 %collective-permute-done.3.refs_1_ = bf16[128,1536]{1,0:T(8,128)(2,1)S(1)} collective-permute-done((bf16[128,1536]{1,0:T(8,128)(2,1)S(1)}, bf16[128,1536]{1,0:T(8,128)(2,1)S(1)}, u32[]{:S(2)}, u32[]{:S(2)}) %collective-permute-start.3) | collective-permute-done | bytes 393248 | tf_op jit(solution)/shard_map/ppermute | solution.py:280
  26.1 2.1 %collective-permute-done.4.refs_2_ = bf16[128,1536]{1,0:T(8,128)(2,1)} collective-permute-done((bf16[128,1536]{1,0:T(8,128)(2,1)S(1)}, bf16[128,1536]{1,0:T(8,128)(2,1)}, u32[]{:S(2)}, u32[]{:S(2)}) %collective-permute-start.4) | collective-permute-done | bytes 393248 | tf_op jit(solution)/shard_map/ppermute | solution.py:280
  28.2 0.9 collective-permute-start.8
  29.0 1.0 %collective-permute-start.9 = (bf16[128,1536]{1,0:T(8,128)(2,1)S(1)}, bf16[128,1536]{1,0:T(8,128)(2,1)}, u32[]{:S(2)}, u32[]{:S(2)}) collective-permute-start(bf16[128,1536]{1,0:T(8,128)(2,1)S(1)} %shard_map.83.refs_0_), channel_id=1, source_target_pairs={{0,24},{1,25},{2,26},{3,27},{4,28},{5,29},{6,30},{7,31},{8,0},{9,1... | collective-permute-start | bytes 1179656 | tf_op jit(solution)/shard_map/ppermute | solution.py:280
  32.1 1.6 %collective-permute-start.11 = (s32[1,16]{1,0:T(1,128)S(1)}, s32[1,16]{1,0:T(1,128)S(1)}, u32[]{:S(2)}, u32[]{:S(2)}) collective-permute-start(s32[1,16]{1,0:T(1,128)S(1)} %bitcast.4), channel_id=1, source_target_pairs={{0,1},{1,0},{2,3},{3,2},{4,5},{5,4},{6,7},{7,6},{8,9},{9,8},{10,11... | collective-permute-start | bytes 200 | tf_op jit(solution)/shard_map/ppermute | solution.py:280
  34.6 1.3 %collective-permute-start.12 = (s32[2,16]{1,0:T(2,128)S(1)}, s32[2,16]{1,0:T(2,128)S(1)}, u32[]{:S(2)}, u32[]{:S(2)}) collective-permute-start(s32[2,16]{1,0:T(2,128)S(1)} %pad_add_fusion.1), channel_id=1, source_target_pairs={{0,2},{1,3},{2,0},{3,1},{4,6},{5,7},{6,4},{7,5},{8,10},{9,11},{10,... | collective-permute-start | bytes 392 | tf_op jit(solution)/shard_map/ppermute | solution.py:280
  35.9 4.4 %collective-permute-done.12 = s32[2,16]{1,0:T(2,128)S(1)} collective-permute-done((s32[2,16]{1,0:T(2,128)S(1)}, s32[2,16]{1,0:T(2,128)S(1)}, u32[]{:S(2)}, u32[]{:S(2)}) %collective-permute-start.12) | collective-permute-done | bytes 160 | tf_op jit(solution)/shard_map/ppermute | solution.py:280
  41.1 1.3 %collective-permute-start.13 = (bf16[128,1536]{1,0:T(8,128)(2,1)}, bf16[128,1536]{1,0:T(8,128)(2,1)S(1)}, u32[]{:S(2)}, u32[]{:S(2)}) collective-permute-start(bf16[128,1536]{1,0:T(8,128)(2,1)} %collective-permute-done.4.refs_2_), channel_id=1, source_target_pairs={{0,8},{1,9},{2,10},{3,11},{4,12},{5,13},{6,14},{7,15},{8,16},{9,17... | collective-permute-start | bytes 1179656 | tf_op jit(solution)/shard_map/ppermute | solution.py:280
  42.4 1.3 %collective-permute-start.14 = (bf16[128,1536]{1,0:T(8,128)(2,1)S(1)}, bf16[128,1536]{1,0:T(8,128)(2,1)S(1)}, u32[]{:S(2)}, u32[]{:S(2)}) collective-permute-start(bf16[128,1536]{1,0:T(8,128)(2,1)S(1)} %collective-permute-done.8.refs_0_), channel_id=1, source_target_pairs={{0,8},{1,9},{2,10},{3,11},{4,12},{5,13},{6,14},{7,15},{8,16},{9,17... | collective-permute-start | bytes 1179656 | tf_op jit(solution)/shard_map/ppermute | solution.py:280
  44.0 1.0 %pad_maximum_fusion = bf16[512,512]{1,0:T(8,128)(2,1)S(1)} fusion(bf16[160,512]{1,0:T(8,128)(2,1)S(1)} %collective-permute-done.7, bf16[352,512]{1,0:T(8,128)(2,1)} %collective-permute-done.6), kind=kLoop, calls=%fused_computation | loop fusion | flops 1048576 | bytes 1048576 | tf_op jit(solution)/shard_map/concatenate | solution.py:340
  45.2 3.0 %collective-permute-start.18 = (bf16[512,1024]{1,0:T(8,128)(2,1)S(1)}, bf16[512,1024]{1,0:T(8,128)(2,1)S(1)}, u32[]{:S(2)}, u32[]{:S(2)}) collective-permute-start(bf16[512,1024]{1,0:T(8,128)(2,1)S(1)} %collective-permute-done.10.refs_4_), channel_id=1, source_target_pairs={{0,4},{1,5},{4,8},{5,9},{6,2},{7,3},{8,12},{9,13},{10,6},{11,7},{1... | collective-permute-start | bytes 3145736 | tf_op jit(solution)/shard_map/ppermute | solution.py:280
  48.2 4.7 %shard_map.84 = (f32[512,512]{1,0:T(8,128)S(1)}, f32[512,512]{1,0:T(8,128)S(1)}) custom-call(s32[4,16]{1,0:T(4,128)S(1)} %pad_add_fusion.meta, bf16[128,1536]{1,0:T(8,128)(2,1)S(1)} %shard_map.83.refs_0_, bf16[128,1536]{1,0:T(8,128)(2,1)S(1)} %collective-permute-done.3.refs_1_, bf16[128,1536]{1,0:T(8,128)(2,1)} %collective-permute-done.4.refs_2_, ...), custom_call_target="tpu_custom_call" | custom-call | flops 1000 | bytes 1000 | tf_op jit(solution)/shard_map/pallas_call | solution.py:78
  53.0 4.4 %shard_map.85 = (f32[512,512]{1,0:T(8,128)S(1)}, f32[512,512]{1,0:T(8,128)S(1)}) custom-call(s32[4,16]{1,0:T(4,128)S(1)} %pad_add_fusion.meta, bf16[128,1536]{1,0:T(8,128)(2,1)S(1)} %shard_map.83.refs_0_, bf16[128,1536]{1,0:T(8,128)(2,1)S(1)} %collective-permute-done.3.refs_1_, bf16[128,1536]{1,0:T(8,128)(2,1)} %collective-permute-done.4.refs_2_, ...), custom_call_target="tpu_custom_call" | custom-call | flops 1000 | bytes 1000 | tf_op jit(solution)/shard_map/pallas_call | solution.py:78
  57.4 4.4 %collective-permute-done.14.refs_2_ = bf16[128,1536]{1,0:T(8,128)(2,1)S(1)} collective-permute-done((bf16[128,1536]{1,0:T(8,128)(2,1)S(1)}, bf16[128,1536]{1,0:T(8,128)(2,1)S(1)}, u32[]{:S(2)}, u32[]{:S(2)}) %collective-permute-start.14) | collective-permute-done | bytes 393248 | tf_op jit(solution)/shard_map/ppermute | solution.py:280
  61.8 2.2 %shard_map.88 = bf16[512,512]{1,0:T(8,128)(2,1)S(1)} custom-call(s32[4,16]{1,0:T(4,128)S(1)} %pad_add_fusion.meta, bf16[128,1536]{1,0:T(8,128)(2,1)S(1)} %collective-permute-done.8.refs_0_, bf16[128,1536]{1,0:T(8,128)(2,1)S(1)} %collective-permute-done.13.refs_1_, bf16[128,1536]{1,0:T(8,128)(2,1)S(1)} %collective-permute-done.14.refs_2_, ...), custom_call_target="tpu_custom_call" | custom-call | flops 1000 | bytes 1000 | tf_op jit(solution)/shard_map/pallas_call | solution.py:78
  64.1 1.4 %collective-permute-start.21 = (bf16[512,512]{1,0:T(8,128)(2,1)S(1)}, bf16[512,512]{1,0:T(8,128)(2,1)S(1)}, u32[]{:S(2)}, u32[]{:S(2)}) collective-permute-start(bf16[512,512]{1,0:T(8,128)(2,1)S(1)} %shard_map.88), channel_id=1, source_target_pairs={{0,1},{1,0},{2,3},{3,2},{4,5},{5,4},{6,7},{7,6},{8,9},{9,8},{10,11... | collective-permute-start | bytes 1572872 | tf_op jit(solution)/shard_map/ppermute | solution.py:280
  65.5 2.0 %shard_map.87.one = f32[512,512]{1,0:T(8,128)S(1)} custom-call(s32[4,16]{1,0:T(4,128)S(1)} %pad_add_fusion.meta, bf16[128,1536]{1,0:T(8,128)(2,1)S(1)} %collective-permute-done.8.refs_0_, bf16[128,1536]{1,0:T(8,128)(2,1)S(1)} %collective-permute-done.13.refs_1_, bf16[128,1536]{1,0:T(8,128)(2,1)S(1)} %collective-permute-done.14.refs_2_, ...), custom_call_target="tpu_custom_call" | custom-call | flops 1000 | bytes 1000 | tf_op jit(solution)/shard_map/pallas_call | solution.py:78
  67.7 1.3 %collective-permute-start.22 = (bf16[512,512]{1,0:T(8,128)(2,1)S(1)}, bf16[512,512]{1,0:T(8,128)(2,1)S(1)}, u32[]{:S(2)}, u32[]{:S(2)}) collective-permute-start(bf16[512,512]{1,0:T(8,128)(2,1)S(1)} %shard_map.89), channel_id=1, source_target_pairs={{0,2},{1,3},{2,0},{3,1},{4,6},{5,7},{6,4},{7,5},{8,10},{9,11},{10,... | collective-permute-start | bytes 1572872 | tf_op jit(solution)/shard_map/ppermute | solution.py:280
  69.0 3.4 %shard_map.86 = (f32[512,512]{1,0:T(8,128)S(1)}, f32[512,512]{1,0:T(8,128)S(1)}) custom-call(s32[4,16]{1,0:T(4,128)S(1)} %pad_add_fusion.meta, bf16[128,1536]{1,0:T(8,128)(2,1)S(1)} %collective-permute-done.8.refs_0_, bf16[128,1536]{1,0:T(8,128)(2,1)S(1)} %collective-permute-done.13.refs_1_, bf16[128,1536]{1,0:T(8,128)(2,1)S(1)} %collective-permute-done.14.refs_2_, ...), custom_call_target="tpu_custom_call" | custom-call | flops 1000 | bytes 1000 | tf_op jit(solution)/shard_map/pallas_call | solution.py:78
  72.4 12.7 %collective-permute-done.18.ypts = bf16[512,1024]{1,0:T(8,128)(2,1)S(1)} collective-permute-done((bf16[512,1024]{1,0:T(8,128)(2,1)S(1)}, bf16[512,1024]{1,0:T(8,128)(2,1)S(1)}, u32[]{:S(2)}, u32[]{:S(2)}) %collective-permute-start.18) | collective-permute-done | bytes 1048608 | tf_op jit(solution)/shard_map/ppermute | solution.py:280
  85.7 1.6 %collective-permute-start.23 = (bf16[256,512]{1,0:T(8,128)(2,1)S(1)}, bf16[256,512]{1,0:T(8,128)(2,1)S(1)}, u32[]{:S(2)}, u32[]{:S(2)}) collective-permute-start(bf16[256,512]{1,0:T(8,128)(2,1)S(1)} %get-tuple-element.77), channel_id=1, source_target_pairs={{0,1},{1,0},{2,3},{3,2},{4,5},{5,4},{6,7},{7,6},{8,9},{9,8},{10,11... | collective-permute-start | bytes 786440 | tf_op jit(solution)/shard_map/ppermute | solution.py:280
  87.5 1.7 %shard_map.90.acc = f32[512,512]{1,0:T(8,128)S(1)} custom-call(s32[4,16]{1,0:T(4,128)S(1)} %pad_add_fusion.meta, bf16[512,1024]{1,0:T(8,128)(2,1)S(1)} %copy-done, f32[512,512]{1,0:T(8,128)S(1)} %get-tuple-element.71.start, bf16[512,1024]{1,0:T(8,128)(2,1)S(1)} %collective-permute-done.18.ypts, bf16[512,512]{1,0:T(8,128)(2,1)S(1)} %collective-permute-done.20.wts, ...), custom_call_target="tpu_custom_call" | custom-call | flops 1000 | bytes 1000 | tf_op jit(solution)/shard_map/pallas_call | solution.py:78
  89.2 1.0 %shard_map.92 = f32[512,512]{1,0:T(8,128)} custom-call(f32[512,512]{1,0:T(8,128)S(1)} %shard_map.90.acc, bf16[256,512]{1,0:T(8,128)(2,1)S(1)} %collective-permute-done.23.upper, bf16[256,512]{1,0:T(8,128)(2,1)S(1)} %collective-permute-done.24.lower), custom_call_target="tpu_custom_call" | custom-call | flops 1000 | bytes 1000 | tf_op jit(solution)/shard_map/pallas_call | solution.py:260
  (50 shorter events, 5.1 us)
Async XLA Ops:
  0.0 15.3 %copy-start = (bf16[512,1024]{1,0:T(8,128)(2,1)S(1)}, bf16[512,1024]{1,0:T(8,128)(2,1)}, u32[]{:S(2)}) copy-start(bf16[512,1024]{1,0:T(8,128)(2,1)} %xpts.1) | copy-start | bytes 3145732
  0.0 17.4 %collective-permute-start.5 = (bf16[512,512]{1,0:T(8,128)(2,1)}, bf16[512,512]{1,0:T(8,128)(2,1)S(1)}, u32[]{:S(2)}, u32[]{:S(2)}) collective-permute-start(bf16[512,512]{1,0:T(8,128)(2,1)} %refs_7_.3), channel_id=1, source_target_pairs={{2,6},{3,7},{4,0},{5,1},{6,10},{7,11},{8,4},{9,5},{10,14},{11,15},... | collective-permute-start | bytes 1572872 | tf_op jit(solution)/shard_map/ppermute | solution.py:280
  3.3 1.1 %copy-start.1 = (bf16[512,512]{1,0:T(8,128)(2,1)S(1)}, bf16[512,512]{1,0:T(8,128)(2,1)}, u32[]{:S(2)}) copy-start(bf16[512,512]{1,0:T(8,128)(2,1)} %refs_7_.3) | copy-start | bytes 1572868
  4.3 1.0 %copy-start.3 = (bf16[512,512]{1,0:T(8,128)(2,1)S(1)}, bf16[512,512]{1,0:T(8,128)(2,1)}, u32[]{:S(2)}) copy-start(bf16[512,512]{1,0:T(8,128)(2,1)} %proj.1) | copy-start | bytes 1572868
  5.9 2.7 %collective-permute-start = (bf16[1,128,512]{2,1,0:T(8,128)(2,1)S(1)}, bf16[1,128,512]{2,1,0:T(8,128)(2,1)S(1)}, u32[]{:S(2)}, u32[]{:S(2)}) collective-permute-start(bf16[1,128,512]{2,1,0:T(8,128)(2,1)S(1)} %get-tuple-element.43), channel_id=1, source_target_pairs={{0,1},{1,0},{2,3},{3,2},{4,5},{5,4},{6,7},{7,6},{8,9},{9,8},{10,11... | collective-permute-start | bytes 393224 | tf_op jit(solution)/shard_map/ppermute | solution.py:280
  6.9 5.1 %collective-permute-start.1 = (bf16[1,128,512]{2,1,0:T(8,128)(2,1)S(1)}, bf16[1,128,512]{2,1,0:T(8,128)(2,1)S(1)}, u32[]{:S(2)}, u32[]{:S(2)}) collective-permute-start(bf16[1,128,512]{2,1,0:T(8,128)(2,1)S(1)} %get-tuple-element.44), channel_id=1, source_target_pairs={{0,2},{1,3},{2,0},{3,1},{4,6},{5,7},{6,4},{7,5},{8,10},{9,11},{10,... | collective-permute-start | bytes 393224 | tf_op jit(solution)/shard_map/ppermute | solution.py:280
  6.9 8.3 %copy-start.4 = (s32[1,128]{1,0:T(1,128)S(1)}, s32[1,128]{1,0:T(1,128)}, u32[]{:S(2)}) copy-start(s32[1,128]{1,0:T(1,128)} %idx.1) | copy-start | bytes 1540
  6.9 8.3 %collective-permute-start.2 = (bf16[1,128,512]{2,1,0:T(8,128)(2,1)S(1)}, bf16[1,128,512]{2,1,0:T(8,128)(2,1)S(1)}, u32[]{:S(2)}, u32[]{:S(2)}) collective-permute-start(bf16[1,128,512]{2,1,0:T(8,128)(2,1)S(1)} %get-tuple-element.45), channel_id=1, source_target_pairs={{0,3},{1,2},{2,1},{3,0},{4,7},{5,6},{6,5},{7,4},{8,11},{9,10},{10,... | collective-permute-start | bytes 393224 | tf_op jit(solution)/shard_map/ppermute | solution.py:280
  15.3 25.7 %collective-permute-start.10 = (bf16[512,1024]{1,0:T(8,128)(2,1)S(1)}, bf16[512,1024]{1,0:T(8,128)(2,1)S(1)}, u32[]{:S(2)}, u32[]{:S(2)}) collective-permute-start(bf16[512,1024]{1,0:T(8,128)(2,1)S(1)} %copy-done), channel_id=1, source_target_pairs={{0,2},{1,3},{2,0},{3,1},{4,6},{5,7},{6,4},{7,5},{8,10},{9,11},{10,... | collective-permute-start | bytes 3145736 | tf_op jit(solution)/shard_map/ppermute | solution.py:280
  15.6 10.5 %collective-permute-start.3 = (bf16[128,1536]{1,0:T(8,128)(2,1)S(1)}, bf16[128,1536]{1,0:T(8,128)(2,1)S(1)}, u32[]{:S(2)}, u32[]{:S(2)}) collective-permute-start(bf16[128,1536]{1,0:T(8,128)(2,1)S(1)} %shard_map.83.refs_0_), channel_id=1, source_target_pairs={{0,4},{1,5},{2,6},{3,7},{4,0},{5,1},{6,2},{7,3},{8,12},{9,13},{10,... | collective-permute-start | bytes 1179656 | tf_op jit(solution)/shard_map/ppermute | solution.py:280
  15.9 12.2 %collective-permute-start.4 = (bf16[128,1536]{1,0:T(8,128)(2,1)S(1)}, bf16[128,1536]{1,0:T(8,128)(2,1)}, u32[]{:S(2)}, u32[]{:S(2)}) collective-permute-start(bf16[128,1536]{1,0:T(8,128)(2,1)S(1)} %shard_map.83.refs_0_), channel_id=1, source_target_pairs={{0,8},{1,9},{2,10},{3,11},{4,12},{5,13},{6,14},{7,15},{8,16},{9,17... | collective-permute-start | bytes 1179656 | tf_op jit(solution)/shard_map/ppermute | solution.py:280
  17.4 10.8 %collective-permute-start.6 = (bf16[352,512]{1,0:T(8,128)(2,1)S(1)}, bf16[352,512]{1,0:T(8,128)(2,1)}, u32[]{:S(2)}, u32[]{:S(2)}) collective-permute-start(bf16[352,512]{1,0:T(8,128)(2,1)S(1)} %split.8), channel_id=1, source_target_pairs={{0,1},{1,0},{2,3},{3,2},{4,5},{5,4},{6,7},{7,6},{8,9},{9,8},{10,11... | collective-permute-start | bytes 1081352 | tf_op jit(solution)/shard_map/ppermute | solution.py:280
  18.2 9.9 %collective-permute-start.7 = (bf16[160,512]{1,0:T(8,128)(2,1)S(1)}, bf16[160,512]{1,0:T(8,128)(2,1)S(1)}, u32[]{:S(2)}, u32[]{:S(2)}) collective-permute-start(bf16[160,512]{1,0:T(8,128)(2,1)S(1)} %split.9), channel_id=1, source_target_pairs={{0,1},{1,0},{2,3},{3,2},{4,5},{5,4},{6,7},{7,6},{8,9},{9,8},{10,11... | collective-permute-start | bytes 491528 | tf_op jit(solution)/shard_map/ppermute | solution.py:280
  28.2 12.8 %collective-permute-start.8 = (bf16[128,1536]{1,0:T(8,128)(2,1)}, bf16[128,1536]{1,0:T(8,128)(2,1)S(1)}, u32[]{:S(2)}, u32[]{:S(2)}) collective-permute-start(bf16[128,1536]{1,0:T(8,128)(2,1)} %collective-permute-done.4.refs_2_), channel_id=1, source_target_pairs={{0,4},{1,5},{2,6},{3,7},{4,0},{5,1},{6,2},{7,3},{8,12},{9,13},{10,... | collective-permute-start | bytes 1179656 | tf_op jit(solution)/shard_map/ppermute | solution.py:280
  29.0 12.0 %collective-permute-start.9 = (bf16[128,1536]{1,0:T(8,128)(2,1)S(1)}, bf16[128,1536]{1,0:T(8,128)(2,1)}, u32[]{:S(2)}, u32[]{:S(2)}) collective-permute-start(bf16[128,1536]{1,0:T(8,128)(2,1)S(1)} %shard_map.83.refs_0_), channel_id=1, source_target_pairs={{0,24},{1,25},{2,26},{3,27},{4,28},{5,29},{6,30},{7,31},{8,0},{9,1... | collective-permute-start | bytes 1179656 | tf_op jit(solution)/shard_map/ppermute | solution.py:280
  31.4 0.7 copy-start.5
  31.4 0.7 copy-start.6
  32.1 2.4 %collective-permute-start.11 = (s32[1,16]{1,0:T(1,128)S(1)}, s32[1,16]{1,0:T(1,128)S(1)}, u32[]{:S(2)}, u32[]{:S(2)}) collective-permute-start(s32[1,16]{1,0:T(1,128)S(1)} %bitcast.4), channel_id=1, source_target_pairs={{0,1},{1,0},{2,3},{3,2},{4,5},{5,4},{6,7},{7,6},{8,9},{9,8},{10,11... | collective-permute-start | bytes 200 | tf_op jit(solution)/shard_map/ppermute | solution.py:280
  34.6 5.7 %collective-permute-start.12 = (s32[2,16]{1,0:T(2,128)S(1)}, s32[2,16]{1,0:T(2,128)S(1)}, u32[]{:S(2)}, u32[]{:S(2)}) collective-permute-start(s32[2,16]{1,0:T(2,128)S(1)} %pad_add_fusion.1), channel_id=1, source_target_pairs={{0,2},{1,3},{2,0},{3,1},{4,6},{5,7},{6,4},{7,5},{8,10},{9,11},{10,... | collective-permute-start | bytes 392 | tf_op jit(solution)/shard_map/ppermute | solution.py:280
  40.3 8.0 %copy-start.2 = (bf16[512,512]{1,0:T(8,128)(2,1)S(1)}, bf16[512,512]{1,0:T(8,128)(2,1)}, u32[]{:S(2)}) copy-start(bf16[512,512]{1,0:T(8,128)(2,1)} %refs_7_.3) | copy-start | bytes 1572868
  40.3 4.7 %collective-permute-start.16 = (bf16[512,1024]{1,0:T(8,128)(2,1)S(1)}, bf16[512,1024]{1,0:T(8,128)(2,1)S(1)}, u32[]{:S(2)}, u32[]{:S(2)}) collective-permute-start(bf16[512,1024]{1,0:T(8,128)(2,1)S(1)} %copy-done), channel_id=1, source_target_pairs={{0,1},{1,0},{2,3},{3,2},{4,5},{5,4},{6,7},{7,6},{8,9},{9,8},{10,11... | collective-permute-start | bytes 3145736 | tf_op jit(solution)/shard_map/ppermute | solution.py:280
  41.0 4.2 %collective-permute-start.17 = (bf16[512,1024]{1,0:T(8,128)(2,1)S(1)}, bf16[512,1024]{1,0:T(8,128)(2,1)S(1)}, u32[]{:S(2)}, u32[]{:S(2)}) collective-permute-start(bf16[512,1024]{1,0:T(8,128)(2,1)S(1)} %collective-permute-done.10.refs_4_), channel_id=1, source_target_pairs={{0,1},{1,0},{2,3},{3,2},{4,5},{5,4},{6,7},{7,6},{8,9},{9,8},{10,11... | collective-permute-start | bytes 3145736 | tf_op jit(solution)/shard_map/ppermute | solution.py:280
  41.1 16.3 %collective-permute-start.13 = (bf16[128,1536]{1,0:T(8,128)(2,1)}, bf16[128,1536]{1,0:T(8,128)(2,1)S(1)}, u32[]{:S(2)}, u32[]{:S(2)}) collective-permute-start(bf16[128,1536]{1,0:T(8,128)(2,1)} %collective-permute-done.4.refs_2_), channel_id=1, source_target_pairs={{0,8},{1,9},{2,10},{3,11},{4,12},{5,13},{6,14},{7,15},{8,16},{9,17... | collective-permute-start | bytes 1179656 | tf_op jit(solution)/shard_map/ppermute | solution.py:280
  42.4 19.4 %collective-permute-start.14 = (bf16[128,1536]{1,0:T(8,128)(2,1)S(1)}, bf16[128,1536]{1,0:T(8,128)(2,1)S(1)}, u32[]{:S(2)}, u32[]{:S(2)}) collective-permute-start(bf16[128,1536]{1,0:T(8,128)(2,1)S(1)} %collective-permute-done.8.refs_0_), channel_id=1, source_target_pairs={{0,8},{1,9},{2,10},{3,11},{4,12},{5,13},{6,14},{7,15},{8,16},{9,17... | collective-permute-start | bytes 1179656 | tf_op jit(solution)/shard_map/ppermute | solution.py:280
  43.7 18.1 %collective-permute-start.15 = (bf16[128,1536]{1,0:T(8,128)(2,1)}, bf16[128,1536]{1,0:T(8,128)(2,1)S(1)}, u32[]{:S(2)}, u32[]{:S(2)}) collective-permute-start(bf16[128,1536]{1,0:T(8,128)(2,1)} %collective-permute-done.9.refs_3_), channel_id=1, source_target_pairs={{0,4},{1,5},{2,6},{3,7},{4,0},{5,1},{6,2},{7,3},{8,12},{9,13},{10,... | collective-permute-start | bytes 1179656 | tf_op jit(solution)/shard_map/ppermute | solution.py:280
  45.0 20.4 %collective-permute-start.19 = (bf16[512,512]{1,0:T(8,128)(2,1)S(1)}, bf16[512,512]{1,0:T(8,128)(2,1)S(1)}, u32[]{:S(2)}, u32[]{:S(2)}) collective-permute-start(bf16[512,512]{1,0:T(8,128)(2,1)S(1)} %pad_maximum_fusion), channel_id=1, source_target_pairs={{0,2},{1,3},{2,0},{3,1},{4,6},{5,7},{6,4},{7,5},{8,10},{9,11},{10,... | collective-permute-start | bytes 1572872 | tf_op jit(solution)/shard_map/ppermute | solution.py:280
  45.2 39.9 %collective-permute-start.18 = (bf16[512,1024]{1,0:T(8,128)(2,1)S(1)}, bf16[512,1024]{1,0:T(8,128)(2,1)S(1)}, u32[]{:S(2)}, u32[]{:S(2)}) collective-permute-start(bf16[512,1024]{1,0:T(8,128)(2,1)S(1)} %collective-permute-done.10.refs_4_), channel_id=1, source_target_pairs={{0,4},{1,5},{4,8},{5,9},{6,2},{7,3},{8,12},{9,13},{10,6},{11,7},{1... | collective-permute-start | bytes 3145736 | tf_op jit(solution)/shard_map/ppermute | solution.py:280
  64.1 3.5 %collective-permute-start.21 = (bf16[512,512]{1,0:T(8,128)(2,1)S(1)}, bf16[512,512]{1,0:T(8,128)(2,1)S(1)}, u32[]{:S(2)}, u32[]{:S(2)}) collective-permute-start(bf16[512,512]{1,0:T(8,128)(2,1)S(1)} %shard_map.88), channel_id=1, source_target_pairs={{0,1},{1,0},{2,3},{3,2},{4,5},{5,4},{6,7},{7,6},{8,9},{9,8},{10,11... | collective-permute-start | bytes 1572872 | tf_op jit(solution)/shard_map/ppermute | solution.py:280
  65.4 7.0 %collective-permute-start.20 = (bf16[512,512]{1,0:T(8,128)(2,1)S(1)}, bf16[512,512]{1,0:T(8,128)(2,1)S(1)}, u32[]{:S(2)}, u32[]{:S(2)}) collective-permute-start(bf16[512,512]{1,0:T(8,128)(2,1)S(1)} %collective-permute-done.19), channel_id=1, source_target_pairs={{0,1},{1,0},{2,3},{3,2},{4,5},{5,4},{6,7},{7,6},{8,9},{9,8},{10,11... | collective-permute-start | bytes 1572872 | tf_op jit(solution)/shard_map/ppermute | solution.py:280
  67.7 19.8 %collective-permute-start.22 = (bf16[512,512]{1,0:T(8,128)(2,1)S(1)}, bf16[512,512]{1,0:T(8,128)(2,1)S(1)}, u32[]{:S(2)}, u32[]{:S(2)}) collective-permute-start(bf16[512,512]{1,0:T(8,128)(2,1)S(1)} %shard_map.89), channel_id=1, source_target_pairs={{0,2},{1,3},{2,0},{3,1},{4,6},{5,7},{6,4},{7,5},{8,10},{9,11},{10,... | collective-permute-start | bytes 1572872 | tf_op jit(solution)/shard_map/ppermute | solution.py:280
  85.7 3.4 %collective-permute-start.23 = (bf16[256,512]{1,0:T(8,128)(2,1)S(1)}, bf16[256,512]{1,0:T(8,128)(2,1)S(1)}, u32[]{:S(2)}, u32[]{:S(2)}) collective-permute-start(bf16[256,512]{1,0:T(8,128)(2,1)S(1)} %get-tuple-element.77), channel_id=1, source_target_pairs={{0,1},{1,0},{2,3},{3,2},{4,5},{5,4},{6,7},{7,6},{8,9},{9,8},{10,11... | collective-permute-start | bytes 786440 | tf_op jit(solution)/shard_map/ppermute | solution.py:280
  87.4 1.8 %collective-permute-start.24 = (bf16[256,512]{1,0:T(8,128)(2,1)S(1)}, bf16[256,512]{1,0:T(8,128)(2,1)S(1)}, u32[]{:S(2)}, u32[]{:S(2)}) collective-permute-start(bf16[256,512]{1,0:T(8,128)(2,1)S(1)} %get-tuple-element.78), channel_id=1, source_target_pairs={{0,1},{1,0},{2,3},{3,2},{4,5},{5,4},{6,7},{7,6},{8,9},{9,8},{10,11... | collective-permute-start | bytes 786440 | tf_op jit(solution)/shard_map/ppermute | solution.py:280
